TPU v7x, 128 devices: a whole 4x4x4 slice. The times are simulated.
128 devices in a mesh: tok: 4 (over z), lat: 32 (over y, x, core).
Axes of the slice: x: 4, y: 4, z: 4, core: 2. Of those that a mesh axis runs over, the one named last changes fastest.
Arguments:
- residuals: bfloat16 [2048, 4096], P('tok', 'lat'), may hold values from -6 to 6
- dictionary: bfloat16 [65536, 4096], P('lat'), may hold values from -0.09375 to 0.09375
- enc_bias: float32 [65536], P('lat'), may hold values from -3 to 3
- dec_bias: float32 [4096], replicated, may hold values from -3 to 3
- tile_ids: int32 [16, 32, 4], P('tok', 'lat'), may hold values from 0 to 31, as said below
- tile_counts: int32 [16, 32], P('tok', 'lat'), may hold values from 0 to 4, as said below
Outputs:
- tile_codes: bfloat16 [16, 32, 4, 8192], P('tok', None, None, 'lat')
- reconstruction: bfloat16 [2048, 4096], P('tok', 'lat')
- decoder_grad: float32 [65536, 4096], P('lat', 'tok')
Inputs may be any that keep to these rules, and one draw needn't show every extreme that they name: `tile_ids`: for each token block and latent shard the 4 entries are distinct latent blocks; only the first tile_counts entries count. `tile_counts`: every draw has token blocks with all 4 slots active on every latent shard.
All inputs are finite; a program needn't handle non-finite values.
Results may differ from a plain program's by a relative error of at most 0.02.
Values may be sent and summed in bfloat16 or wider, within the bound.
No kernel may reach another device: no remote copies, remote signals or barrier semaphores. Data moves between devices by JAX's collectives and lax.ppermute only.
A program may use at most 128 MiB of HBM per device.

v0:
```python
import jax
import jax.numpy as jnp
from jax import lax
from jax.sharding import PartitionSpec as P

TILE_ROWS = 128
LAT_TILE = 64


def body(residuals, dictionary, enc_bias, dec_bias, tile_ids, tile_counts):
    tok_rows = residuals.shape[0]
    lat_rows = dictionary.shape[0]
    model_width = dictionary.shape[1]
    blocks = tok_rows // TILE_ROWS
    lat_blocks = lat_rows // LAT_TILE
    slot_count = tile_ids.shape[2]
    gathered = lax.all_gather(residuals, "lat", axis=1, tiled=True)
    centered = (gathered.astype(jnp.float32) - dec_bias).astype(jnp.bfloat16)
    preact = (
        lax.dot_general(
            centered, dictionary, (((1,), (1,)), ((), ())), preferred_element_type=jnp.float32
        )
        + enc_bias
    )
    live_slots = lax.broadcasted_iota(jnp.int32, (blocks, slot_count), 1) < tile_counts
    block_iota = lax.broadcasted_iota(jnp.int32, (blocks, slot_count, lat_blocks), 2)
    selector = ((tile_ids[:, 0, :, None] == block_iota) & live_slots[:, :, None]).astype(
        jnp.float32
    )
    tile_active = jnp.max(selector, axis=1)
    code_four = (
        jnp.maximum(preact, 0.0).reshape(blocks, TILE_ROWS, lat_blocks, LAT_TILE)
        * tile_active[:, None, :, None]
    )
    code_values = code_four.reshape(tok_rows, lat_rows).astype(jnp.bfloat16)
    picked = lax.dot_general(
        selector.astype(jnp.bfloat16),
        code_values.reshape(blocks, TILE_ROWS, lat_blocks, LAT_TILE),
        (((2,), (2,)), ((0,), (0,))),
        preferred_element_type=jnp.float32,
    )
    tile_send = picked.reshape(blocks, 1, slot_count, TILE_ROWS * LAT_TILE).astype(jnp.bfloat16)
    tile_codes = lax.all_to_all(tile_send, "lat", split_axis=3, concat_axis=1, tiled=True)
    lat_index = lax.axis_index("lat")
    col_width = model_width // lax.axis_size("lat")
    summed = lax.psum_scatter(
        lax.dot_general(
            dictionary, code_values, (((0,), (1,)), ((), ())), preferred_element_type=jnp.float32
        ).astype(jnp.bfloat16),
        "lat",
        scatter_dimension=0,
        tiled=True,
    ).astype(jnp.float32)
    recon_part = summed.T + lax.dynamic_slice_in_dim(dec_bias, lat_index * col_width, col_width, 0)
    reconstruction = recon_part.astype(jnp.bfloat16)
    error_part = (recon_part - residuals.astype(jnp.float32)).astype(jnp.bfloat16)
    error_full = lax.all_gather(error_part, "lat", axis=1, tiled=True)
    partial_value = lax.dot_general(
        code_values, error_full, (((0,), (0,)), ((), ())), preferred_element_type=jnp.float32
    )
    partial_value = partial_value.astype(jnp.bfloat16).astype(jnp.float32)
    decoder_grad = lax.psum_scatter(
        partial_value.astype(jnp.bfloat16), "tok", scatter_dimension=1, tiled=True
    ).astype(jnp.float32)
    return (tile_codes, reconstruction, decoder_grad)


def solution(mesh):
    placed = (
        P("tok", "lat"),
        P("lat", None),
        P("lat"),
        P(),
        P("tok", "lat", None),
        P("tok", "lat"),
    )
    return jax.shard_map(
        body,
        mesh=mesh,
        in_specs=placed,
        out_specs=(P("tok", None, None, "lat"), P("tok", "lat"), P("lat", "tok")),
        check_vma=False,
    )
```

profile of v0, /device:TPU:1, one launch (start us, length us, event | category | flops | bytes accessed | tf_op | source)
XLA Modules:
  0.0 405.7 jit_solution(17756622914051192832)
XLA Ops:
  7.2 0.0 all-gather.3.cloned.1.call-start
  7.2 0.7 all-gather.3.cloned.1.call-update
  7.9 0.0 reduce-scatter.7.cloned.1.call-start
  7.9 0.7 iota_compare_fusion.1
  8.7 0.8 convert_reduce_fusion
  9.4 0.1 copy.15
  9.5 0.6 mul.14
  10.1 2.5 copy.31
  12.6 0.0 copy-start.2
  12.6 0.0 copy-start.3
  12.6 5.5 %copy.16 = f32[512,2048]{1,0:T(8,128)} copy(f32[512,2048]{0,1:T(8,128)} %bitcast.38) | data formatting | bytes 8388608 | tf_op jit(solution)/shard_map/mul | solution.py:32
  18.1 44.9 %all-gather.3.cloned.1.call-done = bf16[512,4096]{1,0:T(8,128)(2,1)} async-done(((bf16[512,128]{1,0:T(8,128)(2,1)}), bf16[512,4096]{1,0:T(8,128)(2,1)}) %all-gather.3.cloned.1.call-update) | async-done | bytes 4194320 | tf_op jit(solution)/shard_map/all_gather | solution.py:17
  63.0 0.0 copy-done.2
  63.0 0.0 copy-done.3
  63.0 14.3 %multiply_convert_fusion = bf16[512,2048]{1,0:T(8,128)(2,1)S(1)} fusion(f32[512,2048]{1,0:T(8,128)} %copy.16, bf16[2048,4096]{1,0:T(8,128)(2,1)} %param.7, bf16[512,4096]{1,0:T(8,128)(2,1)} %all-gather.3.cloned.1.call-done, f32[4096]{0:T(1024)S(1)} %copy-done.2, f32[2048]{0:T(1024)S(1)} %copy-done.3), kind=kOutput, calls=%fused_computation.6 | convolution fusion | flops 8600420352 | bytes 27287552 | tf_op jit(solution)/shard_map/dot_general | solution.py:20
  77.2 13.7 %fusion = bf16[4096,512]{0,1:T(8,128)(2,1)} fusion(bf16[512,2048]{1,0:T(8,128)(2,1)S(1)} %multiply_convert_fusion, bf16[2048,4096]{1,0:T(8,128)(2,1)} %param.7), kind=kOutput, calls=%fused_computation.3 | convolution fusion | flops 8592031744 | bytes 23068672 | tf_op jit(solution)/shard_map/dot_general | solution.py:47
  91.0 6.5 %copy.26 = bf16[4096,512]{1,0:T(8,128)(2,1)} copy(bf16[4096,512]{0,1:T(8,128)(2,1)} %fusion) | data formatting | bytes 8388608
  97.4 0.0 copy-start
  97.4 0.0 reduce-scatter.7.cloned.1.call-update
  97.4 0.0 all-gather.5.cloned.1.call-start
  97.5 0.1 dynamic_slice.3
  97.6 79.3 %reduce-scatter.7.cloned.1.call-done = bf16[128,512]{1,0:T(8,128)(2,1)} async-done(((bf16[4096,512]{1,0:T(8,128)(2,1)}), bf16[128,512]{1,0:T(8,128)(2,1)}) %reduce-scatter.7.cloned.1.call-update) | async-done | bytes 131088
  176.9 1.0 copy.27
  177.9 0.0 copy-done
  177.9 0.7 fusion.3
  178.6 0.0 all-gather.5.cloned.1.call-update
  178.7 0.2 reduce-scatter.5.cloned.1.call-start
  178.9 51.6 %all-gather.5.cloned.1.call-done = bf16[512,4096]{1,0:T(8,128)(2,1)} async-done(((bf16[512,128]{1,0:T(8,128)(2,1)}), bf16[512,4096]{1,0:T(8,128)(2,1)}) %all-gather.5.cloned.1.call-update) | async-done | bytes 4194320 | tf_op jit(solution)/shard_map/all_gather | solution.py:57
  230.4 14.6 %convolution_convert_fusion = bf16[2048,4096]{1,0:T(8,128)(2,1)} fusion(bf16[512,2048]{1,0:T(8,128)(2,1)S(1)} %multiply_convert_fusion, bf16[512,4096]{1,0:T(8,128)(2,1)} %all-gather.5.cloned.1.call-done), kind=kOutput, calls=%fused_computation | convolution fusion | flops 8598323200 | bytes 23068672 | tf_op jit(solution)/shard_map/dot_general | solution.py:58
  245.0 0.0 reduce-scatter.5.cloned.1.call-update
  245.0 5.3 %reshape.53 = bf16[4,128,32,64]{3,2,1,0:T(8,128)(2,1)} reshape(bf16[512,2048]{1,0:T(8,128)(2,1)S(1)} %multiply_convert_fusion) | data formatting | bytes 4194304 | tf_op jit(solution)/shard_map/reshape | solution.py:38
  250.4 0.0 copy-start.1
  250.4 7.7 %copy.18 = bf16[4,128,32,64]{1,2,3,0:T(8,128)(2,1)S(1)} copy(bf16[4,128,32,64]{3,2,1,0:T(8,128)(2,1)} %reshape.53) | data formatting | bytes 4194304 | tf_op jit(solution)/shard_map/reshape | solution.py:38
  258.1 0.0 copy-done.1
  258.1 0.5 convolution_convert_fusion.2
  258.6 8.4 %copy.25 = bf16[4,4,128,64]{1,0,3,2:T(4,128)(2,1)} copy(bf16[4,4,128,64]{2,1,3,0:T(4,128)(2,1)S(1)} %convolution_convert_fusion.2) | data formatting | bytes 524288 | tf_op jit(solution)/shard_map/convert_element_type | solution.py:42
  266.9 16.2 %reshape.56 = bf16[32,2,2048]{2,1,0:T(2,128)(2,1)S(1)} reshape(bf16[8192,1,4,4]{3,2,1,0:T(4,128)(2,1)} %bitcast.35) | data formatting | bytes 524288
  283.1 14.1 %all_to_all.18 = bf16[32,2,2048]{2,1,0:T(2,128)(2,1)S(1)} all-to-all(bf16[32,2,2048]{2,1,0:T(2,128)(2,1)S(1)} %reshape.56), channel_id=1, replica_groups=mesh['tok'=4,'lat'=32] {'lat'}, dimensions={0} | all-to-all | bytes 524288 | tf_op jit(solution)/shard_map/all_to_all | solution.py:43
  297.3 19.0 %reshape.57 = bf16[8192,1,4,4]{3,2,1,0:T(4,128)(2,1)} reshape(bf16[32,2,2048]{2,1,0:T(2,128)(2,1)S(1)} %all_to_all.18) | data formatting | bytes 524288
  316.2 12.4 %copy.21 = bf16[4,1,4,32,256]{4,2,3,0,1:T(4,128)(2,1)} copy(bf16[4,1,4,32,256]{2,0,4,3,1:T(4,128)(2,1)} %bitcast.36) | data formatting | bytes 524288 | tf_op jit(solution)/shard_map/all_to_all | solution.py:43
  328.6 0.7 bitcast_convert_fusion
  329.3 63.2 %reduce-scatter.5.cloned.1.call-done = bf16[2048,1024]{1,0:T(8,128)(2,1)} async-done(((bf16[2048,4096]{1,0:T(8,128)(2,1)}), bf16[2048,1024]{1,0:T(8,128)(2,1)}) %reduce-scatter.5.cloned.1.call-update) | async-done | bytes 4194320 | tf_op jit(solution)/shard_map/reduce_scatter | solution.py:62
  392.5 6.6 %convert_element_type.69 = f32[2048,1024]{1,0:T(8,128)} convert(bf16[2048,1024]{1,0:T(8,128)(2,1)} %reduce-scatter.5.cloned.1.call-done) | non-fusion elementwise | flops 2097152 | bytes 12582912 | tf_op jit(solution)/shard_map/convert_element_type | solution.py:64
Async XLA Ops:
  7.2 55.8 %all-gather.3.cloned.1.call-start = ((), (), s32[]{:S(2)}) async-start(), calls=%async_computation.3 | async-start | bytes 4325376 | tf_op jit(solution)/shard_map/all_gather | solution.py:17
  7.9 169.0 %reduce-scatter.7.cloned.1.call-start = ((), (), s32[]{:S(2)}) async-start(), calls=%async_computation.6 | async-start | bytes 4325376
  12.6 50.4 %copy-start.2 = (f32[4096]{0:T(1024)S(1)}, f32[4096]{0:T(1024)}, u32[]{:S(2)}) copy-start(f32[4096]{0:T(1024)} %param.9) | copy-start | bytes 49156
  12.6 50.4 %copy-start.3 = (f32[2048]{0:T(1024)S(1)}, f32[2048]{0:T(1024)}, u32[]{:S(2)}) copy-start(f32[2048]{0:T(1024)} %param.8) | copy-start | bytes 24580
  97.4 80.5 %copy-start = (bf16[512,128]{1,0:T(8,128)(2,1)S(1)}, bf16[512,128]{1,0:T(8,128)(2,1)}, u32[]{:S(2)}) copy-start(bf16[512,128]{1,0:T(8,128)(2,1)} %param.6) | copy-start | bytes 393220
  97.4 133.0 %all-gather.5.cloned.1.call-start = ((), (), s32[]{:S(2)}) async-start(), calls=%async_computation.4 | async-start | bytes 4325376 | tf_op jit(solution)/shard_map/all_gather | solution.py:57
  178.7 213.9 %reduce-scatter.5.cloned.1.call-start = ((), (), s32[]{:S(2)}) async-start(), calls=%async_computation.5 | async-start | bytes 20971520 | tf_op jit(solution)/shard_map/reduce_scatter | solution.py:62
  250.4 7.8 %copy-start.1 = (s32[4,1,4]{2,1,0:T(1,128)S(1)}, s32[4,1,4]{2,1,0:T(1,128)}, u32[]{:S(2)}) copy-start(s32[4,1,4]{2,1,0:T(1,128)} %param.10) | copy-start | bytes 196
Sparse Core Ops, SparseCore 0:
  10.2 52.7 all-gather.2
  97.6 79.2 reduce-scatter.6
  179.9 50.5 all-gather.4
  245.2 147.3 reduce-scatter.4
where the time goes:
time: 406 us
  waiting for transfers between devices  240 us (59%)
  local copies, waits for them, and re-layouts  85.1 us (21%)
  matrix products  43 us (11%)
  blocking collectives  14.1 us (3%)
  between operations  13.8 us (3%)
  other arithmetic  9.52 us (2%)
    unnamed x5, waiting for transfers between devices  80 us
    reduce_scatter x1, waiting for transfers between devices, body(): lax.psum_scatter(partial_value.astype(jnp.bfloat16), 'tok', scatter_dimen...  63.2 us
    all_gather x1, waiting for transfers between devices, body(): error_full = lax.all_gather(error_part, 'lat', axis=1, tiled=True)  51.6 us
    unnamed x13, local copies, waits for them, and re-layouts  45.1 us
    all_gather x1, waiting for transfers between devices, body(): gathered = lax.all_gather(residuals, 'lat', axis=1, tiled=True)  44.9 us
    dot_general x1, matrix products, body(): lax.dot_general(code_values, error_full, (((0,), (0,)), ((), ())), prefer...  14.6 us
    dot_general x1, matrix products, body(): lax.dot_general(centered, dictionary, (((1,), (1,)), ((), ())), preferred...  14.3 us
    all_to_all x1, blocking collectives, body(): lax.all_to_all(tile_send, 'lat', split_axis=3, concat_axis=1, tiled=True)  14.1 us
  transfers between devices with their start and end apart: 4, of which 4 were waited for; matrix products, arithmetic and copies ran while one was open for 20% of the time, Pallas kernels for 0%

commit v1 on v0

v1 whole, which is shorter than its diff:
```python
import jax
import jax.numpy as jnp
from jax import lax
from jax.experimental import pallas as pl
from jax.experimental.pallas import tpu as pltpu
from jax.sharding import PartitionSpec as P

TILE_ROWS = 128
LAT_TILE = 64
CAP = 4
SIDE = 4
ROWS = 512
WIDTH = 4096
PIECE = 128
SHIFTS = (0, 1, 3, 2)
BF = jnp.bfloat16
F32 = jnp.float32


def lat_of(y, x, c):
    return (y % SIDE) * 8 + (x % SIDE) * 2 + c


def chips():
    return [(y, x, c) for y in range(SIDE) for x in range(SIDE) for c in range(2)]


def short_leg(d):
    return [
        (lat_of(y, x, c), lat_of(y + d, x, c) if c == 0 else lat_of(y, x + d, c))
        for y, x, c in chips()
    ]


def long_leg(d):
    return [
        (lat_of(y, x, c), lat_of(y, x + d, c) if c == 0 else lat_of(y + d, x, c))
        for y, x, c in chips()
    ]


CORE = [(lat_of(y, x, c), lat_of(y, x, 1 - c)) for y, x, c in chips()]
TO_PLANE = [
    (z * 32 + lat_of(y, x, c), ((z + y) % SIDE) * 32 + lat_of(y, x, c))
    for z in range(SIDE)
    for y, x, c in chips()
]
TO_HOME = [
    (z * 32 + lat_of(y, x, c), z * 32 + lat_of(y + z, x, c))
    for z in range(SIDE)
    for y, x, c in chips()
]


def send(value, pairs):
    return lax.ppermute(value, "lat", pairs)


def params(mib):
    return pltpu.CompilerParams(vmem_limit_bytes=mib << 20)


def stack_kernel(a, b, c, d, out):
    for k, ref in enumerate((a, b, c, d)):
        out[k] = ref[...]


def stack4(parts):
    shape = parts[0].shape
    return pl.pallas_call(
        stack_kernel,
        out_shape=jax.ShapeDtypeStruct((4,) + shape, BF),
        compiler_params=params(8),
        name="stack4",
    )(*parts)


def gather_plane(piece):
    line = stack4([piece] + [send(piece, short_leg(d)) for d in SHIFTS[1:]])
    mine = [line] + [send(line, long_leg(d)) for d in SHIFTS[1:]]
    other = [send(v, CORE) for v in mine]
    return mine + other


def encode_kernel(
    ids, counts, where, *refs
):
    pieces = refs[:8]
    tiles = refs[8:12]
    enc_bias, dec_bias = refs[12:14]
    codes_t, tile_send, mine, other, resid, centered = refs[14:]
    b = pl.program_id(0)
    for k in range(8):
        for e in range(4):
            slot = k * 4 + e
            off = pl.multiple_of(where[slot] * PIECE, PIECE)
            raw = pieces[k][e]
            centered[:, pl.ds(off, PIECE)] = (
                raw.astype(F32) - dec_bias[:, pl.ds(off, PIECE)]
            ).astype(BF)
            if k == 0 or (k < 4 and e == 0):

                @pl.when(where[32] == slot)
                def _():
                    resid[...] = raw

    step = 512
    preact = jnp.zeros((TILE_ROWS, CAP * LAT_TILE), F32)
    for k in range(0, WIDTH, step):
        block = jnp.concatenate([t[:, k : k + step] for t in tiles], axis=0)
        preact += lax.dot_general(
            centered[:, k : k + step],
            block,
            (((1,), (1,)), ((), ())),
            preferred_element_type=F32,
        )
    bias = jnp.concatenate(
        [enc_bias[pl.ds(ids[b, s], 1), :] for s in range(CAP)], axis=1
    )
    slot_of = lax.broadcasted_iota(jnp.int32, (TILE_ROWS, CAP * LAT_TILE), 1) // LAT_TILE
    live = slot_of < counts[b]
    values = jnp.where(live, jnp.maximum(preact + bias, 0.0), 0.0)
    codes = values.astype(BF)
    codes_t[...] = values.T.astype(BF)

    stacked = jnp.concatenate(
        [codes[:, s * LAT_TILE : (s + 1) * LAT_TILE] for s in range(CAP)], axis=0
    )
    size = CAP * TILE_ROWS
    row = lax.broadcasted_iota(jnp.int32, (size, size), 0)
    col = lax.broadcasted_iota(jnp.int32, (size, size), 1)
    j, l, c = row // TILE_ROWS, (row % TILE_ROWS) // CAP, row % CAP
    pick = (col == c * TILE_ROWS + 4 * l + j).astype(F32).astype(BF)
    slabs = jnp.dot(pick, stacked, preferred_element_type=F32)
    packed = jnp.concatenate(
        [slabs[s * TILE_ROWS : (s + 1) * TILE_ROWS] for s in range(4)], axis=1
    )
    tile_send[...] = packed.reshape(32, 1, CAP, 4 * LAT_TILE).astype(BF)

    core0 = where[33] == 0
    for n in range(0, WIDTH, step):
        block = jnp.concatenate([t[:, n : n + step] for t in tiles], axis=0)
        part = jnp.dot(codes, block, preferred_element_type=F32)
        for p in range(0, step, 2 * PIECE):
            first = part[:, p : p + PIECE]
            second = part[:, p + PIECE : p + 2 * PIECE]
            at = (n + p) // (2 * PIECE)
            mine[at] = jnp.where(core0, first, second).astype(BF)
            other[at] = jnp.where(core0, second, first).astype(BF)


def encode(ids, counts, where, pieces, dictionary, enc_bias, dec_bias):
    def rows(shape, index):
        return pl.BlockSpec(shape, index)

    piece_spec = rows((4, TILE_ROWS, PIECE), lambda b, *_: (0, b, 0))
    tile_specs = [
        rows((LAT_TILE, WIDTH), lambda b, i, n, w, s=s: (i[b, s], 0)) for s in range(CAP)
    ]
    whole = lambda b, *_: (0, 0)
    return pl.pallas_call(
        encode_kernel,
        grid_spec=pltpu.PrefetchScalarGridSpec(
            num_scalar_prefetch=3,
            grid=(4,),
            in_specs=[piece_spec] * 8
            + tile_specs
            + [rows((32, LAT_TILE), whole), rows((1, WIDTH), whole)],
            out_specs=[
                rows((CAP * LAT_TILE, TILE_ROWS), lambda b, *_: (b, 0)),
                rows((32, 1, CAP, 4 * LAT_TILE), lambda b, *_: (0, b, 0, 0)),
                rows((16, TILE_ROWS, PIECE), lambda b, *_: (0, b, 0)),
                rows((16, TILE_ROWS, PIECE), lambda b, *_: (0, b, 0)),
                rows((TILE_ROWS, PIECE), lambda b, *_: (b, 0)),
            ],
            scratch_shapes=[pltpu.VMEM((TILE_ROWS, WIDTH), BF)],
        ),
        out_shape=[
            jax.ShapeDtypeStruct((4 * CAP * LAT_TILE, TILE_ROWS), BF),
            jax.ShapeDtypeStruct((32, 4, CAP, 4 * LAT_TILE), BF),
            jax.ShapeDtypeStruct((16, ROWS, PIECE), BF),
            jax.ShapeDtypeStruct((16, ROWS, PIECE), BF),
            jax.ShapeDtypeStruct((ROWS, PIECE), BF),
        ],
        compiler_params=params(40),
        cost_estimate=pl.CostEstimate(
            flops=4 * 10**9, bytes_accessed=20 << 20, transcendentals=0
        ),
        name="encode",
    )(ids, counts, where, *pieces, *([dictionary] * CAP), enc_bias, dec_bias)


def first_sum_kernel(table, *refs):
    for k in range(3):
        a, b, out = refs[k], refs[3 + k], refs[6 + k]
        out[...] = (a[...].astype(F32) + b[...].astype(F32)).astype(BF)


def first_sum(table, mine, got):
    specs = [
        pl.BlockSpec((1, ROWS, PIECE), lambda e, tab, k=k: (tab[4 * k + e], 0, 0))
        for k in range(1, 4)
    ]
    return pl.pallas_call(
        first_sum_kernel,
        grid_spec=pltpu.PrefetchScalarGridSpec(
            num_scalar_prefetch=1,
            grid=(4,),
            in_specs=specs + specs,
            out_specs=[pl.BlockSpec((1, ROWS, PIECE), lambda e, tab: (e, 0, 0))] * 3,
        ),
        out_shape=[jax.ShapeDtypeStruct((4, ROWS, PIECE), BF)] * 3,
        compiler_params=params(16),
        name="first_sum",
    )(table, *([mine] * 3), *([got] * 3))


def second_sum_kernel(table, *refs):
    far = refs[6:9]
    for k in range(3):
        total = refs[k][0].astype(F32) + refs[3 + k][0].astype(F32)
        for ref in far:
            total += ref[k + 1].astype(F32)
        refs[9 + k][...] = total.astype(BF)


def second_sum(table, mine, got, far):
    half = ROWS // 2
    specs = [
        pl.BlockSpec((1, half, PIECE), lambda i, tab, e=e: (tab[e], i, 0)) for e in range(1, 4)
    ]
    return pl.pallas_call(
        second_sum_kernel,
        grid_spec=pltpu.PrefetchScalarGridSpec(
            num_scalar_prefetch=1,
            grid=(2,),
            in_specs=specs
            + specs
            + [pl.BlockSpec((4, half, PIECE), lambda i, tab: (0, i, 0))] * 3,
            out_specs=[pl.BlockSpec((half, PIECE), lambda i, tab: (i, 0))] * 3,
        ),
        out_shape=[jax.ShapeDtypeStruct((ROWS, PIECE), BF)] * 3,
        compiler_params=params(16),
        name="second_sum",
    )(table, *([mine] * 3), *([got] * 3), *far)


def error_kernel(table, *refs):
    dec_bias, resid, out, error = refs[8:]
    total = refs[0][0].astype(F32) + refs[1][0].astype(F32)
    for ref in refs[2:5]:
        total += ref[0].astype(F32)
    for ref in refs[5:8]:
        total += ref[...].astype(F32)
    total += dec_bias[...]
    out[...] = total.astype(BF)
    error[...] = (total - resid[...].astype(F32)).astype(BF)


def error_of(table, mine, got, far, near, dec_bias, resid):
    piece = pl.BlockSpec((ROWS, PIECE), lambda i, tab: (0, 0))
    own = pl.BlockSpec((1, ROWS, PIECE), lambda i, tab: (tab[0], 0, 0))
    return pl.pallas_call(
        error_kernel,
        grid_spec=pltpu.PrefetchScalarGridSpec(
            num_scalar_prefetch=1,
            grid=(1,),
            in_specs=[own, own]
            + [pl.BlockSpec((1, ROWS, PIECE), lambda i, tab: (0, 0, 0))] * 3
            + [piece] * 3
            + [pl.BlockSpec((1, PIECE), lambda i, tab: (0, tab[16])), piece],
            out_specs=[piece, piece],
        ),
        out_shape=[jax.ShapeDtypeStruct((ROWS, PIECE), BF)] * 2,
        compiler_params=params(16),
        name="error",
    )(table, mine, got, *far, *near, dec_bias, resid)


def grad_kernel(ids, where, *refs):
    pieces, codes = refs[:8], refs[8:12]
    out, error = refs[12:]

    @pl.when(pl.program_id(0) == 0)
    def _():
        for k in range(8):
            for e in range(4):
                at = k * 4 + e
                row = pl.multiple_of(where[2 * at] * ROWS, ROWS)
                col = where[2 * at + 1]
                error[col // 2, pl.ds(row, ROWS), pl.ds(pl.multiple_of(col % 2 * PIECE, PIECE), PIECE)] = pieces[k][e]

    n = pl.program_id(0)
    out[...] = jnp.zeros_like(out)
    for k, shift in enumerate(SHIFTS):
        for b in range(4):
            row = shift * ROWS + b * TILE_ROWS
            part = jnp.dot(
                codes[k][b * 256 : (b + 1) * 256, :],
                error[n, row : row + TILE_ROWS, :],
                preferred_element_type=F32,
            )
            for s in range(CAP):
                at = pl.multiple_of(ids[k * 16 + b * 4 + s] * LAT_TILE, LAT_TILE)
                out[pl.ds(at, LAT_TILE), :] += part[s * LAT_TILE : (s + 1) * LAT_TILE, :]


def grad(ids, where, pieces, codes):
    width = 2 * PIECE
    return pl.pallas_call(
        grad_kernel,
        grid_spec=pltpu.PrefetchScalarGridSpec(
            num_scalar_prefetch=2,
            grid=(4,),
            in_specs=[pl.BlockSpec((4, ROWS, PIECE), lambda n, *_: (0, 0, 0))] * 8
            + [pl.BlockSpec((4 * CAP * LAT_TILE, TILE_ROWS), lambda n, *_: (0, 0))] * 4,
            out_specs=pl.BlockSpec((2048, width), lambda n, *_: (0, n)),
            scratch_shapes=[pltpu.VMEM((4, 4 * ROWS, width), BF)],
        ),
        out_shape=jax.ShapeDtypeStruct((2048, 1024), F32),
        compiler_params=params(40),
        cost_estimate=pl.CostEstimate(
            flops=10**9, bytes_accessed=14 << 20, transcendentals=0
        ),
        name="grad",
    )(ids, where, *pieces, *codes)


def body(residuals, dictionary, enc_bias, dec_bias, tile_ids, tile_counts):
    t = lax.axis_index("tok")
    lat = lax.axis_index("lat")
    y, x, c = lat // 8, (lat // 2) % SIDE, lat % 2
    shifts = jnp.array(SHIFTS, jnp.int32)

    from_core = jnp.stack([c, 1 - c])[:, None, None]
    far, near = shifts[None, :, None], shifts[None, None, :]
    from_y = (y - jnp.where(from_core == 0, near, far)) % SIDE
    from_x = (x - jnp.where(from_core == 0, far, near)) % SIDE
    lat_from = (from_y * 8 + from_x * 2 + from_core).reshape(32)
    slot = jnp.array([0, 2, 3, 1], jnp.int32)[t]
    own_slot = jnp.where(c == 0, slot, 4 * slot)
    where = jnp.concatenate([lat_from, own_slot[None], c[None]]).astype(jnp.int32)
    grad_where = jnp.stack(
        [
            jnp.broadcast_to(from_y, (2, 4, 4)).reshape(32),
            (from_x * 2 + from_core).reshape(32),
        ],
        axis=1,
    ).reshape(64)
    to_y = jnp.where(c == 0, y + shifts[None, :], y + shifts[:, None])
    to_x = jnp.where(c == 0, x + shifts[:, None], x + shifts[None, :])
    table = (((to_y + t) % SIDE) * 4 + to_x % SIDE).reshape(16)
    own_lat = ((y + t) % SIDE) * 8 + x * 2 + c
    table = jnp.concatenate([table, own_lat[None]]).astype(jnp.int32)

    ids = tile_ids[:, 0, :]
    all_ids = lax.all_gather(ids, "tok", axis=0, tiled=False)
    ids_by_slot = jnp.concatenate(
        [lax.dynamic_index_in_dim(all_ids, (t - s) % SIDE, 0, True) for s in SHIFTS]
    ).reshape(64)

    pieces = gather_plane(residuals)
    codes_t, tile_send, mine, other, resid = encode(
        ids,
        tile_counts[:, 0],
        where,
        pieces,
        dictionary,
        enc_bias.reshape(32, LAT_TILE),
        dec_bias.reshape(1, WIDTH),
    )
    got = send(other, CORE)
    tile_got = lax.all_to_all(tile_send, "lat", split_axis=0, concat_axis=0, tiled=True)
    tile_codes = tile_got.transpose(1, 0, 2, 3)
    codes = [codes_t] + [
        lax.ppermute(codes_t, "tok", [(z, (z + s) % SIDE) for z in range(SIDE)])
        for s in SHIFTS[1:]
    ]

    lines = first_sum(table, mine, got)
    far_in = [send(v, long_leg(d)) for v, d in zip(lines, SHIFTS[1:])]
    parts = second_sum(table, mine, got, far_in)
    near_in = [send(v, short_leg(d)) for v, d in zip(parts, SHIFTS[1:])]
    recon, error = error_of(
        table, mine, got, far_in, near_in, dec_bias.reshape(1, WIDTH), resid
    )
    error = lax.ppermute(error, ("tok", "lat"), TO_PLANE)
    reconstruction = lax.ppermute(recon, ("tok", "lat"), TO_HOME)
    errors = gather_plane(error)
    decoder_grad = grad(ids_by_slot, grad_where, errors, codes)
    return (tile_codes, reconstruction, decoder_grad)


def solution(mesh):
    placed = (
        P("tok", "lat"),
        P("lat", None),
        P("lat"),
        P(),
        P("tok", "lat", None),
        P("tok", "lat"),
    )
    return jax.shard_map(
        body,
        mesh=mesh,
        in_specs=placed,
        out_specs=(P("tok", None, None, "lat"), P("tok", "lat"), P("lat", "tok")),
        check_vma=False,
    )
```

time: 406 us -> 178 us (0.44)
  waiting for transfers between devices: 240 us -> 38.2 us
  starting transfers between devices: 0.34 us -> 66 us
  local copies, waits for them, and re-layouts: 85.1 us -> 28.1 us
  matrix products: 43 us -> 0 us
  Pallas kernels: 0 us -> 27.7 us
  between operations: 13.8 us -> 2.16 us
  other arithmetic: 9.52 us -> 3.14 us
    all_gather x2 -> x0, waiting for transfers between devices: 96.5 us -> none  [the longest x1 51.6 us: body(): error_full = lax.all_gather(error_part, 'lat', axis=1, tiled=True)]
    unnamed x5 -> x0, waiting for transfers between devices: 80 us -> none
    reduce_scatter x1 -> x0, waiting for transfers between devices: 63.2 us -> none  [body(): lax.psum_scatter(partial_value.astype(jnp.bfloat16), 'tok', scatter_dimen...]
    ppermute x0 -> x32, starting transfers between devices: none -> 58 us  [the longest x27 50.2 us: send(): return lax.ppermute(value, 'lat', pairs)]
    dot_general x4 -> x0, matrix products: 43 us -> none  [the longest x1 14.6 us: body(): lax.dot_general(code_values, error_full, (((0,), (0,)), ((), ())), prefer...]
    ppermute x0 -> x32, waiting for transfers between devices: none -> 33.9 us  [the longest x27 33.9 us: send(): return lax.ppermute(value, 'lat', pairs)]
    pallas_call x0 -> x7, Pallas kernels: none -> 27.7 us  [the longest x1 13.5 us: encode(): pl.pallas_call(encode_kernel, grid_spec=pltpu.PrefetchScalarGridSpec(num_...]
    unnamed x13 -> x56, local copies, waits for them, and re-layouts: 45.1 us -> 20.9 us
  transfers between devices with their start and end apart: 4 -> 33, of which waited for: 4 -> 14; matrix products, arithmetic and copies ran while one was open for 20% -> 9% of each run, Pallas kernels for 0% -> 0%
where the time goes in v1:
time: 178 us; the launch traced here: 177 us
  starting transfers between devices  66 us (37%)
  waiting for transfers between devices  38.2 us (21%)
  local copies, waits for them, and re-layouts  28.1 us (16%)
  Pallas kernels  27.7 us (16%)
  blocking collectives  11.3 us (6%)
  other arithmetic  3.14 us (2%)
  between operations  2.16 us (1%)
    ppermute x27, starting transfers between devices, send(): return lax.ppermute(value, 'lat', pairs)  50.2 us
    ppermute x27, waiting for transfers between devices, send(): return lax.ppermute(value, 'lat', pairs)  33.9 us
    unnamed x56, local copies, waits for them, and re-layouts  20.9 us
    pallas_call x1, Pallas kernels, encode(): pl.pallas_call(encode_kernel, grid_spec=pltpu.PrefetchScalarGridSpec(num_...  13.5 us
    all_gather x1, blocking collectives, body(): all_ids = lax.all_gather(ids, 'tok', axis=0, tiled=False)  11.3 us
    all_to_all x1, starting transfers between devices, body(): lax.all_to_all(tile_send, 'lat', split_axis=0, concat_axis=0, tiled=True)  8.01 us
    pallas_call x1, Pallas kernels, grad(): pl.pallas_call(grad_kernel, grid_spec=pltpu.PrefetchScalarGridSpec(num_sc...  7.68 us
    ppermute x3, starting transfers between devices, body(): lax.ppermute(codes_t, 'tok', [(z, (z + s) % SIDE) for z in range(SIDE)])  5.54 us
  transfers between devices with their start and end apart: 33, of which 14 were waited for; matrix products, arithmetic and copies ran while one was open for 9% of the time, Pallas kernels for 0%

profile of v1, /device:TPU:1, one launch (start us, length us, event | category | flops | bytes accessed | tf_op | source)
XLA Modules:
  0.0 176.7 jit_solution(11910271467971855155)
XLA Ops:
  0.6 3.4 %collective-permute-start.1 = (bf16[512,128]{1,0:T(8,128)(2,1)}, bf16[512,128]{1,0:T(8,128)(2,1)S(1)}, u32[]{:S(2)}, u32[]{:S(2)}) collective-permute-start(bf16[512,128]{1,0:T(8,128)(2,1)} %a.1), channel_id=1, source_target_pairs={{0,24},{1,7},{2,26},{3,1},{4,28},{5,3},{6,30},{7,5},{8,0},{9,15},{... | collective-permute-start | bytes 393224 | tf_op jit(solution)/shard_map/ppermute | solution.py:56
  4.0 1.7 collective-permute-start.2
  6.3 4.7 %collective-permute-done.b = bf16[512,128]{1,0:T(8,128)(2,1)S(1)} collective-permute-done((bf16[512,128]{1,0:T(8,128)(2,1)}, bf16[512,128]{1,0:T(8,128)(2,1)S(1)}, u32[]{:S(2)}, u32[]{:S(2)}) %collective-permute-start) | collective-permute-done | bytes 131104 | tf_op jit(solution)/shard_map/ppermute | solution.py:56
  11.0 0.9 copy-done.13
  11.9 2.7 %collective-permute-start.5 = (bf16[4,512,128]{2,1,0:T(8,128)(2,1)S(1)}, bf16[4,512,128]{2,1,0:T(8,128)(2,1)S(1)}, u32[]{:S(2)}, u32[]{:S(2)}) collective-permute-start(bf16[4,512,128]{2,1,0:T(8,128)(2,1)S(1)} %stack4.2.refs_0_), channel_id=1, source_target_pairs={{0,4},{1,17},{2,6},{3,19},{4,0},{5,21},{6,2},{7,23},{8,12},{9,25},... | collective-permute-start | bytes 1572872 | tf_op jit(solution)/shard_map/ppermute | solution.py:56
  14.6 0.8 collective-permute-start.4
  16.1 1.2 dynamic_slice.16
  18.2 3.1 %collective-permute-start.6 = (bf16[4,512,128]{2,1,0:T(8,128)(2,1)S(1)}, bf16[4,512,128]{2,1,0:T(8,128)(2,1)S(1)}, u32[]{:S(2)}, u32[]{:S(2)}) collective-permute-start(bf16[4,512,128]{2,1,0:T(8,128)(2,1)S(1)} %stack4.2.refs_0_), channel_id=1, source_target_pairs={{0,1},{1,0},{2,3},{3,2},{4,5},{5,4},{6,7},{7,6},{8,9},{9,8},{10,11... | collective-permute-start | bytes 1572872 | tf_op jit(solution)/shard_map/ppermute | solution.py:56
  21.8 3.0 %collective-permute-start.9 = (bf16[4,512,128]{2,1,0:T(8,128)(2,1)S(1)}, bf16[4,512,128]{2,1,0:T(8,128)(2,1)S(1)}, u32[]{:S(2)}, u32[]{:S(2)}) collective-permute-start(bf16[4,512,128]{2,1,0:T(8,128)(2,1)S(1)} %collective-permute-done.5.refs_3_), channel_id=1, source_target_pairs={{0,1},{1,0},{2,3},{3,2},{4,5},{5,4},{6,7},{7,6},{8,9},{9,8},{10,11... | collective-permute-start | bytes 1572872 | tf_op jit(solution)/shard_map/ppermute | solution.py:56
  24.8 3.0 %collective-permute-done.4.refs_2_ = bf16[4,512,128]{2,1,0:T(8,128)(2,1)S(1)} collective-permute-done((bf16[4,512,128]{2,1,0:T(8,128)(2,1)S(1)}, bf16[4,512,128]{2,1,0:T(8,128)(2,1)S(1)}, u32[]{:S(2)}, u32[]{:S(2)}) %collective-permute-start.4) | collective-permute-done | bytes 524320 | tf_op jit(solution)/shard_map/ppermute | solution.py:56
  27.8 2.7 %collective-permute-start.8 = (bf16[4,512,128]{2,1,0:T(8,128)(2,1)S(1)}, bf16[4,512,128]{2,1,0:T(8,128)(2,1)}, u32[]{:S(2)}, u32[]{:S(2)}) collective-permute-start(bf16[4,512,128]{2,1,0:T(8,128)(2,1)S(1)} %collective-permute-done.4.refs_2_), channel_id=1, source_target_pairs={{0,1},{1,0},{2,3},{3,2},{4,5},{5,4},{6,7},{7,6},{8,9},{9,8},{10,11... | collective-permute-start | bytes 1572872 | tf_op jit(solution)/shard_map/ppermute | solution.py:56
  30.5 0.8 copy-done
  31.3 0.8 copy-done.2
  32.1 0.8 select_subtract_fusion
  33.0 0.8 reshape.226.refs_12_
  34.6 0.8 copy-done.4
  35.4 0.8 copy-done.6
  36.2 1.0 copy-done.1
  37.2 1.0 copy-done.3
  38.3 1.0 copy-done.5
  39.3 1.0 copy-done.7
  40.4 0.7 copy-done.14
  42.4 13.5 %encode.1 = (bf16[1024,128]{1,0:T(8,128)(2,1)S(1)}, bf16[32,4,4,256]{3,2,1,0:T(4,128)(2,1)S(1)}, bf16[16,512,128]{2,1,0:T(8,128)(2,1)S(1)}, bf16[16,512,128]{2,1,0:T(8,128)(2,1)}, bf16[512,128]{1,0:T(8,128)(2,1)S(1)}) custom-call(s32[4,4]{1,0:T(4,128)S(1)} %bitcast.12, s32[4]{0:T(128)S(1)} %bitcast.13, s32[34]{0:T(128)S(1)} %pad_add_fusion.3.where, ...), custom_call_target="tpu_custom_call" | custom-call | flops 4000000000 | bytes 20971520 | tf_op jit(solution)/shard_map/encode/pallas_call | solution.py:161
  55.9 0.7 copy-done.12
  58.1 3.1 %collective-permute-done.10.refs_3_.refs_4_.refs_5_.refs_1_ = bf16[16,512,128]{2,1,0:T(8,128)(2,1)} collective-permute-done((bf16[16,512,128]{2,1,0:T(8,128)(2,1)}, bf16[16,512,128]{2,1,0:T(8,128)(2,1)}, u32[]{:S(2)}, u32[]{:S(2)}) %collective-permute-start.10) | collective-permute-done | bytes 2097184 | tf_op jit(solution)/shard_map/ppermute | solution.py:56
  61.3 3.1 %first_sum.1 = (bf16[4,512,128]{2,1,0:T(8,128)(2,1)S(1)}, bf16[4,512,128]{2,1,0:T(8,128)(2,1)S(1)}, bf16[4,512,128]{2,1,0:T(8,128)(2,1)S(1)}) custom-call(s32[17]{0:T(128)S(1)} %pad_add_fusion.4.table, bf16[16,512,128]{2,1,0:T(8,128)(2,1)S(1)} %get-tuple-element.17.refs_0_.refs_1_.refs_2_, ...), custom_call_target="tpu_custom_call" | custom-call | tf_op jit(solution)/shard_map/first_sum/pallas_call | solution.py:204
  64.4 2.7 %collective-permute-start.12 = (bf16[4,512,128]{2,1,0:T(8,128)(2,1)S(1)}, bf16[4,512,128]{2,1,0:T(8,128)(2,1)S(1)}, u32[]{:S(2)}, u32[]{:S(2)}) collective-permute-start(bf16[4,512,128]{2,1,0:T(8,128)(2,1)S(1)} %get-tuple-element.20), channel_id=1, source_target_pairs={{0,6},{1,25},{2,0},{3,27},{4,2},{5,29},{6,4},{7,31},{8,14},{9,1},{... | collective-permute-start | bytes 1572872 | tf_op jit(solution)/shard_map/ppermute | solution.py:56
  67.4 6.5 %collective-permute-done.11.refs_6_.refs_2_ = bf16[4,512,128]{2,1,0:T(8,128)(2,1)S(1)} collective-permute-done((bf16[4,512,128]{2,1,0:T(8,128)(2,1)S(1)}, bf16[4,512,128]{2,1,0:T(8,128)(2,1)S(1)}, u32[]{:S(2)}, u32[]{:S(2)}) %collective-permute-start.11) | collective-permute-done | bytes 524320 | tf_op jit(solution)/shard_map/ppermute | solution.py:56
  73.9 4.9 %collective-permute-done.12.refs_7_.refs_3_ = bf16[4,512,128]{2,1,0:T(8,128)(2,1)S(1)} collective-permute-done((bf16[4,512,128]{2,1,0:T(8,128)(2,1)S(1)}, bf16[4,512,128]{2,1,0:T(8,128)(2,1)S(1)}, u32[]{:S(2)}, u32[]{:S(2)}) %collective-permute-start.12) | collective-permute-done | bytes 524320 | tf_op jit(solution)/shard_map/ppermute | solution.py:56
  78.8 1.1 collective-permute-done.13.refs_8_.refs_4_
  79.9 1.8 %second_sum.1 = (bf16[512,128]{1,0:T(8,128)(2,1)S(1)}, bf16[512,128]{1,0:T(8,128)(2,1)S(1)}, bf16[512,128]{1,0:T(8,128)(2,1)S(1)}) custom-call(s32[17]{0:T(128)S(1)} %pad_add_fusion.4.table, bf16[16,512,128]{2,1,0:T(8,128)(2,1)S(1)} %get-tuple-element.17.refs_0_.refs_1_.refs_2_, bf16[16,512,128]{2,1,0:T(8,128)(2,1)S(1)} %get-tuple-element.17.refs_0_.refs_1_.refs_2_, ...), custom_call_target="tpu_custom_call" | custom-call | tf_op jit(solution)/shard_map/second_sum/pallas_call | solution.py:232
  81.7 1.0 collective-permute-start.14
  82.7 1.8 collective-permute-start.15
  84.4 0.9 collective-permute-start.16
  85.3 1.5 collective-permute-done.14.refs_5_
  86.8 3.0 %collective-permute-done.16.refs_7_ = bf16[512,128]{1,0:T(8,128)(2,1)S(1)} collective-permute-done((bf16[512,128]{1,0:T(8,128)(2,1)S(1)}, bf16[512,128]{1,0:T(8,128)(2,1)S(1)}, u32[]{:S(2)}, u32[]{:S(2)}) %collective-permute-start.16) | collective-permute-done | bytes 131104 | tf_op jit(solution)/shard_map/ppermute | solution.py:56
  89.8 1.6 error.1
  92.1 0.9 collective-permute-start.21
  93.0 2.0 %collective-permute-start.20 = (bf16[512,128]{1,0:T(8,128)(2,1)S(1)}, bf16[512,128]{1,0:T(8,128)(2,1)S(1)}, u32[]{:S(2)}, u32[]{:S(2)}) collective-permute-start(bf16[512,128]{1,0:T(8,128)(2,1)S(1)} %collective-permute-done.18.a), channel_id=1, source_target_pairs={{0,24},{1,7},{2,26},{3,1},{4,28},{5,3},{6,30},{7,5},{8,0},{9,15},{... | collective-permute-start | bytes 393224 | tf_op jit(solution)/shard_map/ppermute | solution.py:56
  95.0 2.5 %collective-permute-done.21.d = bf16[512,128]{1,0:T(8,128)(2,1)S(1)} collective-permute-done((bf16[512,128]{1,0:T(8,128)(2,1)S(1)}, bf16[512,128]{1,0:T(8,128)(2,1)S(1)}, u32[]{:S(2)}, u32[]{:S(2)}) %collective-permute-start.21) | collective-permute-done | bytes 131104 | tf_op jit(solution)/shard_map/ppermute | solution.py:56
  97.6 2.4 %collective-permute-done.19.b = bf16[512,128]{1,0:T(8,128)(2,1)S(1)} collective-permute-done((bf16[512,128]{1,0:T(8,128)(2,1)S(1)}, bf16[512,128]{1,0:T(8,128)(2,1)S(1)}, u32[]{:S(2)}, u32[]{:S(2)}) %collective-permute-start.19) | collective-permute-done | bytes 131104 | tf_op jit(solution)/shard_map/ppermute | solution.py:56
  100.1 6.8 %collective-permute-start.24 = (bf16[4,512,128]{2,1,0:T(8,128)(2,1)S(1)}, bf16[4,512,128]{2,1,0:T(8,128)(2,1)S(1)}, u32[]{:S(2)}, u32[]{:S(2)}) collective-permute-start(bf16[4,512,128]{2,1,0:T(8,128)(2,1)S(1)} %stack4.3.refs_0_), channel_id=1, source_target_pairs={{0,4},{1,17},{2,6},{3,19},{4,0},{5,21},{6,2},{7,23},{8,12},{9,25},... | collective-permute-start | bytes 1572872 | tf_op jit(solution)/shard_map/ppermute | solution.py:56
  106.9 3.2 %collective-permute-start.23 = (bf16[4,512,128]{2,1,0:T(8,128)(2,1)S(1)}, bf16[4,512,128]{2,1,0:T(8,128)(2,1)S(1)}, u32[]{:S(2)}, u32[]{:S(2)}) collective-permute-start(bf16[4,512,128]{2,1,0:T(8,128)(2,1)S(1)} %stack4.3.refs_0_), channel_id=1, source_target_pairs={{0,6},{1,25},{2,0},{3,27},{4,2},{5,29},{6,4},{7,31},{8,14},{9,1},{... | collective-permute-start | bytes 1572872 | tf_op jit(solution)/shard_map/ppermute | solution.py:56
  110.2 1.7 collective-permute-start.31
  111.9 1.4 collective-permute-start.30
  113.3 11.3 %all-gather = s32[16,1,4]{2,1,0:T(1,128)S(1)} all-gather(s32[4,1,4]{2,1,0:T(1,128)S(1)} %copy-done.17), channel_id=2, replica_groups=mesh['tok'=4,'lat'=32] {'tok'}, dimensions={0}, use_global_device_ids=true | all-gather | bytes 320 | tf_op jit(solution)/shard_map/all_gather | solution.py:357
  124.6 0.7 copy-done.8
  125.4 1.6 collective-permute-start.17
  126.9 0.7 copy-done.10
  127.6 11.4 %collective-permute-start.25 = (bf16[4,512,128]{2,1,0:T(8,128)(2,1)S(1)}, bf16[4,512,128]{2,1,0:T(8,128)(2,1)S(1)}, u32[]{:S(2)}, u32[]{:S(2)}) collective-permute-start(bf16[4,512,128]{2,1,0:T(8,128)(2,1)S(1)} %stack4.3.refs_0_), channel_id=1, source_target_pairs={{0,1},{1,0},{2,3},{3,2},{4,5},{5,4},{6,7},{7,6},{8,9},{9,8},{10,11... | collective-permute-start | bytes 1572872 | tf_op jit(solution)/shard_map/ppermute | solution.py:56
  140.8 1.3 sub.72
  142.7 0.7 copy.24
  143.5 0.8 copy.26
  144.2 1.3 copy.25
  145.5 1.3 copy.27
  147.7 8.0 %all-to-all-start = ((bf16[32,4,4,256]{3,2,1,0:T(4,128)(2,1)}), bf16[32,4,4,256]{3,2,1,0:T(4,128)(2,1)}, u32[]{:S(2)}, u32[]{:S(2)}) async-start(bf16[32,4,4,256]{3,2,1,0:T(4,128)(2,1)} %copy-done.12), calls=%async_computation | async-start | bytes 524288 | tf_op jit(solution)/shard_map/all_to_all | solution.py:373
  155.8 2.5 %collective-permute-start.29 = (bf16[1024,128]{1,0:T(8,128)(2,1)S(1)}, bf16[1024,128]{1,0:T(8,128)(2,1)}, u32[]{:S(2)}, u32[]{:S(2)}) collective-permute-start(bf16[1024,128]{1,0:T(8,128)(2,1)S(1)} %get-tuple-element.28.refs_8_), channel_id=1, source_target_pairs={{0,32},{32,64},{64,96},{96,0},{1,33},{33,65},{65,97},{97,1},{2,34}... | collective-permute-start | bytes 786440 | tf_op jit(solution)/shard_map/ppermute | solution.py:376
  158.9 0.7 copy.21
  159.6 0.8 reshape.229.where
  160.4 4.3 %all-to-all-done = bf16[32,4,4,256]{3,2,1,0:T(4,128)(2,1)} async-done(((bf16[32,4,4,256]{3,2,1,0:T(4,128)(2,1)}), bf16[32,4,4,256]{3,2,1,0:T(4,128)(2,1)}, u32[]{:S(2)}, u32[]{:S(2)}) %all-to-all-start) | async-done | bytes 262176 | tf_op jit(solution)/shard_map/all_to_all | solution.py:373
  164.7 1.7 copy.22
  166.5 0.9 copy-done.9
  167.4 0.9 copy-done.11
  168.4 7.7 %grad.1 = f32[2048,1024]{1,0:T(8,128)} custom-call(s32[64]{0:T(128)S(1)} %reshape.228.ids, s32[64]{0:T(128)S(1)} %reshape.229.where, bf16[4,512,128]{2,1,0:T(8,128)(2,1)S(1)} %stack4.3.refs_0_, bf16[4,512,128]{2,1,0:T(8,128)(2,1)S(1)} %collective-permute-done.22.refs_1_, bf16[4,512,128]{2,1,0:T(8,128)(2,1)S(1)} %collective-permute-done.23.refs_2_, ...), custom_call_target="tpu_custom_call" | custom-call | flops 1000000000 | bytes 14680064 | tf_op jit(solution)/shard_map/grad/pallas_call | solution.py:310
  (93 shorter events, 11.2 us)
Async XLA Ops:
  0.6 5.6 %collective-permute-start.1 = (bf16[512,128]{1,0:T(8,128)(2,1)}, bf16[512,128]{1,0:T(8,128)(2,1)S(1)}, u32[]{:S(2)}, u32[]{:S(2)}) collective-permute-start(bf16[512,128]{1,0:T(8,128)(2,1)} %a.1), channel_id=1, source_target_pairs={{0,24},{1,7},{2,26},{3,1},{4,28},{5,3},{6,30},{7,5},{8,0},{9,15},{... | collective-permute-start | bytes 393224 | tf_op jit(solution)/shard_map/ppermute | solution.py:56
  4.0 6.9 %collective-permute-start = (bf16[512,128]{1,0:T(8,128)(2,1)}, bf16[512,128]{1,0:T(8,128)(2,1)S(1)}, u32[]{:S(2)}, u32[]{:S(2)}) collective-permute-start(bf16[512,128]{1,0:T(8,128)(2,1)} %a.1), channel_id=1, source_target_pairs={{0,8},{1,3},{2,10},{3,5},{4,12},{5,7},{6,14},{7,1},{8,16},{9,11},{... | collective-permute-start | bytes 393224 | tf_op jit(solution)/shard_map/ppermute | solution.py:56
  4.0 6.9 %collective-permute-start.2 = (bf16[512,128]{1,0:T(8,128)(2,1)}, bf16[512,128]{1,0:T(8,128)(2,1)S(1)}, u32[]{:S(2)}, u32[]{:S(2)}) collective-permute-start(bf16[512,128]{1,0:T(8,128)(2,1)} %a.1), channel_id=1, source_target_pairs={{0,16},{1,5},{2,18},{3,7},{4,20},{5,1},{6,22},{7,3},{8,24},{9,13},... | collective-permute-start | bytes 393224 | tf_op jit(solution)/shard_map/ppermute | solution.py:56
  10.9 0.9 copy-start.13
  11.9 10.0 %collective-permute-start.5 = (bf16[4,512,128]{2,1,0:T(8,128)(2,1)S(1)}, bf16[4,512,128]{2,1,0:T(8,128)(2,1)S(1)}, u32[]{:S(2)}, u32[]{:S(2)}) collective-permute-start(bf16[4,512,128]{2,1,0:T(8,128)(2,1)S(1)} %stack4.2.refs_0_), channel_id=1, source_target_pairs={{0,4},{1,17},{2,6},{3,19},{4,0},{5,21},{6,2},{7,23},{8,12},{9,25},... | collective-permute-start | bytes 1572872 | tf_op jit(solution)/shard_map/ppermute | solution.py:56
  14.6 13.2 %collective-permute-start.4 = (bf16[4,512,128]{2,1,0:T(8,128)(2,1)S(1)}, bf16[4,512,128]{2,1,0:T(8,128)(2,1)S(1)}, u32[]{:S(2)}, u32[]{:S(2)}) collective-permute-start(bf16[4,512,128]{2,1,0:T(8,128)(2,1)S(1)} %stack4.2.refs_0_), channel_id=1, source_target_pairs={{0,6},{1,25},{2,0},{3,27},{4,2},{5,29},{6,4},{7,31},{8,14},{9,1},{... | collective-permute-start | bytes 1572872 | tf_op jit(solution)/shard_map/ppermute | solution.py:56
  15.4 15.9 %collective-permute-start.3 = (bf16[4,512,128]{2,1,0:T(8,128)(2,1)S(1)}, bf16[4,512,128]{2,1,0:T(8,128)(2,1)S(1)}, u32[]{:S(2)}, u32[]{:S(2)}) collective-permute-start(bf16[4,512,128]{2,1,0:T(8,128)(2,1)S(1)} %stack4.2.refs_0_), channel_id=1, source_target_pairs={{0,2},{1,9},{2,4},{3,11},{4,6},{5,13},{6,0},{7,15},{8,10},{9,17},{... | collective-permute-start | bytes 1572872 | tf_op jit(solution)/shard_map/ppermute | solution.py:56
  18.1 18.1 %copy-start.20 = (s32[2,4,4]{2,1,0:T(4,128)}, s32[2,4,4]{2,1,0:T(4,128)S(1)}, u32[]{:S(2)}) copy-start(s32[2,4,4]{2,1,0:T(4,128)S(1)} %add.163) | copy-start | bytes 388
  18.2 16.4 %collective-permute-start.6 = (bf16[4,512,128]{2,1,0:T(8,128)(2,1)S(1)}, bf16[4,512,128]{2,1,0:T(8,128)(2,1)S(1)}, u32[]{:S(2)}, u32[]{:S(2)}) collective-permute-start(bf16[4,512,128]{2,1,0:T(8,128)(2,1)S(1)} %stack4.2.refs_0_), channel_id=1, source_target_pairs={{0,1},{1,0},{2,3},{3,2},{4,5},{5,4},{6,7},{7,6},{8,9},{9,8},{10,11... | collective-permute-start | bytes 1572872 | tf_op jit(solution)/shard_map/ppermute | solution.py:56
  21.8 13.5 %collective-permute-start.9 = (bf16[4,512,128]{2,1,0:T(8,128)(2,1)S(1)}, bf16[4,512,128]{2,1,0:T(8,128)(2,1)S(1)}, u32[]{:S(2)}, u32[]{:S(2)}) collective-permute-start(bf16[4,512,128]{2,1,0:T(8,128)(2,1)S(1)} %collective-permute-done.5.refs_3_), channel_id=1, source_target_pairs={{0,1},{1,0},{2,3},{3,2},{4,5},{5,4},{6,7},{7,6},{8,9},{9,8},{10,11... | collective-permute-start | bytes 1572872 | tf_op jit(solution)/shard_map/ppermute | solution.py:56
  27.8 8.4 %collective-permute-start.8 = (bf16[4,512,128]{2,1,0:T(8,128)(2,1)S(1)}, bf16[4,512,128]{2,1,0:T(8,128)(2,1)}, u32[]{:S(2)}, u32[]{:S(2)}) collective-permute-start(bf16[4,512,128]{2,1,0:T(8,128)(2,1)S(1)} %collective-permute-done.4.refs_2_), channel_id=1, source_target_pairs={{0,1},{1,0},{2,3},{3,2},{4,5},{5,4},{6,7},{7,6},{8,9},{9,8},{10,11... | collective-permute-start | bytes 1572872 | tf_op jit(solution)/shard_map/ppermute | solution.py:56
  30.5 0.8 copy-start
  31.3 4.9 %collective-permute-start.7 = (bf16[4,512,128]{2,1,0:T(8,128)(2,1)S(1)}, bf16[4,512,128]{2,1,0:T(8,128)(2,1)}, u32[]{:S(2)}, u32[]{:S(2)}) collective-permute-start(bf16[4,512,128]{2,1,0:T(8,128)(2,1)S(1)} %collective-permute-done.3.refs_1_), channel_id=1, source_target_pairs={{0,1},{1,0},{2,3},{3,2},{4,5},{5,4},{6,7},{7,6},{8,9},{9,8},{10,11... | collective-permute-start | bytes 1572872 | tf_op jit(solution)/shard_map/ppermute | solution.py:56
  31.3 0.8 copy-start.2
  32.9 3.3 %copy-start.22 = (s32[2,4,4]{2,1,0:T(4,128)}, s32[2,4,4]{2,1,0:T(4,128)S(1)}, u32[]{:S(2)}) copy-start(s32[2,4,4]{2,1,0:T(4,128)S(1)} %get-tuple-element.45) | copy-start | bytes 388
  32.9 3.3 %copy-start.24 = (s32[2,4,4]{2,1,0:T(4,128)}, s32[2,4,4]{2,1,0:T(4,128)S(1)}, u32[]{:S(2)}) copy-start(s32[2,4,4]{2,1,0:T(4,128)S(1)} %get-tuple-element.44) | copy-start | bytes 388
  34.6 0.8 copy-start.4
  35.4 0.8 copy-start.6
  36.2 1.0 copy-start.1
  37.2 1.0 copy-start.3
  38.3 1.0 copy-start.5
  39.3 1.0 copy-start.7
  40.4 0.7 copy-start.14
  41.1 0.7 copy-start.16
  41.8 0.7 copy-start.18
  55.9 0.7 copy-start.12
  56.6 4.6 %collective-permute-start.10 = (bf16[16,512,128]{2,1,0:T(8,128)(2,1)}, bf16[16,512,128]{2,1,0:T(8,128)(2,1)}, u32[]{:S(2)}, u32[]{:S(2)}) collective-permute-start(bf16[16,512,128]{2,1,0:T(8,128)(2,1)} %get-tuple-element.18), channel_id=1, source_target_pairs={{0,1},{1,0},{2,3},{3,2},{4,5},{5,4},{6,7},{7,6},{8,9},{9,8},{10,11... | collective-permute-start | bytes 6291464 | tf_op jit(solution)/shard_map/ppermute | solution.py:56
  64.3 9.6 %collective-permute-start.11 = (bf16[4,512,128]{2,1,0:T(8,128)(2,1)S(1)}, bf16[4,512,128]{2,1,0:T(8,128)(2,1)S(1)}, u32[]{:S(2)}, u32[]{:S(2)}) collective-permute-start(bf16[4,512,128]{2,1,0:T(8,128)(2,1)S(1)} %get-tuple-element.19), channel_id=1, source_target_pairs={{0,2},{1,9},{2,4},{3,11},{4,6},{5,13},{6,0},{7,15},{8,10},{9,17},{... | collective-permute-start | bytes 1572872 | tf_op jit(solution)/shard_map/ppermute | solution.py:56
  64.4 14.4 %collective-permute-start.12 = (bf16[4,512,128]{2,1,0:T(8,128)(2,1)S(1)}, bf16[4,512,128]{2,1,0:T(8,128)(2,1)S(1)}, u32[]{:S(2)}, u32[]{:S(2)}) collective-permute-start(bf16[4,512,128]{2,1,0:T(8,128)(2,1)S(1)} %get-tuple-element.20), channel_id=1, source_target_pairs={{0,6},{1,25},{2,0},{3,27},{4,2},{5,29},{6,4},{7,31},{8,14},{9,1},{... | collective-permute-start | bytes 1572872 | tf_op jit(solution)/shard_map/ppermute | solution.py:56
  67.1 22.7 %copy-start.15 = (f32[4096]{0:T(1024)S(1)}, f32[4096]{0:T(1024)}, u32[]{:S(2)}) copy-start(f32[4096]{0:T(1024)} %param.11) | copy-start | bytes 49156
  67.1 12.8 %collective-permute-start.13 = (bf16[4,512,128]{2,1,0:T(8,128)(2,1)S(1)}, bf16[4,512,128]{2,1,0:T(8,128)(2,1)S(1)}, u32[]{:S(2)}, u32[]{:S(2)}) collective-permute-start(bf16[4,512,128]{2,1,0:T(8,128)(2,1)S(1)} %get-tuple-element.21), channel_id=1, source_target_pairs={{0,4},{1,17},{2,6},{3,19},{4,0},{5,21},{6,2},{7,23},{8,12},{9,25},... | collective-permute-start | bytes 1572872 | tf_op jit(solution)/shard_map/ppermute | solution.py:56
  81.7 5.1 %collective-permute-start.14 = (bf16[512,128]{1,0:T(8,128)(2,1)S(1)}, bf16[512,128]{1,0:T(8,128)(2,1)S(1)}, u32[]{:S(2)}, u32[]{:S(2)}) collective-permute-start(bf16[512,128]{1,0:T(8,128)(2,1)S(1)} %get-tuple-element.22), channel_id=1, source_target_pairs={{0,8},{1,3},{2,10},{3,5},{4,12},{5,7},{6,14},{7,1},{8,16},{9,11},{... | collective-permute-start | bytes 393224 | tf_op jit(solution)/shard_map/ppermute | solution.py:56
  82.7 4.1 %collective-permute-start.15 = (bf16[512,128]{1,0:T(8,128)(2,1)S(1)}, bf16[512,128]{1,0:T(8,128)(2,1)S(1)}, u32[]{:S(2)}, u32[]{:S(2)}) collective-permute-start(bf16[512,128]{1,0:T(8,128)(2,1)S(1)} %get-tuple-element.23), channel_id=1, source_target_pairs={{0,24},{1,7},{2,26},{3,1},{4,28},{5,3},{6,30},{7,5},{8,0},{9,15},{... | collective-permute-start | bytes 393224 | tf_op jit(solution)/shard_map/ppermute | solution.py:56
  84.4 5.3 %collective-permute-start.16 = (bf16[512,128]{1,0:T(8,128)(2,1)S(1)}, bf16[512,128]{1,0:T(8,128)(2,1)S(1)}, u32[]{:S(2)}, u32[]{:S(2)}) collective-permute-start(bf16[512,128]{1,0:T(8,128)(2,1)S(1)} %get-tuple-element.24), channel_id=1, source_target_pairs={{0,16},{1,5},{2,18},{3,7},{4,20},{5,1},{6,22},{7,3},{8,24},{9,13},... | collective-permute-start | bytes 393224 | tf_op jit(solution)/shard_map/ppermute | solution.py:56
  89.8 23.5 %copy-start.17 = (s32[4,1,4]{2,1,0:T(1,128)S(1)}, s32[4,1,4]{2,1,0:T(1,128)}, u32[]{:S(2)}) copy-start(s32[4,1,4]{2,1,0:T(1,128)} %param.12) | copy-start | bytes 196
  89.8 50.5 %copy-start.21 = (s32[2,4,4]{2,1,0:T(4,128)S(1)}, s32[2,4,4]{2,1,0:T(4,128)}, u32[]{:S(2)}) copy-start(s32[2,4,4]{2,1,0:T(4,128)} %copy-done.20) | copy-start | bytes 388
  89.8 52.4 %copy-start.23 = (s32[2,4,4]{2,1,0:T(4,128)S(1)}, s32[2,4,4]{2,1,0:T(4,128)}, u32[]{:S(2)}) copy-start(s32[2,4,4]{2,1,0:T(4,128)} %copy-done.22) | copy-start | bytes 388
  91.4 18.8 %copy-start.19 = (bf16[512,128]{1,0:T(8,128)(2,1)}, bf16[512,128]{1,0:T(8,128)(2,1)S(1)}, u32[]{:S(2)}) copy-start(bf16[512,128]{1,0:T(8,128)(2,1)S(1)} %get-tuple-element.26) | copy-start | bytes 393220
  91.4 0.7 collective-permute-start.18
  92.1 5.4 %collective-permute-start.21 = (bf16[512,128]{1,0:T(8,128)(2,1)S(1)}, bf16[512,128]{1,0:T(8,128)(2,1)S(1)}, u32[]{:S(2)}, u32[]{:S(2)}) collective-permute-start(bf16[512,128]{1,0:T(8,128)(2,1)S(1)} %collective-permute-done.18.a), channel_id=1, source_target_pairs={{0,16},{1,5},{2,18},{3,7},{4,20},{5,1},{6,22},{7,3},{8,24},{9,13},... | collective-permute-start | bytes 393224 | tf_op jit(solution)/shard_map/ppermute | solution.py:56
  93.0 4.6 %collective-permute-start.20 = (bf16[512,128]{1,0:T(8,128)(2,1)S(1)}, bf16[512,128]{1,0:T(8,128)(2,1)S(1)}, u32[]{:S(2)}, u32[]{:S(2)}) collective-permute-start(bf16[512,128]{1,0:T(8,128)(2,1)S(1)} %collective-permute-done.18.a), channel_id=1, source_target_pairs={{0,24},{1,7},{2,26},{3,1},{4,28},{5,3},{6,30},{7,5},{8,0},{9,15},{... | collective-permute-start | bytes 393224 | tf_op jit(solution)/shard_map/ppermute | solution.py:56
  95.0 5.0 %collective-permute-start.19 = (bf16[512,128]{1,0:T(8,128)(2,1)S(1)}, bf16[512,128]{1,0:T(8,128)(2,1)S(1)}, u32[]{:S(2)}, u32[]{:S(2)}) collective-permute-start(bf16[512,128]{1,0:T(8,128)(2,1)S(1)} %collective-permute-done.18.a), channel_id=1, source_target_pairs={{0,8},{1,3},{2,10},{3,5},{4,12},{5,7},{6,14},{7,1},{8,16},{9,11},{... | collective-permute-start | bytes 393224 | tf_op jit(solution)/shard_map/ppermute | solution.py:56
  100.1 39.0 %collective-permute-start.24 = (bf16[4,512,128]{2,1,0:T(8,128)(2,1)S(1)}, bf16[4,512,128]{2,1,0:T(8,128)(2,1)S(1)}, u32[]{:S(2)}, u32[]{:S(2)}) collective-permute-start(bf16[4,512,128]{2,1,0:T(8,128)(2,1)S(1)} %stack4.3.refs_0_), channel_id=1, source_target_pairs={{0,4},{1,17},{2,6},{3,19},{4,0},{5,21},{6,2},{7,23},{8,12},{9,25},... | collective-permute-start | bytes 1572872 | tf_op jit(solution)/shard_map/ppermute | solution.py:56
  106.9 32.2 %collective-permute-start.23 = (bf16[4,512,128]{2,1,0:T(8,128)(2,1)S(1)}, bf16[4,512,128]{2,1,0:T(8,128)(2,1)S(1)}, u32[]{:S(2)}, u32[]{:S(2)}) collective-permute-start(bf16[4,512,128]{2,1,0:T(8,128)(2,1)S(1)} %stack4.3.refs_0_), channel_id=1, source_target_pairs={{0,6},{1,25},{2,0},{3,27},{4,2},{5,29},{6,4},{7,31},{8,14},{9,1},{... | collective-permute-start | bytes 1572872 | tf_op jit(solution)/shard_map/ppermute | solution.py:56
  110.1 29.5 %collective-permute-start.22 = (bf16[4,512,128]{2,1,0:T(8,128)(2,1)S(1)}, bf16[4,512,128]{2,1,0:T(8,128)(2,1)S(1)}, u32[]{:S(2)}, u32[]{:S(2)}) collective-permute-start(bf16[4,512,128]{2,1,0:T(8,128)(2,1)S(1)} %stack4.3.refs_0_), channel_id=1, source_target_pairs={{0,2},{1,9},{2,4},{3,11},{4,6},{5,13},{6,0},{7,15},{8,10},{9,17},{... | collective-permute-start | bytes 1572872 | tf_op jit(solution)/shard_map/ppermute | solution.py:56
  110.2 14.4 %collective-permute-start.31 = (bf16[1024,128]{1,0:T(8,128)(2,1)S(1)}, bf16[1024,128]{1,0:T(8,128)(2,1)S(1)}, u32[]{:S(2)}, u32[]{:S(2)}) collective-permute-start(bf16[1024,128]{1,0:T(8,128)(2,1)S(1)} %get-tuple-element.28.refs_8_), channel_id=1, source_target_pairs={{0,64},{32,96},{64,0},{96,32},{1,65},{33,97},{65,1},{97,33},{2,66}... | collective-permute-start | bytes 786440 | tf_op jit(solution)/shard_map/ppermute | solution.py:376
  111.9 15.0 %collective-permute-start.30 = (bf16[1024,128]{1,0:T(8,128)(2,1)S(1)}, bf16[1024,128]{1,0:T(8,128)(2,1)S(1)}, u32[]{:S(2)}, u32[]{:S(2)}) collective-permute-start(bf16[1024,128]{1,0:T(8,128)(2,1)S(1)} %get-tuple-element.28.refs_8_), channel_id=1, source_target_pairs={{0,96},{32,0},{64,32},{96,64},{1,97},{33,1},{65,33},{97,65},{2,98}... | collective-permute-start | bytes 786440 | tf_op jit(solution)/shard_map/ppermute | solution.py:376
  124.6 0.7 copy-start.8
  125.4 30.4 %collective-permute-start.17 = (bf16[512,128]{1,0:T(8,128)(2,1)}, bf16[512,128]{1,0:T(8,128)(2,1)S(1)}, u32[]{:S(2)}, u32[]{:S(2)}) collective-permute-start(bf16[512,128]{1,0:T(8,128)(2,1)} %copy-done.19), channel_id=1, source_target_pairs={{0,0},{1,1},{2,2},{3,3},{4,4},{5,5},{6,6},{7,7},{8,8},{9,9},{10,10... | collective-permute-start | bytes 393224 | tf_op jit(solution)/shard_map/ppermute | solution.py:388
  126.9 0.7 copy-start.10
  127.6 38.8 %collective-permute-start.25 = (bf16[4,512,128]{2,1,0:T(8,128)(2,1)S(1)}, bf16[4,512,128]{2,1,0:T(8,128)(2,1)S(1)}, u32[]{:S(2)}, u32[]{:S(2)}) collective-permute-start(bf16[4,512,128]{2,1,0:T(8,128)(2,1)S(1)} %stack4.3.refs_0_), channel_id=1, source_target_pairs={{0,1},{1,0},{2,3},{3,2},{4,5},{5,4},{6,7},{7,6},{8,9},{9,8},{10,11... | collective-permute-start | bytes 1572872 | tf_op jit(solution)/shard_map/ppermute | solution.py:56
  139.1 27.4 %collective-permute-start.28 = (bf16[4,512,128]{2,1,0:T(8,128)(2,1)S(1)}, bf16[4,512,128]{2,1,0:T(8,128)(2,1)S(1)}, u32[]{:S(2)}, u32[]{:S(2)}) collective-permute-start(bf16[4,512,128]{2,1,0:T(8,128)(2,1)S(1)} %collective-permute-done.24.refs_3_), channel_id=1, source_target_pairs={{0,1},{1,0},{2,3},{3,2},{4,5},{5,4},{6,7},{7,6},{8,9},{9,8},{10,11... | collective-permute-start | bytes 1572872 | tf_op jit(solution)/shard_map/ppermute | solution.py:56
  139.1 27.4 %collective-permute-start.27 = (bf16[4,512,128]{2,1,0:T(8,128)(2,1)S(1)}, bf16[4,512,128]{2,1,0:T(8,128)(2,1)}, u32[]{:S(2)}, u32[]{:S(2)}) collective-permute-start(bf16[4,512,128]{2,1,0:T(8,128)(2,1)S(1)} %collective-permute-done.23.refs_2_), channel_id=1, source_target_pairs={{0,1},{1,0},{2,3},{3,2},{4,5},{5,4},{6,7},{7,6},{8,9},{9,8},{10,11... | collective-permute-start | bytes 1572872 | tf_op jit(solution)/shard_map/ppermute | solution.py:56
  139.6 26.9 %collective-permute-start.26 = (bf16[4,512,128]{2,1,0:T(8,128)(2,1)S(1)}, bf16[4,512,128]{2,1,0:T(8,128)(2,1)}, u32[]{:S(2)}, u32[]{:S(2)}) collective-permute-start(bf16[4,512,128]{2,1,0:T(8,128)(2,1)S(1)} %collective-permute-done.22.refs_1_), channel_id=1, source_target_pairs={{0,1},{1,0},{2,3},{3,2},{4,5},{5,4},{6,7},{7,6},{8,9},{9,8},{10,11... | collective-permute-start | bytes 1572872 | tf_op jit(solution)/shard_map/ppermute | solution.py:56
  147.7 17.0 %all-to-all-start = ((bf16[32,4,4,256]{3,2,1,0:T(4,128)(2,1)}), bf16[32,4,4,256]{3,2,1,0:T(4,128)(2,1)}, u32[]{:S(2)}, u32[]{:S(2)}) async-start(bf16[32,4,4,256]{3,2,1,0:T(4,128)(2,1)} %copy-done.12), calls=%async_computation | async-start | bytes 524288 | tf_op jit(solution)/shard_map/all_to_all | solution.py:373
  155.8 10.7 %collective-permute-start.29 = (bf16[1024,128]{1,0:T(8,128)(2,1)S(1)}, bf16[1024,128]{1,0:T(8,128)(2,1)}, u32[]{:S(2)}, u32[]{:S(2)}) collective-permute-start(bf16[1024,128]{1,0:T(8,128)(2,1)S(1)} %get-tuple-element.28.refs_8_), channel_id=1, source_target_pairs={{0,32},{32,64},{64,96},{96,0},{1,33},{33,65},{65,97},{97,1},{2,34}... | collective-permute-start | bytes 786440 | tf_op jit(solution)/shard_map/ppermute | solution.py:376
  166.5 1.0 copy-start.9
  167.4 0.9 copy-start.11

commit v2 on v1

v2 whole, which is shorter than its diff:
```python
import functools

import jax
import jax.numpy as jnp
import numpy as np
from jax import lax
from jax.experimental import pallas as pl
from jax.experimental.pallas import tpu as pltpu
from jax.sharding import PartitionSpec as P

TILE_ROWS = 128
LAT_TILE = 64
CAP = 4
SIDE = 4
ROWS = 512
WIDTH = 4096
PIECE = 128
SHIFTS = (0, 2, 1, 3)
PARTS = 1
HALF = ROWS // PARTS
BF = jnp.bfloat16
F32 = jnp.float32


def lat_of(y, x, c):
    return (y % SIDE) * 8 + (x % SIDE) * 2 + c


def chips():
    return [(y, x, c) for y in range(SIDE) for x in range(SIDE) for c in range(2)]


def short_leg(d):
    return [
        (lat_of(y, x, c), lat_of(y + d, x, c) if c == 0 else lat_of(y, x + d, c))
        for y, x, c in chips()
    ]


def long_leg(d):
    return [
        (lat_of(y, x, c), lat_of(y, x + d, c) if c == 0 else lat_of(y + d, x, c))
        for y, x, c in chips()
    ]


CORE = [(lat_of(y, x, c), lat_of(y, x, 1 - c)) for y, x, c in chips()]


def plane_leg(d):
    return [
        (z * 32 + a, (z + a // 8) % SIDE * 32 + b) for z in range(SIDE) for a, b in short_leg(d)
    ]


TO_HOME = [
    (z * 32 + lat_of(y, x, c), z * 32 + lat_of(y + z, x, c))
    for z in range(SIDE)
    for y, x, c in chips()
]


def place_table():
    rows = []
    for z in range(SIDE):
        for y, x, c in chips():
            from_lat, at = [], []
            for core in (c, 1 - c):
                for far in SHIFTS:
                    for near in SHIFTS:
                        fy = (y - (near if core == 0 else far)) % SIDE
                        fx = (x - (far if core == 0 else near)) % SIDE
                        from_lat.append(lat_of(fy, fx, core))
                        at += [fy, fx * 2 + core]
            slot = SHIFTS.index((-z) % SIDE)
            sums = []
            for far in SHIFTS:
                for near in SHIFTS:
                    ty = y + (near if c == 0 else far)
                    tx = x + (far if c == 0 else near)
                    sums.append((ty + z) % SIDE * SIDE + tx % SIDE)
            sums.append(lat_of(y + z, x, c))
            rows.append(from_lat + [slot if c == 0 else 4 * slot, c] + at + sums)
    return np.array(rows, np.int32)


def pick_matrix():
    row = np.arange(CAP * TILE_ROWS)
    j, l, c = row // TILE_ROWS, row % TILE_ROWS // CAP, row % CAP
    pick = np.zeros((row.size, row.size), np.float32)
    pick[row, c * TILE_ROWS + 4 * l + j] = 1.0
    return pick


def send(value, pairs):
    return lax.ppermute(value, "lat", pairs)


ANY = pl.BlockSpec(memory_space=pltpu.HBM)
LARGE = pltpu.CompilerParams(vmem_limit_bytes=40 << 20)
SMALL = pltpu.CompilerParams(vmem_limit_bytes=16 << 20)
PLACES = (34, 98)


def stack_kernel(*refs):
    for k in range(4):
        refs[-1][k] = refs[k][...]


def stack4(parts, after):
    shape = parts[0].shape
    whole = pl.BlockSpec(memory_space=pltpu.VMEM)
    return pl.pallas_call(
        stack_kernel,
        in_specs=[whole] * 4 + [ANY] * len(after),
        out_specs=whole,
        out_shape=jax.ShapeDtypeStruct((4,) + shape, BF),
        compiler_params=SMALL,
        name="stack4",
    )(*parts, *after)


def short_gather(piece):
    return [piece] + [send(piece, short_leg(d)) for d in SHIFTS[1:]]


def long_gather(line):
    mine = [line] + [send(line, long_leg(d)) for d in SHIFTS[1:]]
    return mine + [send(v, CORE) for v in mine]


def encode_kernel(first, ids, counts, where, *refs):
    pieces = refs[:8]
    tiles = refs[8:12]
    enc_bias, dec_bias = refs[12:14]
    codes_out, mine, other, resid, centered = refs[-5:]
    b = first + pl.program_id(0)
    for k in range(8):
        for e in range(4):
            slot = k * 4 + e
            off = pl.multiple_of(where[slot] * PIECE, PIECE)
            raw = pieces[k][e]
            centered[:, pl.ds(off, PIECE)] = (
                raw.astype(F32) - dec_bias[:, pl.ds(off, PIECE)]
            ).astype(BF)
            if k == 0 or (k < 4 and e == 0):

                @pl.when(where[32] == slot)
                def _():
                    resid[...] = raw

    step = 512
    preact = jnp.zeros((TILE_ROWS, CAP * LAT_TILE), F32)
    for k in range(0, WIDTH, step):
        block = jnp.concatenate([t[:, k : k + step] for t in tiles], axis=0)
        preact += lax.dot_general(
            centered[:, k : k + step],
            block,
            (((1,), (1,)), ((), ())),
            preferred_element_type=F32,
        )
    bias = jnp.concatenate(
        [enc_bias[pl.ds(ids[b, s], 1), :] for s in range(CAP)], axis=1
    )
    slot_of = lax.broadcasted_iota(jnp.int32, (TILE_ROWS, CAP * LAT_TILE), 1) // LAT_TILE
    live = slot_of < counts[b]
    values = jnp.where(live, jnp.maximum(preact + bias, 0.0), 0.0)
    codes = values.astype(BF)
    codes_out[...] = codes

    core0 = where[33] == 0
    for n in range(0, WIDTH, step):
        block = jnp.concatenate([t[:, n : n + step] for t in tiles], axis=0)
        part = jnp.dot(codes, block, preferred_element_type=F32)
        for p in range(0, step, 2 * PIECE):
            first = part[:, p : p + PIECE]
            second = part[:, p + PIECE : p + 2 * PIECE]
            at = (n + p) // (2 * PIECE)
            mine[at] = jnp.where(core0, first, second).astype(BF)
            other[at] = jnp.where(core0, second, first).astype(BF)


def encode(first, ids, counts, places, pieces, dictionary, enc_bias, dec_bias, after):
    rows = pieces[0].shape[1]
    piece_spec = pl.BlockSpec((4, TILE_ROWS, PIECE), lambda b, *_: (0, b, 0))
    tile_specs = [
        pl.BlockSpec((LAT_TILE, WIDTH), lambda b, i, n, w, s=s: (i[first + b, s], 0))
        for s in range(CAP)
    ]
    whole = lambda b, *_: (0, 0)
    return pl.pallas_call(
        functools.partial(encode_kernel, first),
        grid_spec=pltpu.PrefetchScalarGridSpec(
            num_scalar_prefetch=3,
            grid=(rows // TILE_ROWS,),
            in_specs=[piece_spec] * 8
            + tile_specs
            + [pl.BlockSpec((32, LAT_TILE), whole), pl.BlockSpec((1, WIDTH), whole)]
            + [ANY] * len(after),
            out_specs=[
                pl.BlockSpec((TILE_ROWS, CAP * LAT_TILE), lambda b, *_: (b, 0)),
                pl.BlockSpec((16, TILE_ROWS, PIECE), lambda b, *_: (0, b, 0)),
                pl.BlockSpec((16, TILE_ROWS, PIECE), lambda b, *_: (0, b, 0)),
                pl.BlockSpec((TILE_ROWS, PIECE), lambda b, *_: (b, 0)),
            ],
            scratch_shapes=[pltpu.VMEM((TILE_ROWS, WIDTH), BF)],
        ),
        out_shape=[
            jax.ShapeDtypeStruct((rows, CAP * LAT_TILE), BF),
            jax.ShapeDtypeStruct((16, rows, PIECE), BF),
            jax.ShapeDtypeStruct((16, rows, PIECE), BF),
            jax.ShapeDtypeStruct((rows, PIECE), BF),
        ],
        compiler_params=LARGE,
        cost_estimate=pl.CostEstimate(
            flops=rows << 23, bytes_accessed=rows << 15, transcendentals=0
        ),
        name="encode",
    )(ids, counts, places, *pieces, *([dictionary] * CAP), enc_bias, dec_bias, *after)


def turn_kernel(*refs):
    codes_t = refs[-1]
    ids = refs[PARTS]
    size = CAP * LAT_TILE
    for b in range(4):
        at = b * TILE_ROWS
        codes = refs[at // HALF][at % HALF : at % HALF + TILE_ROWS, :]
        codes_t[b * size : (b + 1) * size, :] = codes.astype(F32).T.astype(BF)
    codes_t[4 * size :, :] = ids[...]


def turn(codes, ids, after):
    id_rows = jnp.zeros((16, TILE_ROWS), BF).at[0, :16].set(ids.reshape(16).astype(BF))
    whole = pl.BlockSpec(memory_space=pltpu.VMEM)
    return pl.pallas_call(
        turn_kernel,
        in_specs=[whole] * (PARTS + 1) + [ANY] * len(after),
        out_specs=whole,
        out_shape=jax.ShapeDtypeStruct((4 * CAP * LAT_TILE + 16, TILE_ROWS), BF),
        compiler_params=SMALL,
        name="turn",
    )(*codes, id_rows, *after)


def pack_kernel(*refs):
    pick, tile_send = refs[PARTS], refs[-1]
    for b in range(4):
        at = b * TILE_ROWS
        codes = refs[at // HALF][at % HALF : at % HALF + TILE_ROWS, :]
        stacked = jnp.concatenate(
            [codes[:, s * LAT_TILE : (s + 1) * LAT_TILE] for s in range(CAP)], axis=0
        )
        slabs = jnp.dot(pick[...], stacked, preferred_element_type=F32)
        packed = jnp.concatenate(
            [slabs[s * TILE_ROWS : (s + 1) * TILE_ROWS] for s in range(4)], axis=1
        )
        tile_send[:, b] = packed.reshape(32, CAP, 4 * LAT_TILE).astype(BF)


def pack(codes, after):
    whole = pl.BlockSpec(memory_space=pltpu.VMEM)
    return pl.pallas_call(
        pack_kernel,
        in_specs=[whole] * (PARTS + 1) + [ANY] * len(after),
        out_specs=whole,
        out_shape=jax.ShapeDtypeStruct((32, 4, CAP, 4 * LAT_TILE), BF),
        compiler_params=SMALL,
        name="pack",
    )(*codes, jnp.asarray(pick_matrix(), BF), *after)


def first_sum_kernel(table, *refs):
    for k in range(3):
        a, b, out = refs[k], refs[3 + k], refs[k - 3]
        out[...] = (a[...].astype(F32) + b[...].astype(F32)).astype(BF)


def first_sum(places, mine, got, after):
    rows = mine.shape[1]
    specs = [
        pl.BlockSpec((1, rows, PIECE), lambda e, p, k=k: (p[PLACES[1] + 4 * k + e], 0, 0))
        for k in range(1, 4)
    ]
    return pl.pallas_call(
        first_sum_kernel,
        grid_spec=pltpu.PrefetchScalarGridSpec(
            num_scalar_prefetch=1,
            grid=(4,),
            in_specs=specs + specs + [ANY] * len(after),
            out_specs=[pl.BlockSpec((1, rows, PIECE), lambda e, p: (e, 0, 0))] * 3,
        ),
        out_shape=[jax.ShapeDtypeStruct((4, rows, PIECE), BF)] * 3,
        compiler_params=LARGE,
        name="first_sum",
    )(places, *([mine] * 3), *([got] * 3), *after)


def second_sum_kernel(table, *refs):
    far = refs[6:9]
    outs = refs[-3:]
    for k in range(3):
        total = refs[k][0].astype(F32) + refs[3 + k][0].astype(F32)
        for ref in far:
            total += ref[k + 1].astype(F32)
        outs[k][...] = total.astype(BF)


def second_sum(places, mine, got, far, after):
    rows = mine.shape[1]
    half = rows // 2
    specs = [
        pl.BlockSpec((1, half, PIECE), lambda i, p, e=e: (p[PLACES[1] + e], i, 0))
        for e in range(1, 4)
    ]
    return pl.pallas_call(
        second_sum_kernel,
        grid_spec=pltpu.PrefetchScalarGridSpec(
            num_scalar_prefetch=1,
            grid=(2,),
            in_specs=specs
            + specs
            + [pl.BlockSpec((4, half, PIECE), lambda i, p: (0, i, 0))] * 3
            + [ANY] * len(after),
            out_specs=[pl.BlockSpec((half, PIECE), lambda i, p: (i, 0))] * 3,
        ),
        out_shape=[jax.ShapeDtypeStruct((rows, PIECE), BF)] * 3,
        compiler_params=LARGE,
        name="second_sum",
    )(places, *([mine] * 3), *([got] * 3), *far, *after)


def error_kernel(table, *refs):
    dec_bias, resid = refs[8:10]
    out, error = refs[-2:]
    total = refs[0][0].astype(F32) + refs[1][0].astype(F32)
    for ref in refs[2:5]:
        total += ref[0].astype(F32)
    for ref in refs[5:8]:
        total += ref[...].astype(F32)
    total += dec_bias[...]
    out[...] = total.astype(BF)
    error[...] = (total - resid[...].astype(F32)).astype(BF)


def error_of(places, mine, got, far, near, dec_bias, resid, after):
    rows = mine.shape[1]
    piece = pl.BlockSpec((rows, PIECE), lambda i, p: (0, 0))
    own = pl.BlockSpec((1, rows, PIECE), lambda i, p: (p[PLACES[1]], 0, 0))
    return pl.pallas_call(
        error_kernel,
        grid_spec=pltpu.PrefetchScalarGridSpec(
            num_scalar_prefetch=1,
            grid=(1,),
            in_specs=[own, own]
            + [pl.BlockSpec((1, rows, PIECE), lambda i, p: (0, 0, 0))] * 3
            + [piece] * 3
            + [pl.BlockSpec((1, PIECE), lambda i, p: (0, p[PLACES[1] + 16])), piece]
            + [ANY] * len(after),
            out_specs=[piece, piece],
        ),
        out_shape=[jax.ShapeDtypeStruct((rows, PIECE), BF)] * 2,
        compiler_params=LARGE,
        name="error",
    )(places, mine, got, *far, *near, dec_bias, resid, *after)


def grad_kernel(ids, places, *refs):
    pieces, codes = refs[: 8 * PARTS], refs[8 * PARTS : 8 * PARTS + 4]
    out, error = refs[-2:]
    n = pl.program_id(0)

    @pl.when(n == 0)
    def _():
        for h in range(PARTS):
            for k in range(8):
                for e in range(4):
                    at = PLACES[0] + 2 * (k * 4 + e)
                    row = pl.multiple_of(places[at] * ROWS + h * HALF, HALF)
                    col = places[at + 1]
                    lane = pl.multiple_of(col % 2 * PIECE, PIECE)
                    error[col // 2, pl.ds(row, HALF), pl.ds(lane, PIECE)] = pieces[8 * h + k][e]

    out[...] = jnp.zeros_like(out)
    for k, shift in enumerate(SHIFTS):
        for b in range(4):
            row = shift * ROWS + b * TILE_ROWS
            part = jnp.dot(
                codes[k][b * 256 : (b + 1) * 256, :],
                error[n, row : row + TILE_ROWS, :],
                preferred_element_type=F32,
            )
            for s in range(CAP):
                at = pl.multiple_of(ids[k * 16 + b * 4 + s] * LAT_TILE, LAT_TILE)
                out[pl.ds(at, LAT_TILE), :] += part[s * LAT_TILE : (s + 1) * LAT_TILE, :]


def grad(ids, places, pieces, codes, after):
    width = 2 * PIECE
    return pl.pallas_call(
        grad_kernel,
        grid_spec=pltpu.PrefetchScalarGridSpec(
            num_scalar_prefetch=2,
            grid=(4,),
            in_specs=[pl.BlockSpec((4, HALF, PIECE), lambda n, *_: (0, 0, 0))] * (8 * PARTS)
            + [pl.BlockSpec((4 * CAP * LAT_TILE + 16, TILE_ROWS), lambda n, *_: (0, 0))] * 4
            + [ANY] * len(after),
            out_specs=pl.BlockSpec((2048, width), lambda n, *_: (0, n)),
            scratch_shapes=[pltpu.VMEM((4, 4 * ROWS, width), BF)],
        ),
        out_shape=jax.ShapeDtypeStruct((2048, 1024), F32),
        compiler_params=LARGE,
        cost_estimate=pl.CostEstimate(
            flops=10**9, bytes_accessed=14 << 20, transcendentals=0
        ),
        name="grad",
    )(ids, places, *pieces, *codes, *after)


def body(residuals, dictionary, enc_bias, dec_bias, tile_ids, tile_counts):
    device = lax.axis_index("tok") * 32 + lax.axis_index("lat")
    places = lax.dynamic_index_in_dim(jnp.asarray(place_table()), device, 0, False)
    ids = tile_ids[:, 0, :]
    counts = tile_counts[:, 0]
    enc_rows = enc_bias.reshape(32, LAT_TILE)
    dec_row = dec_bias.reshape(1, WIDTH)
    halves = range(PARTS)

    near = [short_gather(residuals[h * HALF : (h + 1) * HALF]) for h in halves]
    lines = []
    for h in halves:
        lines.append(stack4(near[h], [enc_rows, places] if h == 0 else [lines[-1]]))
    pieces = [long_gather(lines[h]) for h in halves]

    codes, mine, got, resid, sums = [], [], [], [], []
    for h in halves:
        c, m, o, r = encode(
            h * HALF // TILE_ROWS, ids, counts, places, pieces[h], dictionary,
            enc_rows, dec_row, sums[-1][:1] if sums else [],
        )
        codes.append(c), mine.append(m), resid.append(r)
        got.append(send(o, CORE))
        sums.append(first_sum(places, mine[h], got[h], []))
    far = [[send(v, long_leg(d)) for v, d in zip(sums[h], SHIFTS[1:])] for h in halves]

    codes_t = turn(codes, ids, [])
    all_codes = [codes_t] + [
        lax.ppermute(codes_t, "tok", [(z, (z + s) % SIDE) for z in range(SIDE)])
        for s in SHIFTS[1:]
    ]
    all_ids = jnp.concatenate([v[4 * CAP * LAT_TILE, :16] for v in all_codes]).astype(jnp.int32)
    tile_send = pack(codes, [sums[-1][0], codes_t])
    tile_got = lax.all_to_all(tile_send, "lat", split_axis=0, concat_axis=0, tiled=True)
    tile_codes = tile_got.transpose(1, 0, 2, 3)

    recon, error = [], []
    parts = []
    last = tile_send
    for h in halves:
        parts.append(second_sum(places, mine[h], got[h], far[h], [last]))
        last = parts[h][0]
    for h in halves:
        back = [send(v, short_leg(d)) for v, d in zip(parts[h], SHIFTS[1:])]
        r, e = error_of(
            places, mine[h], got[h], far[h], back, dec_row, resid[h],
            [last] if h else [last, all_ids, tile_got],
        )
        last = r
        recon.append(r)
        error.append(e)
    whole = recon[0] if PARTS == 1 else jnp.concatenate(recon)
    reconstruction = lax.ppermute(whole, ("tok", "lat"), TO_HOME)
    last = reconstruction
    error_lines = []
    for h in halves:
        legs = [lax.ppermute(error[h], ("tok", "lat"), plane_leg(d)) for d in SHIFTS]
        error_lines.append(stack4(legs, [last]))
        last = error_lines[h]
    errors = [long_gather(error_lines[h]) for h in halves]
    decoder_grad = grad(all_ids, places, sum(errors, []), all_codes, [])
    return (tile_codes, reconstruction, decoder_grad)


def solution(mesh):
    placed = (
        P("tok", "lat"),
        P("lat", None),
        P("lat"),
        P(),
        P("tok", "lat", None),
        P("tok", "lat"),
    )
    return jax.shard_map(
        body,
        mesh=mesh,
        in_specs=placed,
        out_specs=(P("tok", None, None, "lat"), P("tok", "lat"), P("lat", "tok")),
        check_vma=False,
    )
```

time: 178 us -> 136 us (0.76)
  local copies, waits for them, and re-layouts: 28.1 us -> 9.75 us
  waiting for transfers between devices: 38.2 us -> 23.7 us
  blocking collectives: 11.3 us -> 0 us
  starting transfers between devices: 66 us -> 70.5 us
  other arithmetic: 3.14 us -> 0.1 us
  Pallas kernels: 27.7 us -> 29.7 us
    ppermute x27 -> x24, waiting for transfers between devices: 33.9 us -> 18.7 us  [send(): return lax.ppermute(value, 'lat', pairs)]
    unnamed x56 -> x24, local copies, waits for them, and re-layouts: 20.9 us -> 5.87 us
    all_gather x1 -> x0, blocking collectives: 11.3 us -> none  [body(): all_ids = lax.all_gather(ids, 'tok', axis=0, tiled=False)]
    ppermute x2 -> x5, waiting for transfers between devices: 0.01 us -> 4.01 us  [the longest x4 4 us: body(): lax.ppermute(error[h], ('tok', 'lat'), plane_leg(d))]
    all_to_all x1, waiting for transfers between devices: 4.31 us -> 1.05 us  [body(): lax.all_to_all(tile_send, 'lat', split_axis=0, concat_axis=0, tiled=True)]
    squeeze x0 -> x5, local copies, waits for them, and re-layouts: none -> 3.03 us  [the longest x4 2.33 us: body(): v[4 * CAP * LAT_TILE, :16]]
    sub x4 -> x0, local copies, waits for them, and re-layouts: 2.04 us -> none  [the longest x2 1.39 us: body(): from_x = (x - jnp.where(from_core == 0, far, near)) % SIDE]
    ppermute x2 -> x5, starting transfers between devices: 2.22 us -> 4.25 us  [the longest x4 3.58 us: body(): lax.ppermute(error[h], ('tok', 'lat'), plane_leg(d))]
  transfers between devices with their start and end apart: 33 -> 33, of which waited for: 14 -> 14; matrix products, arithmetic and copies ran while one was open for 9% -> 4% of each run, Pallas kernels for 0% -> 6%
where the time goes in v2:
time: 136 us; the launch traced here: 135 us
  starting transfers between devices  70.5 us (52%)
  Pallas kernels  29.7 us (22%)
  waiting for transfers between devices  23.7 us (17%)
  local copies, waits for them, and re-layouts  9.75 us (7%)
    ppermute x24, starting transfers between devices, send(): return lax.ppermute(value, 'lat', pairs)  51.4 us
    ppermute x24, waiting for transfers between devices, send(): return lax.ppermute(value, 'lat', pairs)  18.7 us
    pallas_call x1, Pallas kernels, encode(): pl.pallas_call(functools.partial(encode_kernel, first), grid_spec=pltpu.P...  11.7 us
    ppermute x3, starting transfers between devices, body(): lax.ppermute(codes_t, 'tok', [(z, (z + s) % SIDE) for z in range(SIDE)])  7.48 us
    pallas_call x1, Pallas kernels, grad(): pl.pallas_call(grad_kernel, grid_spec=pltpu.PrefetchScalarGridSpec(num_sc...  7.43 us
    all_to_all x1, starting transfers between devices, body(): lax.all_to_all(tile_send, 'lat', split_axis=0, concat_axis=0, tiled=True)  7.37 us
    unnamed x24, local copies, waits for them, and re-layouts  5.87 us
    pallas_call x1, Pallas kernels, first_sum(): pl.pallas_call(first_sum_kernel, grid_spec=pltpu.PrefetchScalarGridSpec(n...  4.18 us
  transfers between devices with their start and end apart: 33, of which 14 were waited for; matrix products, arithmetic and copies ran while one was open for 4% of the time, Pallas kernels for 6%

profile of v2, /device:TPU:1, one launch (start us, length us, event | category | flops | bytes accessed | tf_op | source)
XLA Modules:
  0.0 134.6 jit_solution(14979982953579324012)
XLA Ops:
  0.6 2.1 %collective-permute-start.1 = (bf16[512,128]{1,0:T(8,128)(2,1)}, bf16[512,128]{1,0:T(8,128)(2,1)S(1)}, u32[]{:S(2)}, u32[]{:S(2)}) collective-permute-start(bf16[512,128]{1,0:T(8,128)(2,1)} %refs_0_.1), channel_id=1, source_target_pairs={{0,8},{1,3},{2,10},{3,5},{4,12},{5,7},{6,14},{7,1},{8,16},{9,11},{... | collective-permute-start | bytes 393224 | tf_op jit(solution)/shard_map/ppermute | solution.py:96
  2.7 2.5 %collective-permute-start = (bf16[512,128]{1,0:T(8,128)(2,1)}, bf16[512,128]{1,0:T(8,128)(2,1)S(1)}, u32[]{:S(2)}, u32[]{:S(2)}) collective-permute-start(bf16[512,128]{1,0:T(8,128)(2,1)} %refs_0_.1), channel_id=1, source_target_pairs={{0,16},{1,5},{2,18},{3,7},{4,20},{5,1},{6,22},{7,3},{8,24},{9,13},... | collective-permute-start | bytes 393224 | tf_op jit(solution)/shard_map/ppermute | solution.py:96
  5.2 1.2 collective-permute-start.2
  6.3 0.8 reshape.48.refs_4_.refs_12_
  7.1 0.7 dynamic-slice_bitcast_fusion.refs_5_.where.table.places
  7.8 1.6 %collective-permute-done.refs_1_ = bf16[512,128]{1,0:T(8,128)(2,1)S(1)} collective-permute-done((bf16[512,128]{1,0:T(8,128)(2,1)}, bf16[512,128]{1,0:T(8,128)(2,1)S(1)}, u32[]{:S(2)}, u32[]{:S(2)}) %collective-permute-start) | collective-permute-done | bytes 131104 | tf_op jit(solution)/shard_map/ppermute | solution.py:96
  9.5 0.9 copy-done.3
  10.5 2.5 %collective-permute-start.5 = (bf16[4,512,128]{2,1,0:T(8,128)(2,1)S(1)}, bf16[4,512,128]{2,1,0:T(8,128)(2,1)S(1)}, u32[]{:S(2)}, u32[]{:S(2)}) collective-permute-start(bf16[4,512,128]{2,1,0:T(8,128)(2,1)S(1)} %stack4.2.refs_0_), channel_id=1, source_target_pairs={{0,6},{1,25},{2,0},{3,27},{4,2},{5,29},{6,4},{7,31},{8,14},{9,1},{... | collective-permute-start | bytes 1572872 | tf_op jit(solution)/shard_map/ppermute | solution.py:96
  13.0 1.9 %collective-permute-start.3 = (bf16[4,512,128]{2,1,0:T(8,128)(2,1)S(1)}, bf16[4,512,128]{2,1,0:T(8,128)(2,1)S(1)}, u32[]{:S(2)}, u32[]{:S(2)}) collective-permute-start(bf16[4,512,128]{2,1,0:T(8,128)(2,1)S(1)} %stack4.2.refs_0_), channel_id=1, source_target_pairs={{0,4},{1,17},{2,6},{3,19},{4,0},{5,21},{6,2},{7,23},{8,12},{9,25},... | collective-permute-start | bytes 1572872 | tf_op jit(solution)/shard_map/ppermute | solution.py:96
  14.9 3.0 %collective-permute-start.6 = (bf16[4,512,128]{2,1,0:T(8,128)(2,1)S(1)}, bf16[4,512,128]{2,1,0:T(8,128)(2,1)S(1)}, u32[]{:S(2)}, u32[]{:S(2)}) collective-permute-start(bf16[4,512,128]{2,1,0:T(8,128)(2,1)S(1)} %stack4.2.refs_0_), channel_id=1, source_target_pairs={{0,1},{1,0},{2,3},{3,2},{4,5},{5,4},{6,7},{7,6},{8,9},{9,8},{10,11... | collective-permute-start | bytes 1572872 | tf_op jit(solution)/shard_map/ppermute | solution.py:96
  17.9 6.8 %collective-permute-done.5.refs_3_ = bf16[4,512,128]{2,1,0:T(8,128)(2,1)S(1)} collective-permute-done((bf16[4,512,128]{2,1,0:T(8,128)(2,1)S(1)}, bf16[4,512,128]{2,1,0:T(8,128)(2,1)S(1)}, u32[]{:S(2)}, u32[]{:S(2)}) %collective-permute-start.5) | collective-permute-done | bytes 524320 | tf_op jit(solution)/shard_map/ppermute | solution.py:96
  24.7 3.3 %collective-permute-start.9 = (bf16[4,512,128]{2,1,0:T(8,128)(2,1)S(1)}, bf16[4,512,128]{2,1,0:T(8,128)(2,1)S(1)}, u32[]{:S(2)}, u32[]{:S(2)}) collective-permute-start(bf16[4,512,128]{2,1,0:T(8,128)(2,1)S(1)} %collective-permute-done.5.refs_3_), channel_id=1, source_target_pairs={{0,1},{1,0},{2,3},{3,2},{4,5},{5,4},{6,7},{7,6},{8,9},{9,8},{10,11... | collective-permute-start | bytes 1572872 | tf_op jit(solution)/shard_map/ppermute | solution.py:96
  28.0 0.1 collective-permute-done.4.refs_2_
  28.1 3.5 %collective-permute-start.8 = (bf16[4,512,128]{2,1,0:T(8,128)(2,1)S(1)}, bf16[4,512,128]{2,1,0:T(8,128)(2,1)S(1)}, u32[]{:S(2)}, u32[]{:S(2)}) collective-permute-start(bf16[4,512,128]{2,1,0:T(8,128)(2,1)S(1)} %collective-permute-done.4.refs_2_), channel_id=1, source_target_pairs={{0,1},{1,0},{2,3},{3,2},{4,5},{5,4},{6,7},{7,6},{8,9},{9,8},{10,11... | collective-permute-start | bytes 1572872 | tf_op jit(solution)/shard_map/ppermute | solution.py:96
  31.7 1.5 %collective-permute-done.8.refs_6_ = bf16[4,512,128]{2,1,0:T(8,128)(2,1)S(1)} collective-permute-done((bf16[4,512,128]{2,1,0:T(8,128)(2,1)S(1)}, bf16[4,512,128]{2,1,0:T(8,128)(2,1)S(1)}, u32[]{:S(2)}, u32[]{:S(2)}) %collective-permute-start.8) | collective-permute-done | bytes 524320 | tf_op jit(solution)/shard_map/ppermute | solution.py:96
  33.2 0.7 collective-permute-done.7.refs_5_
  33.9 0.7 copy-done.4
  34.6 0.7 copy-done.6
  35.3 0.7 copy-done.7
  36.0 11.7 %encode.1 = (bf16[512,256]{1,0:T(8,128)(2,1)S(1)}, bf16[16,512,128]{2,1,0:T(8,128)(2,1)S(1)}, bf16[16,512,128]{2,1,0:T(8,128)(2,1)}, bf16[512,128]{1,0:T(8,128)(2,1)S(1)}) custom-call(s32[4,4]{1,0:T(4,128)S(1)} %bitcast.17, s32[4]{0:T(128)S(1)} %bitcast.18, s32[115]{0:T(128)S(1)} %dynamic-slice_bitcast_fusion.refs_5_.where.table.places, ...), custom_call_target="tpu_custom_call" | custom-call | flops 4294967296 | bytes 16777216 | tf_op jit(solution)/shard_map/encode/pallas_call | solution.py:191
  47.8 0.1 convert_element_type.15
  47.9 0.1 turn.1.refs_3_.refs_8_
  48.0 3.9 %collective-permute-start.19 = (bf16[1040,128]{1,0:T(8,128)(2,1)S(1)}, bf16[1040,128]{1,0:T(8,128)(2,1)S(1)}, u32[]{:S(2)}, u32[]{:S(2)}) collective-permute-start(bf16[1040,128]{1,0:T(8,128)(2,1)S(1)} %turn.1.refs_3_.refs_8_), channel_id=1, source_target_pairs={{0,96},{32,0},{64,32},{96,64},{1,97},{33,1},{65,33},{97,65},{2,98}... | collective-permute-start | bytes 798728 | tf_op jit(solution)/shard_map/ppermute | solution.py:448
  51.9 0.3 collective-permute-done.10.refs_3_.refs_4_.refs_5_.refs_1_
  52.2 4.2 %first_sum.1 = (bf16[4,512,128]{2,1,0:T(8,128)(2,1)}, bf16[4,512,128]{2,1,0:T(8,128)(2,1)}, bf16[4,512,128]{2,1,0:T(8,128)(2,1)}) custom-call(s32[115]{0:T(128)S(1)} %dynamic-slice_bitcast_fusion.refs_5_.where.table.places, bf16[16,512,128]{2,1,0:T(8,128)(2,1)S(1)} %get-tuple-element.28.refs_0_.refs_1_.refs_2_, ...), custom_call_target="tpu_custom_call" | custom-call | tf_op jit(solution)/shard_map/first_sum/pallas_call | solution.py:285
  56.4 0.4 collective-permute-start.12
  56.8 2.3 %collective-permute-start.13 = (bf16[4,512,128]{2,1,0:T(8,128)(2,1)}, bf16[4,512,128]{2,1,0:T(8,128)(2,1)}, u32[]{:S(2)}, u32[]{:S(2)}) collective-permute-start(bf16[4,512,128]{2,1,0:T(8,128)(2,1)} %get-tuple-element.32), channel_id=1, source_target_pairs={{0,6},{1,25},{2,0},{3,27},{4,2},{5,29},{6,4},{7,31},{8,14},{9,1},{... | collective-permute-start | bytes 1572872 | tf_op jit(solution)/shard_map/ppermute | solution.py:96
  59.1 0.5 collective-permute-start.11
  59.5 0.6 slice_bitcast_fusion.3
  60.1 3.6 %collective-permute-start.17 = (bf16[1040,128]{1,0:T(8,128)(2,1)S(1)}, bf16[1040,128]{1,0:T(8,128)(2,1)}, u32[]{:S(2)}, u32[]{:S(2)}) collective-permute-start(bf16[1040,128]{1,0:T(8,128)(2,1)S(1)} %turn.1.refs_3_.refs_8_), channel_id=1, source_target_pairs={{0,64},{32,96},{64,0},{96,32},{1,65},{33,97},{65,1},{97,33},{2,66}... | collective-permute-start | bytes 798728 | tf_op jit(solution)/shard_map/ppermute | solution.py:448
  63.7 0.5 slice_bitcast_fusion
  64.2 0.6 slice_bitcast_fusion.1
  64.8 0.7 copy-done.1
  65.5 1.5 %pack.1.refs_9_ = bf16[32,4,4,256]{3,2,1,0:T(4,128)(2,1)} custom-call(bf16[512,256]{1,0:T(8,128)(2,1)S(1)} %get-tuple-element.27.refs_0_, bf16[512,512]{1,0:T(8,128)(2,1)S(1)} %copy-done, bf16[4,512,128]{2,1,0:T(8,128)(2,1)} %get-tuple-element.30.refs_2_, bf16[1040,128]{1,0:T(8,128)(2,1)S(1)} %turn.1.refs_3_.refs_8_), custom_call_target="tpu_custom_call" | custom-call | tf_op jit(solution)/shard_map/pack/pallas_call | solution.py:263
  67.1 7.4 %all-to-all-start = ((bf16[32,4,4,256]{3,2,1,0:T(4,128)(2,1)}), bf16[32,4,4,256]{3,2,1,0:T(4,128)(2,1)S(1)}, u32[]{:S(2)}, u32[]{:S(2)}) async-start(bf16[32,4,4,256]{3,2,1,0:T(4,128)(2,1)} %pack.1.refs_9_), calls=%async_computation | async-start | bytes 524288 | tf_op jit(solution)/shard_map/all_to_all | solution.py:453
  74.5 2.7 %second_sum.1 = (bf16[512,128]{1,0:T(8,128)(2,1)}, bf16[512,128]{1,0:T(8,128)(2,1)}, bf16[512,128]{1,0:T(8,128)(2,1)}) custom-call(s32[115]{0:T(128)S(1)} %dynamic-slice_bitcast_fusion.refs_5_.where.table.places, bf16[16,512,128]{2,1,0:T(8,128)(2,1)S(1)} %get-tuple-element.28.refs_0_.refs_1_.refs_2_, ...), custom_call_target="tpu_custom_call" | custom-call | tf_op jit(solution)/shard_map/second_sum/pallas_call | solution.py:316
  77.2 1.4 %collective-permute-start.15 = (bf16[512,128]{1,0:T(8,128)(2,1)}, bf16[512,128]{1,0:T(8,128)(2,1)}, u32[]{:S(2)}, u32[]{:S(2)}) collective-permute-start(bf16[512,128]{1,0:T(8,128)(2,1)} %get-tuple-element.34), channel_id=1, source_target_pairs={{0,8},{1,3},{2,10},{3,5},{4,12},{5,7},{6,14},{7,1},{8,16},{9,11},{... | collective-permute-start | bytes 393224 | tf_op jit(solution)/shard_map/ppermute | solution.py:96
  78.6 1.3 collective-permute-start.16
  79.9 1.7 %collective-permute-start.14 = (bf16[512,128]{1,0:T(8,128)(2,1)}, bf16[512,128]{1,0:T(8,128)(2,1)}, u32[]{:S(2)}, u32[]{:S(2)}) collective-permute-start(bf16[512,128]{1,0:T(8,128)(2,1)} %get-tuple-element.33.refs_10_), channel_id=1, source_target_pairs={{0,16},{1,5},{2,18},{3,7},{4,20},{5,1},{6,22},{7,3},{8,24},{9,13},... | collective-permute-start | bytes 393224 | tf_op jit(solution)/shard_map/ppermute | solution.py:96
  81.6 0.7 slice_bitcast_fusion.2
  82.3 0.1 maximum_convert_fusion.refs_11_.ids
  82.3 1.1 all-to-all-done.refs_12_
  83.4 2.4 %collective-permute-done.14.refs_5_ = bf16[512,128]{1,0:T(8,128)(2,1)} collective-permute-done((bf16[512,128]{1,0:T(8,128)(2,1)}, bf16[512,128]{1,0:T(8,128)(2,1)}, u32[]{:S(2)}, u32[]{:S(2)}) %collective-permute-start.14) | collective-permute-done | bytes 131104 | tf_op jit(solution)/shard_map/ppermute | solution.py:96
  85.8 0.7 copy-done.5
  86.5 1.9 %error.1 = (bf16[512,128]{1,0:T(8,128)(2,1)S(1)}, bf16[512,128]{1,0:T(8,128)(2,1)S(1)}) custom-call(s32[115]{0:T(128)S(1)} %dynamic-slice_bitcast_fusion.refs_5_.where.table.places, bf16[16,512,128]{2,1,0:T(8,128)(2,1)S(1)} %get-tuple-element.28.refs_0_.refs_1_.refs_2_, bf16[16,512,128]{2,1,0:T(8,128)(2,1)} %collective-permute-done.10.refs_3_.refs_4_.refs_5_.refs_1_, ...), custom_call_target="tpu_custom_call" | custom-call | tf_op jit(solution)/shard_map/error/pallas_call | solution.py:350
  88.5 0.7 collective-permute-start.20
  89.1 1.2 collective-permute-start.24
  90.3 0.4 collective-permute-start.23
  90.7 1.4 %collective-permute-start.22 = (bf16[512,128]{1,0:T(8,128)(2,1)S(1)}, bf16[512,128]{1,0:T(8,128)(2,1)S(1)}, u32[]{:S(2)}, u32[]{:S(2)}) collective-permute-start(bf16[512,128]{1,0:T(8,128)(2,1)S(1)} %get-tuple-element.38), channel_id=1, source_target_pairs={{0,16},{1,5},{2,18},{3,7},{4,20},{5,1},{6,22},{7,3},{8,56},{9,45},... | collective-permute-start | bytes 393224 | tf_op jit(solution)/shard_map/ppermute | solution.py:476
  92.1 0.7 collective-permute-start.21
  92.7 0.3 collective-permute-done.24.refs_3_
  93.0 3.7 %collective-permute-done.23.refs_2_ = bf16[512,128]{1,0:T(8,128)(2,1)S(1)} collective-permute-done((bf16[512,128]{1,0:T(8,128)(2,1)S(1)}, bf16[512,128]{1,0:T(8,128)(2,1)S(1)}, u32[]{:S(2)}, u32[]{:S(2)}) %collective-permute-start.23) | collective-permute-done | bytes 131104 | tf_op jit(solution)/shard_map/ppermute | solution.py:476
  96.8 8.6 %collective-permute-start.27 = (bf16[4,512,128]{2,1,0:T(8,128)(2,1)S(1)}, bf16[4,512,128]{2,1,0:T(8,128)(2,1)S(1)}, u32[]{:S(2)}, u32[]{:S(2)}) collective-permute-start(bf16[4,512,128]{2,1,0:T(8,128)(2,1)S(1)} %stack4.3.refs_0_), channel_id=1, source_target_pairs={{0,6},{1,25},{2,0},{3,27},{4,2},{5,29},{6,4},{7,31},{8,14},{9,1},{... | collective-permute-start | bytes 1572872 | tf_op jit(solution)/shard_map/ppermute | solution.py:96
  105.4 1.1 collective-permute-start.26
  106.5 2.3 %collective-permute-start.25 = (bf16[4,512,128]{2,1,0:T(8,128)(2,1)S(1)}, bf16[4,512,128]{2,1,0:T(8,128)(2,1)S(1)}, u32[]{:S(2)}, u32[]{:S(2)}) collective-permute-start(bf16[4,512,128]{2,1,0:T(8,128)(2,1)S(1)} %stack4.3.refs_0_), channel_id=1, source_target_pairs={{0,4},{1,17},{2,6},{3,19},{4,0},{5,21},{6,2},{7,23},{8,12},{9,25},... | collective-permute-start | bytes 1572872 | tf_op jit(solution)/shard_map/ppermute | solution.py:96
  108.8 1.0 collective-permute-start.28
  109.7 3.5 %collective-permute-done.27.refs_3_ = bf16[4,512,128]{2,1,0:T(8,128)(2,1)S(1)} collective-permute-done((bf16[4,512,128]{2,1,0:T(8,128)(2,1)S(1)}, bf16[4,512,128]{2,1,0:T(8,128)(2,1)S(1)}, u32[]{:S(2)}, u32[]{:S(2)}) %collective-permute-start.27) | collective-permute-done | bytes 524320 | tf_op jit(solution)/shard_map/ppermute | solution.py:96
  113.3 7.3 %collective-permute-start.31 = (bf16[4,512,128]{2,1,0:T(8,128)(2,1)S(1)}, bf16[4,512,128]{2,1,0:T(8,128)(2,1)S(1)}, u32[]{:S(2)}, u32[]{:S(2)}) collective-permute-start(bf16[4,512,128]{2,1,0:T(8,128)(2,1)S(1)} %collective-permute-done.27.refs_3_), channel_id=1, source_target_pairs={{0,1},{1,0},{2,3},{3,2},{4,5},{5,4},{6,7},{7,6},{8,9},{9,8},{10,11... | collective-permute-start | bytes 1572872 | tf_op jit(solution)/shard_map/ppermute | solution.py:96
  120.5 3.7 %collective-permute-start.30 = (bf16[4,512,128]{2,1,0:T(8,128)(2,1)S(1)}, bf16[4,512,128]{2,1,0:T(8,128)(2,1)S(1)}, u32[]{:S(2)}, u32[]{:S(2)}) collective-permute-start(bf16[4,512,128]{2,1,0:T(8,128)(2,1)S(1)} %collective-permute-done.26.refs_2_), channel_id=1, source_target_pairs={{0,1},{1,0},{2,3},{3,2},{4,5},{5,4},{6,7},{7,6},{8,9},{9,8},{10,11... | collective-permute-start | bytes 1572872 | tf_op jit(solution)/shard_map/ppermute | solution.py:96
  124.2 0.8 copy.11
  125.0 0.7 collective-permute-done.30.refs_6_
  125.7 0.7 collective-permute-done.29.refs_5_
  126.5 7.4 %grad.1 = f32[2048,1024]{1,0:T(8,128)} custom-call(s32[64]{0:T(128)S(1)} %maximum_convert_fusion.refs_11_.ids, s32[115]{0:T(128)S(1)} %dynamic-slice_bitcast_fusion.refs_5_.where.table.places, bf16[4,512,128]{2,1,0:T(8,128)(2,1)S(1)} %stack4.3.refs_0_, bf16[4,512,128]{2,1,0:T(8,128)(2,1)S(1)} %collective-permute-done.25.refs_1_, ...), custom_call_target="tpu_custom_call" | custom-call | flops 1000000000 | bytes 14680064 | tf_op jit(solution)/shard_map/grad/pallas_call | solution.py:400
  133.9 0.7 copy.13
  (45 shorter events, 0.3 us)
Async XLA Ops:
  0.6 7.2 %collective-permute-start.1 = (bf16[512,128]{1,0:T(8,128)(2,1)}, bf16[512,128]{1,0:T(8,128)(2,1)S(1)}, u32[]{:S(2)}, u32[]{:S(2)}) collective-permute-start(bf16[512,128]{1,0:T(8,128)(2,1)} %refs_0_.1), channel_id=1, source_target_pairs={{0,8},{1,3},{2,10},{3,5},{4,12},{5,7},{6,14},{7,1},{8,16},{9,11},{... | collective-permute-start | bytes 393224 | tf_op jit(solution)/shard_map/ppermute | solution.py:96
  2.7 6.7 %collective-permute-start = (bf16[512,128]{1,0:T(8,128)(2,1)}, bf16[512,128]{1,0:T(8,128)(2,1)S(1)}, u32[]{:S(2)}, u32[]{:S(2)}) collective-permute-start(bf16[512,128]{1,0:T(8,128)(2,1)} %refs_0_.1), channel_id=1, source_target_pairs={{0,16},{1,5},{2,18},{3,7},{4,20},{5,1},{6,22},{7,3},{8,24},{9,13},... | collective-permute-start | bytes 393224 | tf_op jit(solution)/shard_map/ppermute | solution.py:96
  5.2 4.3 %collective-permute-start.2 = (bf16[512,128]{1,0:T(8,128)(2,1)}, bf16[512,128]{1,0:T(8,128)(2,1)S(1)}, u32[]{:S(2)}, u32[]{:S(2)}) collective-permute-start(bf16[512,128]{1,0:T(8,128)(2,1)} %refs_0_.1), channel_id=1, source_target_pairs={{0,24},{1,7},{2,26},{3,1},{4,28},{5,3},{6,30},{7,5},{8,0},{9,15},{... | collective-permute-start | bytes 393224 | tf_op jit(solution)/shard_map/ppermute | solution.py:96
  9.5 0.9 copy-start.3
  10.5 14.3 %collective-permute-start.5 = (bf16[4,512,128]{2,1,0:T(8,128)(2,1)S(1)}, bf16[4,512,128]{2,1,0:T(8,128)(2,1)S(1)}, u32[]{:S(2)}, u32[]{:S(2)}) collective-permute-start(bf16[4,512,128]{2,1,0:T(8,128)(2,1)S(1)} %stack4.2.refs_0_), channel_id=1, source_target_pairs={{0,6},{1,25},{2,0},{3,27},{4,2},{5,29},{6,4},{7,31},{8,14},{9,1},{... | collective-permute-start | bytes 1572872 | tf_op jit(solution)/shard_map/ppermute | solution.py:96
  13.0 15.2 %collective-permute-start.4 = (bf16[4,512,128]{2,1,0:T(8,128)(2,1)S(1)}, bf16[4,512,128]{2,1,0:T(8,128)(2,1)S(1)}, u32[]{:S(2)}, u32[]{:S(2)}) collective-permute-start(bf16[4,512,128]{2,1,0:T(8,128)(2,1)S(1)} %stack4.2.refs_0_), channel_id=1, source_target_pairs={{0,2},{1,9},{2,4},{3,11},{4,6},{5,13},{6,0},{7,15},{8,10},{9,17},{... | collective-permute-start | bytes 1572872 | tf_op jit(solution)/shard_map/ppermute | solution.py:96
  13.0 18.7 %collective-permute-start.3 = (bf16[4,512,128]{2,1,0:T(8,128)(2,1)S(1)}, bf16[4,512,128]{2,1,0:T(8,128)(2,1)S(1)}, u32[]{:S(2)}, u32[]{:S(2)}) collective-permute-start(bf16[4,512,128]{2,1,0:T(8,128)(2,1)S(1)} %stack4.2.refs_0_), channel_id=1, source_target_pairs={{0,4},{1,17},{2,6},{3,19},{4,0},{5,21},{6,2},{7,23},{8,12},{9,25},... | collective-permute-start | bytes 1572872 | tf_op jit(solution)/shard_map/ppermute | solution.py:96
  14.9 16.7 %collective-permute-start.6 = (bf16[4,512,128]{2,1,0:T(8,128)(2,1)S(1)}, bf16[4,512,128]{2,1,0:T(8,128)(2,1)S(1)}, u32[]{:S(2)}, u32[]{:S(2)}) collective-permute-start(bf16[4,512,128]{2,1,0:T(8,128)(2,1)S(1)} %stack4.2.refs_0_), channel_id=1, source_target_pairs={{0,1},{1,0},{2,3},{3,2},{4,5},{5,4},{6,7},{7,6},{8,9},{9,8},{10,11... | collective-permute-start | bytes 1572872 | tf_op jit(solution)/shard_map/ppermute | solution.py:96
  24.7 6.9 %collective-permute-start.9 = (bf16[4,512,128]{2,1,0:T(8,128)(2,1)S(1)}, bf16[4,512,128]{2,1,0:T(8,128)(2,1)S(1)}, u32[]{:S(2)}, u32[]{:S(2)}) collective-permute-start(bf16[4,512,128]{2,1,0:T(8,128)(2,1)S(1)} %collective-permute-done.5.refs_3_), channel_id=1, source_target_pairs={{0,1},{1,0},{2,3},{3,2},{4,5},{5,4},{6,7},{7,6},{8,9},{9,8},{10,11... | collective-permute-start | bytes 1572872 | tf_op jit(solution)/shard_map/ppermute | solution.py:96
  28.1 5.1 %collective-permute-start.8 = (bf16[4,512,128]{2,1,0:T(8,128)(2,1)S(1)}, bf16[4,512,128]{2,1,0:T(8,128)(2,1)S(1)}, u32[]{:S(2)}, u32[]{:S(2)}) collective-permute-start(bf16[4,512,128]{2,1,0:T(8,128)(2,1)S(1)} %collective-permute-done.4.refs_2_), channel_id=1, source_target_pairs={{0,1},{1,0},{2,3},{3,2},{4,5},{5,4},{6,7},{7,6},{8,9},{9,8},{10,11... | collective-permute-start | bytes 1572872 | tf_op jit(solution)/shard_map/ppermute | solution.py:96
  31.6 2.3 %collective-permute-start.7 = (bf16[4,512,128]{2,1,0:T(8,128)(2,1)S(1)}, bf16[4,512,128]{2,1,0:T(8,128)(2,1)S(1)}, u32[]{:S(2)}, u32[]{:S(2)}) collective-permute-start(bf16[4,512,128]{2,1,0:T(8,128)(2,1)S(1)} %collective-permute-done.3.refs_1_), channel_id=1, source_target_pairs={{0,1},{1,0},{2,3},{3,2},{4,5},{5,4},{6,7},{7,6},{8,9},{9,8},{10,11... | collective-permute-start | bytes 1572872 | tf_op jit(solution)/shard_map/ppermute | solution.py:96
  33.9 0.7 copy-start.4
  34.6 0.7 copy-start.6
  35.3 0.7 copy-start.7
  47.7 4.5 %collective-permute-start.10 = (bf16[16,512,128]{2,1,0:T(8,128)(2,1)}, bf16[16,512,128]{2,1,0:T(8,128)(2,1)}, u32[]{:S(2)}, u32[]{:S(2)}) collective-permute-start(bf16[16,512,128]{2,1,0:T(8,128)(2,1)} %get-tuple-element.29), channel_id=1, source_target_pairs={{0,1},{1,0},{2,3},{3,2},{4,5},{5,4},{6,7},{7,6},{8,9},{9,8},{10,11... | collective-permute-start | bytes 6291464 | tf_op jit(solution)/shard_map/ppermute | solution.py:96
  48.0 12.1 %collective-permute-start.19 = (bf16[1040,128]{1,0:T(8,128)(2,1)S(1)}, bf16[1040,128]{1,0:T(8,128)(2,1)S(1)}, u32[]{:S(2)}, u32[]{:S(2)}) collective-permute-start(bf16[1040,128]{1,0:T(8,128)(2,1)S(1)} %turn.1.refs_3_.refs_8_), channel_id=1, source_target_pairs={{0,96},{32,0},{64,32},{96,64},{1,97},{33,1},{65,33},{97,65},{2,98}... | collective-permute-start | bytes 798728 | tf_op jit(solution)/shard_map/ppermute | solution.py:448
  51.9 12.4 %collective-permute-start.18 = (bf16[1040,128]{1,0:T(8,128)(2,1)S(1)}, bf16[1040,128]{1,0:T(8,128)(2,1)S(1)}, u32[]{:S(2)}, u32[]{:S(2)}) collective-permute-start(bf16[1040,128]{1,0:T(8,128)(2,1)S(1)} %turn.1.refs_3_.refs_8_), channel_id=1, source_target_pairs={{0,32},{32,64},{64,96},{96,0},{1,33},{33,65},{65,97},{97,1},{2,34}... | collective-permute-start | bytes 798728 | tf_op jit(solution)/shard_map/ppermute | solution.py:448
  52.2 13.3 %copy-start = (bf16[512,512]{1,0:T(8,128)(2,1)S(1)}, bf16[512,512]{1,0:T(8,128)(2,1)}, u32[]{:S(2)}) copy-start(bf16[512,512]{1,0:T(8,128)(2,1)} %constant.49.clone.refs_1_) | copy-start | bytes 1572868
  56.4 18.1 %collective-permute-start.12 = (bf16[4,512,128]{2,1,0:T(8,128)(2,1)}, bf16[4,512,128]{2,1,0:T(8,128)(2,1)S(1)}, u32[]{:S(2)}, u32[]{:S(2)}) collective-permute-start(bf16[4,512,128]{2,1,0:T(8,128)(2,1)} %get-tuple-element.31), channel_id=1, source_target_pairs={{0,2},{1,9},{2,4},{3,11},{4,6},{5,13},{6,0},{7,15},{8,10},{9,17},{... | collective-permute-start | bytes 1572872 | tf_op jit(solution)/shard_map/ppermute | solution.py:96
  56.8 17.7 %collective-permute-start.13 = (bf16[4,512,128]{2,1,0:T(8,128)(2,1)}, bf16[4,512,128]{2,1,0:T(8,128)(2,1)}, u32[]{:S(2)}, u32[]{:S(2)}) collective-permute-start(bf16[4,512,128]{2,1,0:T(8,128)(2,1)} %get-tuple-element.32), channel_id=1, source_target_pairs={{0,6},{1,25},{2,0},{3,27},{4,2},{5,29},{6,4},{7,31},{8,14},{9,1},{... | collective-permute-start | bytes 1572872 | tf_op jit(solution)/shard_map/ppermute | solution.py:96
  59.1 15.4 %collective-permute-start.11 = (bf16[4,512,128]{2,1,0:T(8,128)(2,1)}, bf16[4,512,128]{2,1,0:T(8,128)(2,1)}, u32[]{:S(2)}, u32[]{:S(2)}) collective-permute-start(bf16[4,512,128]{2,1,0:T(8,128)(2,1)} %get-tuple-element.30.refs_2_), channel_id=1, source_target_pairs={{0,4},{1,17},{2,6},{3,19},{4,0},{5,21},{6,2},{7,23},{8,12},{9,25},... | collective-permute-start | bytes 1572872 | tf_op jit(solution)/shard_map/ppermute | solution.py:96
  60.1 21.4 %collective-permute-start.17 = (bf16[1040,128]{1,0:T(8,128)(2,1)S(1)}, bf16[1040,128]{1,0:T(8,128)(2,1)}, u32[]{:S(2)}, u32[]{:S(2)}) collective-permute-start(bf16[1040,128]{1,0:T(8,128)(2,1)S(1)} %turn.1.refs_3_.refs_8_), channel_id=1, source_target_pairs={{0,64},{32,96},{64,0},{96,32},{1,65},{33,97},{65,1},{97,33},{2,66}... | collective-permute-start | bytes 798728 | tf_op jit(solution)/shard_map/ppermute | solution.py:448
  64.8 0.7 copy-start.1
  67.1 16.3 %all-to-all-start = ((bf16[32,4,4,256]{3,2,1,0:T(4,128)(2,1)}), bf16[32,4,4,256]{3,2,1,0:T(4,128)(2,1)S(1)}, u32[]{:S(2)}, u32[]{:S(2)}) async-start(bf16[32,4,4,256]{3,2,1,0:T(4,128)(2,1)} %pack.1.refs_9_), calls=%async_computation | async-start | bytes 524288 | tf_op jit(solution)/shard_map/all_to_all | solution.py:453
  74.5 7.8 %copy-start.8 = (bf16[16]{0:T(256)(128)(2,1)S(1)}, bf16[16]{0:T(256)(128)(2,1)}, u32[]{:S(2)}) copy-start(bf16[16]{0:T(256)(128)(2,1)} %slice_bitcast_fusion.3) | copy-start | bytes 100
  74.5 7.8 %copy-start.9 = (bf16[16]{0:T(256)(128)(2,1)S(1)}, bf16[16]{0:T(256)(128)(2,1)}, u32[]{:S(2)}) copy-start(bf16[16]{0:T(256)(128)(2,1)} %slice_bitcast_fusion) | copy-start | bytes 100
  74.5 7.8 %copy-start.10 = (bf16[16]{0:T(256)(128)(2,1)S(1)}, bf16[16]{0:T(256)(128)(2,1)}, u32[]{:S(2)}) copy-start(bf16[16]{0:T(256)(128)(2,1)} %slice_bitcast_fusion.1) | copy-start | bytes 100
  77.2 6.2 %collective-permute-start.15 = (bf16[512,128]{1,0:T(8,128)(2,1)}, bf16[512,128]{1,0:T(8,128)(2,1)}, u32[]{:S(2)}, u32[]{:S(2)}) collective-permute-start(bf16[512,128]{1,0:T(8,128)(2,1)} %get-tuple-element.34), channel_id=1, source_target_pairs={{0,8},{1,3},{2,10},{3,5},{4,12},{5,7},{6,14},{7,1},{8,16},{9,11},{... | collective-permute-start | bytes 393224 | tf_op jit(solution)/shard_map/ppermute | solution.py:96
  78.6 4.8 %collective-permute-start.16 = (bf16[512,128]{1,0:T(8,128)(2,1)}, bf16[512,128]{1,0:T(8,128)(2,1)}, u32[]{:S(2)}, u32[]{:S(2)}) collective-permute-start(bf16[512,128]{1,0:T(8,128)(2,1)} %get-tuple-element.35), channel_id=1, source_target_pairs={{0,24},{1,7},{2,26},{3,1},{4,28},{5,3},{6,30},{7,5},{8,0},{9,15},{... | collective-permute-start | bytes 393224 | tf_op jit(solution)/shard_map/ppermute | solution.py:96
  79.9 5.9 %collective-permute-start.14 = (bf16[512,128]{1,0:T(8,128)(2,1)}, bf16[512,128]{1,0:T(8,128)(2,1)}, u32[]{:S(2)}, u32[]{:S(2)}) collective-permute-start(bf16[512,128]{1,0:T(8,128)(2,1)} %get-tuple-element.33.refs_10_), channel_id=1, source_target_pairs={{0,16},{1,5},{2,18},{3,7},{4,20},{5,1},{6,22},{7,3},{8,24},{9,13},... | collective-permute-start | bytes 393224 | tf_op jit(solution)/shard_map/ppermute | solution.py:96
  85.8 0.7 copy-start.5
  86.5 40.0 %copy-start.2 = (bf16[1040,128]{1,0:T(8,128)(2,1)S(1)}, bf16[1040,128]{1,0:T(8,128)(2,1)}, u32[]{:S(2)}) copy-start(bf16[1040,128]{1,0:T(8,128)(2,1)} %copy-done.1) | copy-start | bytes 798724
  88.5 4.3 %collective-permute-start.20 = (bf16[512,128]{1,0:T(8,128)(2,1)S(1)}, bf16[512,128]{1,0:T(8,128)(2,1)S(1)}, u32[]{:S(2)}, u32[]{:S(2)}) collective-permute-start(bf16[512,128]{1,0:T(8,128)(2,1)S(1)} %get-tuple-element.37), channel_id=1, source_target_pairs={{0,0},{1,1},{2,2},{3,3},{4,4},{5,5},{6,6},{7,7},{8,8},{9,9},{10,10... | collective-permute-start | bytes 393224 | tf_op jit(solution)/shard_map/ppermute | solution.py:472
  89.1 3.9 %collective-permute-start.24 = (bf16[512,128]{1,0:T(8,128)(2,1)S(1)}, bf16[512,128]{1,0:T(8,128)(2,1)S(1)}, u32[]{:S(2)}, u32[]{:S(2)}) collective-permute-start(bf16[512,128]{1,0:T(8,128)(2,1)S(1)} %get-tuple-element.38), channel_id=1, source_target_pairs={{0,24},{1,7},{2,26},{3,1},{4,28},{5,3},{6,30},{7,5},{8,32},{9,47},... | collective-permute-start | bytes 393224 | tf_op jit(solution)/shard_map/ppermute | solution.py:476
  90.3 6.4 %collective-permute-start.23 = (bf16[512,128]{1,0:T(8,128)(2,1)S(1)}, bf16[512,128]{1,0:T(8,128)(2,1)S(1)}, u32[]{:S(2)}, u32[]{:S(2)}) collective-permute-start(bf16[512,128]{1,0:T(8,128)(2,1)S(1)} %get-tuple-element.38), channel_id=1, source_target_pairs={{0,8},{1,3},{2,10},{3,5},{4,12},{5,7},{6,14},{7,1},{8,48},{9,43},{... | collective-permute-start | bytes 393224 | tf_op jit(solution)/shard_map/ppermute | solution.py:476
  90.7 6.1 %collective-permute-start.22 = (bf16[512,128]{1,0:T(8,128)(2,1)S(1)}, bf16[512,128]{1,0:T(8,128)(2,1)S(1)}, u32[]{:S(2)}, u32[]{:S(2)}) collective-permute-start(bf16[512,128]{1,0:T(8,128)(2,1)S(1)} %get-tuple-element.38), channel_id=1, source_target_pairs={{0,16},{1,5},{2,18},{3,7},{4,20},{5,1},{6,22},{7,3},{8,56},{9,45},... | collective-permute-start | bytes 393224 | tf_op jit(solution)/shard_map/ppermute | solution.py:476
  92.1 4.7 %collective-permute-start.21 = (bf16[512,128]{1,0:T(8,128)(2,1)S(1)}, bf16[512,128]{1,0:T(8,128)(2,1)S(1)}, u32[]{:S(2)}, u32[]{:S(2)}) collective-permute-start(bf16[512,128]{1,0:T(8,128)(2,1)S(1)} %get-tuple-element.38), channel_id=1, source_target_pairs={{0,0},{1,1},{2,2},{3,3},{4,4},{5,5},{6,6},{7,7},{8,40},{9,41},{10,... | collective-permute-start | bytes 393224 | tf_op jit(solution)/shard_map/ppermute | solution.py:476
  96.8 16.5 %collective-permute-start.27 = (bf16[4,512,128]{2,1,0:T(8,128)(2,1)S(1)}, bf16[4,512,128]{2,1,0:T(8,128)(2,1)S(1)}, u32[]{:S(2)}, u32[]{:S(2)}) collective-permute-start(bf16[4,512,128]{2,1,0:T(8,128)(2,1)S(1)} %stack4.3.refs_0_), channel_id=1, source_target_pairs={{0,6},{1,25},{2,0},{3,27},{4,2},{5,29},{6,4},{7,31},{8,14},{9,1},{... | collective-permute-start | bytes 1572872 | tf_op jit(solution)/shard_map/ppermute | solution.py:96
  105.4 15.1 %collective-permute-start.26 = (bf16[4,512,128]{2,1,0:T(8,128)(2,1)S(1)}, bf16[4,512,128]{2,1,0:T(8,128)(2,1)S(1)}, u32[]{:S(2)}, u32[]{:S(2)}) collective-permute-start(bf16[4,512,128]{2,1,0:T(8,128)(2,1)S(1)} %stack4.3.refs_0_), channel_id=1, source_target_pairs={{0,2},{1,9},{2,4},{3,11},{4,6},{5,13},{6,0},{7,15},{8,10},{9,17},{... | collective-permute-start | bytes 1572872 | tf_op jit(solution)/shard_map/ppermute | solution.py:96
  106.5 17.7 %collective-permute-start.25 = (bf16[4,512,128]{2,1,0:T(8,128)(2,1)S(1)}, bf16[4,512,128]{2,1,0:T(8,128)(2,1)S(1)}, u32[]{:S(2)}, u32[]{:S(2)}) collective-permute-start(bf16[4,512,128]{2,1,0:T(8,128)(2,1)S(1)} %stack4.3.refs_0_), channel_id=1, source_target_pairs={{0,4},{1,17},{2,6},{3,19},{4,0},{5,21},{6,2},{7,23},{8,12},{9,25},... | collective-permute-start | bytes 1572872 | tf_op jit(solution)/shard_map/ppermute | solution.py:96
  108.8 16.3 %collective-permute-start.28 = (bf16[4,512,128]{2,1,0:T(8,128)(2,1)S(1)}, bf16[4,512,128]{2,1,0:T(8,128)(2,1)S(1)}, u32[]{:S(2)}, u32[]{:S(2)}) collective-permute-start(bf16[4,512,128]{2,1,0:T(8,128)(2,1)S(1)} %stack4.3.refs_0_), channel_id=1, source_target_pairs={{0,1},{1,0},{2,3},{3,2},{4,5},{5,4},{6,7},{7,6},{8,9},{9,8},{10,11... | collective-permute-start | bytes 1572872 | tf_op jit(solution)/shard_map/ppermute | solution.py:96
  113.3 11.8 %collective-permute-start.31 = (bf16[4,512,128]{2,1,0:T(8,128)(2,1)S(1)}, bf16[4,512,128]{2,1,0:T(8,128)(2,1)S(1)}, u32[]{:S(2)}, u32[]{:S(2)}) collective-permute-start(bf16[4,512,128]{2,1,0:T(8,128)(2,1)S(1)} %collective-permute-done.27.refs_3_), channel_id=1, source_target_pairs={{0,1},{1,0},{2,3},{3,2},{4,5},{5,4},{6,7},{7,6},{8,9},{9,8},{10,11... | collective-permute-start | bytes 1572872 | tf_op jit(solution)/shard_map/ppermute | solution.py:96
  120.5 5.2 %collective-permute-start.30 = (bf16[4,512,128]{2,1,0:T(8,128)(2,1)S(1)}, bf16[4,512,128]{2,1,0:T(8,128)(2,1)S(1)}, u32[]{:S(2)}, u32[]{:S(2)}) collective-permute-start(bf16[4,512,128]{2,1,0:T(8,128)(2,1)S(1)} %collective-permute-done.26.refs_2_), channel_id=1, source_target_pairs={{0,1},{1,0},{2,3},{3,2},{4,5},{5,4},{6,7},{7,6},{8,9},{9,8},{10,11... | collective-permute-start | bytes 1572872 | tf_op jit(solution)/shard_map/ppermute | solution.py:96
  124.2 2.3 %collective-permute-start.29 = (bf16[4,512,128]{2,1,0:T(8,128)(2,1)S(1)}, bf16[4,512,128]{2,1,0:T(8,128)(2,1)S(1)}, u32[]{:S(2)}, u32[]{:S(2)}) collective-permute-start(bf16[4,512,128]{2,1,0:T(8,128)(2,1)S(1)} %collective-permute-done.25.refs_1_), channel_id=1, source_target_pairs={{0,1},{1,0},{2,3},{3,2},{4,5},{5,4},{6,7},{7,6},{8,9},{9,8},{10,11... | collective-permute-start | bytes 1572872 | tf_op jit(solution)/shard_map/ppermute | solution.py:96

commit v3 on v2

--- a/solution.py
+++ b/solution.py
@@ -129,36 +129,76 @@
     return mine + [send(v, CORE) for v in mine]
 
 
-def encode_kernel(first, ids, counts, where, *refs):
-    pieces = refs[:8]
+def add_pieces(total, places, numbers, pieces, tiles, dec_bias):
+    for k, ref in zip(numbers, pieces):
+        for e in range(0, 4, 2):
+            offs = [pl.multiple_of(places[4 * k + e + i] * PIECE, PIECE) for i in range(2)]
+            centered = [
+                (ref[e + i].astype(F32) - dec_bias[:, pl.ds(offs[i], PIECE)]).astype(BF)
+                for i in range(2)
+            ]
+            block = [
+                jnp.concatenate([t[:, pl.ds(offs[i], PIECE)] for t in tiles], axis=0)
+                for i in range(2)
+            ]
+            total += lax.dot_general(
+                jnp.concatenate(centered, axis=1),
+                jnp.concatenate(block, axis=1),
+                (((1,), (1,)), ((), ())),
+                preferred_element_type=F32,
+            )
+    return total
+
+
+EARLY, LATE = (0, 1, 4), (2, 3, 5, 6, 7)
+
+
+def begin_kernel(ids, places, *refs):
+    pieces, tiles, dec_bias, out = refs[:3], refs[3:7], refs[7], refs[8]
+    total = jnp.zeros((TILE_ROWS, CAP * LAT_TILE), F32)
+    out[...] = add_pieces(total, places, EARLY, pieces, tiles, dec_bias)
+
+
+def begin(ids, places, pieces, dictionary, dec_bias):
+    return pl.pallas_call(
+        begin_kernel,
+        grid_spec=pltpu.PrefetchScalarGridSpec(
+            num_scalar_prefetch=2,
+            grid=(4,),
+            in_specs=[pl.BlockSpec((4, TILE_ROWS, PIECE), lambda b, *_: (0, b, 0))] * 3
+            + [
+                pl.BlockSpec((LAT_TILE, WIDTH), lambda b, i, w, s=s: (i[b, s], 0))
+                for s in range(CAP)
+            ]
+            + [pl.BlockSpec((1, WIDTH), lambda b, *_: (0, 0))],
+            out_specs=pl.BlockSpec((TILE_ROWS, CAP * LAT_TILE), lambda b, *_: (b, 0)),
+        ),
+        out_shape=jax.ShapeDtypeStruct((ROWS, CAP * LAT_TILE), F32),
+        compiler_params=LARGE,
+        cost_estimate=pl.CostEstimate(
+            flops=10**9, bytes_accessed=48 << 20, transcendentals=0
+        ),
+        name="begin",
+    )(ids, places, *pieces, *([dictionary] * CAP), dec_bias)
+
+
+def encode_kernel(ids, counts, where, *refs):
+    pieces = refs[:5]
+    own_line, next_line, begun = refs[5:8]
     tiles = refs[8:12]
     enc_bias, dec_bias = refs[12:14]
-    codes_out, mine, other, resid, centered = refs[-5:]
-    b = first + pl.program_id(0)
-    for k in range(8):
-        for e in range(4):
-            slot = k * 4 + e
-            off = pl.multiple_of(where[slot] * PIECE, PIECE)
-            raw = pieces[k][e]
-            centered[:, pl.ds(off, PIECE)] = (
-                raw.astype(F32) - dec_bias[:, pl.ds(off, PIECE)]
-            ).astype(BF)
-            if k == 0 or (k < 4 and e == 0):
-
-                @pl.when(where[32] == slot)
-                def _():
-                    resid[...] = raw
-
+    codes_out, mine, other, resid = refs[14:]
+    b = pl.program_id(0)
     step = 512
-    preact = jnp.zeros((TILE_ROWS, CAP * LAT_TILE), F32)
-    for k in range(0, WIDTH, step):
-        block = jnp.concatenate([t[:, k : k + step] for t in tiles], axis=0)
-        preact += lax.dot_general(
-            centered[:, k : k + step],
-            block,
-            (((1,), (1,)), ((), ())),
-            preferred_element_type=F32,
-        )
+    held = [(e, own_line, e) for e in range(4)]
+    held += [(4, next_line, 0), (8, pieces[0], 0), (12, pieces[1], 0)]
+    for slot, ref, e in held:
+
+        @pl.when(where[32] == slot)
+        def _():
+            resid[...] = ref[e]
+
+    preact = add_pieces(begun[...], where, LATE, pieces, tiles, dec_bias)
     bias = jnp.concatenate(
         [enc_bias[pl.ds(ids[b, s], 1), :] for s in range(CAP)], axis=1
     )
@@ -180,52 +220,54 @@
             other[at] = jnp.where(core0, second, first).astype(BF)
 
 
-def encode(first, ids, counts, places, pieces, dictionary, enc_bias, dec_bias, after):
-    rows = pieces[0].shape[1]
+def encode(ids, counts, places, pieces, begun, dictionary, enc_bias, dec_bias):
     piece_spec = pl.BlockSpec((4, TILE_ROWS, PIECE), lambda b, *_: (0, b, 0))
+    code_spec = pl.BlockSpec((TILE_ROWS, CAP * LAT_TILE), lambda b, *_: (b, 0))
     tile_specs = [
-        pl.BlockSpec((LAT_TILE, WIDTH), lambda b, i, n, w, s=s: (i[first + b, s], 0))
-        for s in range(CAP)
+        pl.BlockSpec((LAT_TILE, WIDTH), lambda b, i, n, w, s=s: (i[b, s], 0)) for s in range(CAP)
     ]
     whole = lambda b, *_: (0, 0)
     return pl.pallas_call(
-        functools.partial(encode_kernel, first),
+        encode_kernel,
         grid_spec=pltpu.PrefetchScalarGridSpec(
             num_scalar_prefetch=3,
-            grid=(rows // TILE_ROWS,),
-            in_specs=[piece_spec] * 8
+            grid=(4,),
+            in_specs=[piece_spec] * 6
+            + [pl.BlockSpec((1, TILE_ROWS, PIECE), lambda b, *_: (0, b, 0)), code_spec]
             + tile_specs
-            + [pl.BlockSpec((32, LAT_TILE), whole), pl.BlockSpec((1, WIDTH), whole)]
-            + [ANY] * len(after),
+            + [pl.BlockSpec((32, LAT_TILE), whole), pl.BlockSpec((1, WIDTH), whole)],
             out_specs=[
-                pl.BlockSpec((TILE_ROWS, CAP * LAT_TILE), lambda b, *_: (b, 0)),
-                pl.BlockSpec((16, TILE_ROWS, PIECE), lambda b, *_: (0, b, 0)),
-                pl.BlockSpec((16, TILE_ROWS, PIECE), lambda b, *_: (0, b, 0)),
+                code_spec,
+                piece_spec_of(16),
+                piece_spec_of(16),
                 pl.BlockSpec((TILE_ROWS, PIECE), lambda b, *_: (b, 0)),
             ],
-            scratch_shapes=[pltpu.VMEM((TILE_ROWS, WIDTH), BF)],
         ),
         out_shape=[
-            jax.ShapeDtypeStruct((rows, CAP * LAT_TILE), BF),
-            jax.ShapeDtypeStruct((16, rows, PIECE), BF),
-            jax.ShapeDtypeStruct((16, rows, PIECE), BF),
-            jax.ShapeDtypeStruct((rows, PIECE), BF),
+            jax.ShapeDtypeStruct((ROWS, CAP * LAT_TILE), BF),
+            jax.ShapeDtypeStruct((16, ROWS, PIECE), BF),
+            jax.ShapeDtypeStruct((16, ROWS, PIECE), BF),
+            jax.ShapeDtypeStruct((ROWS, PIECE), BF),
         ],
         compiler_params=LARGE,
-        cost_estimate=pl.CostEstimate(
-            flops=rows << 23, bytes_accessed=rows << 15, transcendentals=0
-        ),
         name="encode",
-    )(ids, counts, places, *pieces, *([dictionary] * CAP), enc_bias, dec_bias, *after)
+    )(
+        ids, counts, places, *[pieces[k] for k in LATE], pieces[0], pieces[1], begun,
+        *([dictionary] * CAP), enc_bias, dec_bias,
+    )
+
+
+def piece_spec_of(count):
+    return pl.BlockSpec((count, TILE_ROWS, PIECE), lambda b, *_: (0, b, 0))
 
 
 def turn_kernel(*refs):
     codes_t = refs[-1]
-    ids = refs[PARTS]
+    ids = refs[1]
     size = CAP * LAT_TILE
     for b in range(4):
         at = b * TILE_ROWS
-        codes = refs[at // HALF][at % HALF : at % HALF + TILE_ROWS, :]
+        codes = refs[0][at : at + TILE_ROWS, :]
         codes_t[b * size : (b + 1) * size, :] = codes.astype(F32).T.astype(BF)
     codes_t[4 * size :, :] = ids[...]
 
@@ -235,19 +277,19 @@
     whole = pl.BlockSpec(memory_space=pltpu.VMEM)
     return pl.pallas_call(
         turn_kernel,
-        in_specs=[whole] * (PARTS + 1) + [ANY] * len(after),
+        in_specs=[whole] * 2 + [ANY] * len(after),
         out_specs=whole,
         out_shape=jax.ShapeDtypeStruct((4 * CAP * LAT_TILE + 16, TILE_ROWS), BF),
         compiler_params=SMALL,
         name="turn",
-    )(*codes, id_rows, *after)
+    )(codes, id_rows, *after)
 
 
 def pack_kernel(*refs):
-    pick, tile_send = refs[PARTS], refs[-1]
+    pick, tile_send = refs[1], refs[-1]
     for b in range(4):
         at = b * TILE_ROWS
-        codes = refs[at // HALF][at % HALF : at % HALF + TILE_ROWS, :]
+        codes = refs[0][at : at + TILE_ROWS, :]
         stacked = jnp.concatenate(
             [codes[:, s * LAT_TILE : (s + 1) * LAT_TILE] for s in range(CAP)], axis=0
         )
@@ -262,12 +304,12 @@
     whole = pl.BlockSpec(memory_space=pltpu.VMEM)
     return pl.pallas_call(
         pack_kernel,
-        in_specs=[whole] * (PARTS + 1) + [ANY] * len(after),
+        in_specs=[whole] * 2 + [ANY] * len(after),
         out_specs=whole,
         out_shape=jax.ShapeDtypeStruct((32, 4, CAP, 4 * LAT_TILE), BF),
         compiler_params=SMALL,
         name="pack",
-    )(*codes, jnp.asarray(pick_matrix(), BF), *after)
+    )(codes, jnp.asarray(pick_matrix(), BF), *after)
 
 
 def first_sum_kernel(table, *refs):
@@ -426,22 +468,20 @@
     dec_row = dec_bias.reshape(1, WIDTH)
     halves = range(PARTS)
 
-    near = [short_gather(residuals[h * HALF : (h + 1) * HALF]) for h in halves]
-    lines = []
-    for h in halves:
-        lines.append(stack4(near[h], [enc_rows, places] if h == 0 else [lines[-1]]))
-    pieces = [long_gather(lines[h]) for h in halves]
-
-    codes, mine, got, resid, sums = [], [], [], [], []
-    for h in halves:
-        c, m, o, r = encode(
-            h * HALF // TILE_ROWS, ids, counts, places, pieces[h], dictionary,
-            enc_rows, dec_row, sums[-1][:1] if sums else [],
-        )
-        codes.append(c), mine.append(m), resid.append(r)
-        got.append(send(o, CORE))
-        sums.append(first_sum(places, mine[h], got[h], []))
-    far = [[send(v, long_leg(d)) for v, d in zip(sums[h], SHIFTS[1:])] for h in halves]
+    line = stack4(short_gather(residuals), [enc_rows, places])
+    own = [line] + [send(line, long_leg(d)) for d in SHIFTS[1:]]
+    swapped = [send(v, CORE) for v in own[:1]]
+    begun = begin(ids, places, own[:2] + swapped, dictionary, dec_row)
+    own[3], begun = lax.optimization_barrier((own[3], begun))
+    pieces = own + swapped + [send(v, CORE) for v in own[1:]]
+
+    codes, m, other, r = encode(
+        ids, counts, places, pieces, begun, dictionary, enc_rows, dec_row
+    )
+    mine, resid = [m], [r]
+    got = [send(other, CORE)]
+    sums = [first_sum(places, m, got[0], [])]
+    far = [[send(v, long_leg(d)) for v, d in zip(sums[0], SHIFTS[1:])]]
 
     codes_t = turn(codes, ids, [])
     all_codes = [codes_t] + [
@@ -469,14 +509,17 @@
         recon.append(r)
         error.append(e)
     whole = recon[0] if PARTS == 1 else jnp.concatenate(recon)
-    reconstruction = lax.ppermute(whole, ("tok", "lat"), TO_HOME)
-    last = reconstruction
     error_lines = []
     for h in halves:
         legs = [lax.ppermute(error[h], ("tok", "lat"), plane_leg(d)) for d in SHIFTS]
         error_lines.append(stack4(legs, [last]))
         last = error_lines[h]
-    errors = [long_gather(error_lines[h]) for h in halves]
+    line = error_lines[0]
+    own = [line] + [send(line, long_leg(d)) for d in SHIFTS[1:]]
+    own[1], whole = lax.optimization_barrier((own[1], whole))
+    reconstruction = lax.ppermute(whole, ("tok", "lat"), TO_HOME)
+    own[3], reconstruction = lax.optimization_barrier((own[3], reconstruction))
+    errors = [own + [send(v, CORE) for v in own]]
     decoder_grad = grad(all_ids, places, sum(errors, []), all_codes, [])
     return (tile_codes, reconstruction, decoder_grad)
 

time: 136 us -> 128 us (0.941)
  starting transfers between devices: 70.5 us -> 58 us
  Pallas kernels: 29.7 us -> 32.7 us
  waiting for transfers between devices: 23.7 us -> 26.3 us
  local copies, waits for them, and re-layouts: 9.75 us -> 8.26 us
    ppermute x24, starting transfers between devices: 51.4 us -> 39 us  [send(): return lax.ppermute(value, 'lat', pairs)]
    pallas_call x3 -> x4, Pallas kernels: 13.4 us -> 16.4 us  [the longest x1 9.43 us: encode(): pl.pallas_call(encode_kernel, grid_spec=pltpu.PrefetchScalarGridSpec(num_...]
    ppermute x24, waiting for transfers between devices: 18.7 us -> 21.2 us  [send(): return lax.ppermute(value, 'lat', pairs)]
    squeeze x4, local copies, waits for them, and re-layouts: 2.33 us -> 0.66 us  [body(): v[4 * CAP * LAT_TILE, :16]]
    unnamed x24 -> x22, local copies, waits for them, and re-layouts: 5.87 us -> 6.04 us
  transfers between devices with their start and end apart: 33 -> 33, of which waited for: 14 -> 12; matrix products, arithmetic and copies ran while one was open for 4% -> 2% of each run, Pallas kernels for 6% -> 11%
where the time goes in v3:
time: 128 us; the launch traced here: 126 us
  starting transfers between devices  58 us (45%)
  Pallas kernels  32.7 us (26%)
  waiting for transfers between devices  26.3 us (21%)
  local copies, waits for them, and re-layouts  8.26 us (6%)
    ppermute x24, starting transfers between devices, send(): return lax.ppermute(value, 'lat', pairs)  39 us
    ppermute x24, waiting for transfers between devices, send(): return lax.ppermute(value, 'lat', pairs)  21.2 us
    pallas_call x1, Pallas kernels, encode(): pl.pallas_call(encode_kernel, grid_spec=pltpu.PrefetchScalarGridSpec(num_...  9.43 us
    pallas_call x1, Pallas kernels, grad(): pl.pallas_call(grad_kernel, grid_spec=pltpu.PrefetchScalarGridSpec(num_sc...  7.44 us
    all_to_all x1, starting transfers between devices, body(): lax.all_to_all(tile_send, 'lat', split_axis=0, concat_axis=0, tiled=True)  7.24 us
    ppermute x3, starting transfers between devices, body(): lax.ppermute(codes_t, 'tok', [(z, (z + s) % SIDE) for z in range(SIDE)])  7.22 us
    unnamed x22, local copies, waits for them, and re-layouts  6.04 us
    pallas_call x1, Pallas kernels, begin(): pl.pallas_call(begin_kernel, grid_spec=pltpu.PrefetchScalarGridSpec(num_s...  5.3 us
  transfers between devices with their start and end apart: 33, of which 12 were waited for; matrix products, arithmetic and copies ran while one was open for 2% of the time, Pallas kernels for 11%

profile of v3, /device:TPU:1, one launch (start us, length us, event | category | flops | bytes accessed | tf_op | source)
XLA Modules:
  0.0 126.1 jit_solution(10932840787853808239)
XLA Ops:
  0.6 2.1 %collective-permute-start.1 = (bf16[512,128]{1,0:T(8,128)(2,1)}, bf16[512,128]{1,0:T(8,128)(2,1)S(1)}, u32[]{:S(2)}, u32[]{:S(2)}) collective-permute-start(bf16[512,128]{1,0:T(8,128)(2,1)} %refs_0_.1), channel_id=1, source_target_pairs={{0,8},{1,3},{2,10},{3,5},{4,12},{5,7},{6,14},{7,1},{8,16},{9,11},{... | collective-permute-start | bytes 393224 | tf_op jit(solution)/shard_map/ppermute | solution.py:96
  2.7 2.5 %collective-permute-start = (bf16[512,128]{1,0:T(8,128)(2,1)}, bf16[512,128]{1,0:T(8,128)(2,1)S(1)}, u32[]{:S(2)}, u32[]{:S(2)}) collective-permute-start(bf16[512,128]{1,0:T(8,128)(2,1)} %refs_0_.1), channel_id=1, source_target_pairs={{0,16},{1,5},{2,18},{3,7},{4,20},{5,1},{6,22},{7,3},{8,24},{9,13},... | collective-permute-start | bytes 393224 | tf_op jit(solution)/shard_map/ppermute | solution.py:96
  5.2 1.2 collective-permute-start.2
  6.3 0.8 reshape.48.refs_4_.refs_12_
  7.1 0.7 dynamic-slice_bitcast_fusion.refs_5_.places.where.table
  7.8 1.6 %collective-permute-done.refs_1_ = bf16[512,128]{1,0:T(8,128)(2,1)S(1)} collective-permute-done((bf16[512,128]{1,0:T(8,128)(2,1)}, bf16[512,128]{1,0:T(8,128)(2,1)S(1)}, u32[]{:S(2)}, u32[]{:S(2)}) %collective-permute-start) | collective-permute-done | bytes 131104 | tf_op jit(solution)/shard_map/ppermute | solution.py:96
  9.5 0.1 collective-permute-done.2.refs_3_
  9.5 0.9 copy-done.7
  10.5 2.4 %collective-permute-start.6 = (bf16[4,512,128]{2,1,0:T(8,128)(2,1)S(1)}, bf16[4,512,128]{2,1,0:T(8,128)(2,1)S(1)}, u32[]{:S(2)}, u32[]{:S(2)}) collective-permute-start(bf16[4,512,128]{2,1,0:T(8,128)(2,1)S(1)} %stack4.2.refs_0_.refs_5_), channel_id=1, source_target_pairs={{0,1},{1,0},{2,3},{3,2},{4,5},{5,4},{6,7},{7,6},{8,9},{9,8},{10,11... | collective-permute-start | bytes 1572872 | tf_op jit(solution)/shard_map/ppermute | solution.py:96
  12.9 2.0 %collective-permute-start.5 = (bf16[4,512,128]{2,1,0:T(8,128)(2,1)S(1)}, bf16[4,512,128]{2,1,0:T(8,128)(2,1)S(1)}, u32[]{:S(2)}, u32[]{:S(2)}) collective-permute-start(bf16[4,512,128]{2,1,0:T(8,128)(2,1)S(1)} %stack4.2.refs_0_.refs_5_), channel_id=1, source_target_pairs={{0,4},{1,17},{2,6},{3,19},{4,0},{5,21},{6,2},{7,23},{8,12},{9,25},... | collective-permute-start | bytes 1572872 | tf_op jit(solution)/shard_map/ppermute | solution.py:96
  14.8 1.1 collective-permute-start.4
  15.9 0.4 collective-permute-start.3
  16.3 6.4 %collective-permute-done.5.refs_1_.refs_6_ = bf16[4,512,128]{2,1,0:T(8,128)(2,1)S(1)} collective-permute-done((bf16[4,512,128]{2,1,0:T(8,128)(2,1)S(1)}, bf16[4,512,128]{2,1,0:T(8,128)(2,1)S(1)}, u32[]{:S(2)}, u32[]{:S(2)}) %collective-permute-start.5) | collective-permute-done | bytes 524320 | tf_op jit(solution)/shard_map/ppermute | solution.py:96
  22.8 0.7 copy-done.3
  23.5 0.7 copy-done.8
  24.2 5.3 %begin.1.refs_7_ = f32[512,256]{1,0:T(8,128)S(1)} custom-call(s32[4,4]{1,0:T(4,128)S(1)} %bitcast.18, s32[115]{0:T(128)S(1)} %dynamic-slice_bitcast_fusion.refs_5_.places.where.table, bf16[4,512,128]{2,1,0:T(8,128)(2,1)S(1)} %stack4.2.refs_0_.refs_5_, bf16[4,512,128]{2,1,0:T(8,128)(2,1)S(1)} %collective-permute-done.5.refs_1_.refs_6_, ...), custom_call_target="tpu_custom_call" | custom-call | flops 1000000000 | bytes 50331648 | tf_op jit(solution)/shard_map/begin/pallas_call | solution.py:163
  29.5 1.1 collective-permute-start.9
  30.6 0.1 collective-permute-start.7
  30.7 0.4 collective-permute-start.8
  31.1 1.8 %collective-permute-done.7.refs_2_ = bf16[4,512,128]{2,1,0:T(8,128)(2,1)S(1)} collective-permute-done((bf16[4,512,128]{2,1,0:T(8,128)(2,1)S(1)}, bf16[4,512,128]{2,1,0:T(8,128)(2,1)S(1)}, u32[]{:S(2)}, u32[]{:S(2)}) %collective-permute-start.7) | collective-permute-done | bytes 524320 | tf_op jit(solution)/shard_map/ppermute | solution.py:96
  32.9 0.7 collective-permute-done.8.refs_3_
  33.6 9.4 %encode.1 = (bf16[512,256]{1,0:T(8,128)(2,1)S(1)}, bf16[16,512,128]{2,1,0:T(8,128)(2,1)S(1)}, bf16[16,512,128]{2,1,0:T(8,128)(2,1)}, bf16[512,128]{1,0:T(8,128)(2,1)S(1)}) custom-call(s32[4,4]{1,0:T(4,128)S(1)} %bitcast.19, s32[4]{0:T(128)S(1)} %bitcast.20, s32[115]{0:T(128)S(1)} %dynamic-slice_bitcast_fusion.refs_5_.places.where.table, ...), custom_call_target="tpu_custom_call" | custom-call | tf_op jit(solution)/shard_map/encode/pallas_call | solution.py:230
  43.0 0.7 copy-done.5
  43.7 0.4 collective-permute-start.10
  44.1 0.1 convert_element_type.15
  44.2 0.1 turn.1.refs_3_.refs_8_
  44.3 4.0 %collective-permute-start.19 = (bf16[1040,128]{1,0:T(8,128)(2,1)S(1)}, bf16[1040,128]{1,0:T(8,128)(2,1)S(1)}, u32[]{:S(2)}, u32[]{:S(2)}) collective-permute-start(bf16[1040,128]{1,0:T(8,128)(2,1)S(1)} %turn.1.refs_3_.refs_8_), channel_id=1, source_target_pairs={{0,96},{32,0},{64,32},{96,64},{1,97},{33,1},{65,33},{97,65},{2,98}... | collective-permute-start | bytes 798728 | tf_op jit(solution)/shard_map/ppermute | solution.py:488
  48.3 4.2 %first_sum.1 = (bf16[4,512,128]{2,1,0:T(8,128)(2,1)}, bf16[4,512,128]{2,1,0:T(8,128)(2,1)}, bf16[4,512,128]{2,1,0:T(8,128)(2,1)}) custom-call(s32[115]{0:T(128)S(1)} %dynamic-slice_bitcast_fusion.refs_5_.places.where.table, bf16[16,512,128]{2,1,0:T(8,128)(2,1)S(1)} %get-tuple-element.36.refs_0_.refs_1_.refs_2_, ...), custom_call_target="tpu_custom_call" | custom-call | tf_op jit(solution)/shard_map/first_sum/pallas_call | solution.py:327
  52.5 0.7 collective-permute-start.12
  53.2 1.9 %collective-permute-start.13 = (bf16[4,512,128]{2,1,0:T(8,128)(2,1)}, bf16[4,512,128]{2,1,0:T(8,128)(2,1)}, u32[]{:S(2)}, u32[]{:S(2)}) collective-permute-start(bf16[4,512,128]{2,1,0:T(8,128)(2,1)} %get-tuple-element.40), channel_id=1, source_target_pairs={{0,6},{1,25},{2,0},{3,27},{4,2},{5,29},{6,4},{7,31},{8,14},{9,1},{... | collective-permute-start | bytes 1572872 | tf_op jit(solution)/shard_map/ppermute | solution.py:96
  55.2 1.1 collective-permute-start.11
  56.3 3.2 %collective-permute-start.17 = (bf16[1040,128]{1,0:T(8,128)(2,1)S(1)}, bf16[1040,128]{1,0:T(8,128)(2,1)}, u32[]{:S(2)}, u32[]{:S(2)}) collective-permute-start(bf16[1040,128]{1,0:T(8,128)(2,1)S(1)} %turn.1.refs_3_.refs_8_), channel_id=1, source_target_pairs={{0,64},{32,96},{64,0},{96,32},{1,65},{33,97},{65,1},{97,33},{2,66}... | collective-permute-start | bytes 798728 | tf_op jit(solution)/shard_map/ppermute | solution.py:488
  59.6 0.7 copy-done.1
  60.3 1.5 %pack.1.refs_9_ = bf16[32,4,4,256]{3,2,1,0:T(4,128)(2,1)} custom-call(bf16[512,256]{1,0:T(8,128)(2,1)S(1)} %get-tuple-element.35.refs_0_, bf16[512,512]{1,0:T(8,128)(2,1)S(1)} %copy-done, bf16[4,512,128]{2,1,0:T(8,128)(2,1)} %get-tuple-element.38.refs_2_, bf16[1040,128]{1,0:T(8,128)(2,1)S(1)} %turn.1.refs_3_.refs_8_), custom_call_target="tpu_custom_call" | custom-call | tf_op jit(solution)/shard_map/pack/pallas_call | solution.py:305
  61.8 7.2 %all-to-all-start = ((bf16[32,4,4,256]{3,2,1,0:T(4,128)(2,1)}), bf16[32,4,4,256]{3,2,1,0:T(4,128)(2,1)S(1)}, u32[]{:S(2)}, u32[]{:S(2)}) async-start(bf16[32,4,4,256]{3,2,1,0:T(4,128)(2,1)} %pack.1.refs_9_), calls=%async_computation | async-start | bytes 524288 | tf_op jit(solution)/shard_map/all_to_all | solution.py:493
  69.1 2.7 %second_sum.1 = (bf16[512,128]{1,0:T(8,128)(2,1)}, bf16[512,128]{1,0:T(8,128)(2,1)}, bf16[512,128]{1,0:T(8,128)(2,1)}) custom-call(s32[115]{0:T(128)S(1)} %dynamic-slice_bitcast_fusion.refs_5_.places.where.table, bf16[16,512,128]{2,1,0:T(8,128)(2,1)S(1)} %get-tuple-element.36.refs_0_.refs_1_.refs_2_, ...), custom_call_target="tpu_custom_call" | custom-call | tf_op jit(solution)/shard_map/second_sum/pallas_call | solution.py:358
  71.8 1.4 %collective-permute-start.15 = (bf16[512,128]{1,0:T(8,128)(2,1)}, bf16[512,128]{1,0:T(8,128)(2,1)}, u32[]{:S(2)}, u32[]{:S(2)}) collective-permute-start(bf16[512,128]{1,0:T(8,128)(2,1)} %get-tuple-element.42), channel_id=1, source_target_pairs={{0,8},{1,3},{2,10},{3,5},{4,12},{5,7},{6,14},{7,1},{8,16},{9,11},{... | collective-permute-start | bytes 393224 | tf_op jit(solution)/shard_map/ppermute | solution.py:96
  73.2 1.3 %collective-permute-start.16 = (bf16[512,128]{1,0:T(8,128)(2,1)}, bf16[512,128]{1,0:T(8,128)(2,1)}, u32[]{:S(2)}, u32[]{:S(2)}) collective-permute-start(bf16[512,128]{1,0:T(8,128)(2,1)} %get-tuple-element.43), channel_id=1, source_target_pairs={{0,24},{1,7},{2,26},{3,1},{4,28},{5,3},{6,30},{7,5},{8,0},{9,15},{... | collective-permute-start | bytes 393224 | tf_op jit(solution)/shard_map/ppermute | solution.py:96
  74.5 1.7 %collective-permute-start.14 = (bf16[512,128]{1,0:T(8,128)(2,1)}, bf16[512,128]{1,0:T(8,128)(2,1)}, u32[]{:S(2)}, u32[]{:S(2)}) collective-permute-start(bf16[512,128]{1,0:T(8,128)(2,1)} %get-tuple-element.41.refs_10_), channel_id=1, source_target_pairs={{0,16},{1,5},{2,18},{3,7},{4,20},{5,1},{6,22},{7,3},{8,24},{9,13},... | collective-permute-start | bytes 393224 | tf_op jit(solution)/shard_map/ppermute | solution.py:96
  76.2 0.7 slice_bitcast_fusion.2
  76.8 0.1 maximum_convert_fusion.refs_11_.ids
  76.9 1.1 all-to-all-done.refs_12_
  78.0 2.1 %collective-permute-done.14.refs_5_ = bf16[512,128]{1,0:T(8,128)(2,1)} collective-permute-done((bf16[512,128]{1,0:T(8,128)(2,1)}, bf16[512,128]{1,0:T(8,128)(2,1)}, u32[]{:S(2)}, u32[]{:S(2)}) %collective-permute-start.14) | collective-permute-done | bytes 131104 | tf_op jit(solution)/shard_map/ppermute | solution.py:96
  80.1 0.9 copy-done.6
  81.0 1.9 %error.1 = (bf16[512,128]{1,0:T(8,128)(2,1)S(1)}, bf16[512,128]{1,0:T(8,128)(2,1)S(1)}) custom-call(s32[115]{0:T(128)S(1)} %dynamic-slice_bitcast_fusion.refs_5_.places.where.table, bf16[16,512,128]{2,1,0:T(8,128)(2,1)S(1)} %get-tuple-element.36.refs_0_.refs_1_.refs_2_, bf16[16,512,128]{2,1,0:T(8,128)(2,1)} %collective-permute-done.10.refs_3_.refs_4_.refs_5_.refs_1_, ...), custom_call_target="tpu_custom_call" | custom-call | tf_op jit(solution)/shard_map/error/pallas_call | solution.py:392
  82.9 1.5 %collective-permute-start.23 = (bf16[512,128]{1,0:T(8,128)(2,1)S(1)}, bf16[512,128]{1,0:T(8,128)(2,1)S(1)}, u32[]{:S(2)}, u32[]{:S(2)}) collective-permute-start(bf16[512,128]{1,0:T(8,128)(2,1)S(1)} %get-tuple-element.45), channel_id=1, source_target_pairs={{0,24},{1,7},{2,26},{3,1},{4,28},{5,3},{6,30},{7,5},{8,32},{9,47},... | collective-permute-start | bytes 393224 | tf_op jit(solution)/shard_map/ppermute | solution.py:514
  84.4 0.1 collective-permute-start.22
  84.5 1.7 %collective-permute-start.21 = (bf16[512,128]{1,0:T(8,128)(2,1)S(1)}, bf16[512,128]{1,0:T(8,128)(2,1)S(1)}, u32[]{:S(2)}, u32[]{:S(2)}) collective-permute-start(bf16[512,128]{1,0:T(8,128)(2,1)S(1)} %get-tuple-element.45), channel_id=1, source_target_pairs={{0,16},{1,5},{2,18},{3,7},{4,20},{5,1},{6,22},{7,3},{8,56},{9,45},... | collective-permute-start | bytes 393224 | tf_op jit(solution)/shard_map/ppermute | solution.py:514
  86.1 0.7 collective-permute-start.20
  86.8 4.0 %collective-permute-done.22.refs_2_ = bf16[512,128]{1,0:T(8,128)(2,1)S(1)} collective-permute-done((bf16[512,128]{1,0:T(8,128)(2,1)S(1)}, bf16[512,128]{1,0:T(8,128)(2,1)S(1)}, u32[]{:S(2)}, u32[]{:S(2)}) %collective-permute-start.22) | collective-permute-done | bytes 131104 | tf_op jit(solution)/shard_map/ppermute | solution.py:514
  90.9 10.4 %collective-permute-start.25 = (bf16[4,512,128]{2,1,0:T(8,128)(2,1)S(1)}, bf16[4,512,128]{2,1,0:T(8,128)(2,1)S(1)}, u32[]{:S(2)}, u32[]{:S(2)}) collective-permute-start(bf16[4,512,128]{2,1,0:T(8,128)(2,1)S(1)} %stack4.3.refs_0_), channel_id=1, source_target_pairs={{0,4},{1,17},{2,6},{3,19},{4,0},{5,21},{6,2},{7,23},{8,12},{9,25},... | collective-permute-start | bytes 1572872 | tf_op jit(solution)/shard_map/ppermute | solution.py:96
  101.3 2.7 %collective-permute-start.24 = (bf16[4,512,128]{2,1,0:T(8,128)(2,1)S(1)}, bf16[4,512,128]{2,1,0:T(8,128)(2,1)S(1)}, u32[]{:S(2)}, u32[]{:S(2)}) collective-permute-start(bf16[4,512,128]{2,1,0:T(8,128)(2,1)S(1)} %stack4.3.refs_0_), channel_id=1, source_target_pairs={{0,6},{1,25},{2,0},{3,27},{4,2},{5,29},{6,4},{7,31},{8,14},{9,1},{... | collective-permute-start | bytes 1572872 | tf_op jit(solution)/shard_map/ppermute | solution.py:96
  103.9 4.2 %collective-permute-done.25.refs_1_ = bf16[4,512,128]{2,1,0:T(8,128)(2,1)S(1)} collective-permute-done((bf16[4,512,128]{2,1,0:T(8,128)(2,1)S(1)}, bf16[4,512,128]{2,1,0:T(8,128)(2,1)S(1)}, u32[]{:S(2)}, u32[]{:S(2)}) %collective-permute-start.25) | collective-permute-done | bytes 524320 | tf_op jit(solution)/shard_map/ppermute | solution.py:96
  108.2 0.7 collective-permute-start.26
  108.8 2.1 %collective-permute-start.28 = (bf16[4,512,128]{2,1,0:T(8,128)(2,1)S(1)}, bf16[4,512,128]{2,1,0:T(8,128)(2,1)S(1)}, u32[]{:S(2)}, u32[]{:S(2)}) collective-permute-start(bf16[4,512,128]{2,1,0:T(8,128)(2,1)S(1)} %stack4.3.refs_0_), channel_id=1, source_target_pairs={{0,1},{1,0},{2,3},{3,2},{4,5},{5,4},{6,7},{7,6},{8,9},{9,8},{10,11... | collective-permute-start | bytes 1572872 | tf_op jit(solution)/shard_map/ppermute | solution.py:96
  111.0 0.1 collective-permute-start.29
  111.0 2.7 %collective-permute-done.27.refs_2_ = bf16[4,512,128]{2,1,0:T(8,128)(2,1)S(1)} collective-permute-done((bf16[4,512,128]{2,1,0:T(8,128)(2,1)S(1)}, bf16[4,512,128]{2,1,0:T(8,128)(2,1)S(1)}, u32[]{:S(2)}, u32[]{:S(2)}) %collective-permute-start.27) | collective-permute-done | bytes 524320 | tf_op jit(solution)/shard_map/ppermute | solution.py:96
  113.7 2.0 %collective-permute-start.30 = (bf16[4,512,128]{2,1,0:T(8,128)(2,1)S(1)}, bf16[4,512,128]{2,1,0:T(8,128)(2,1)S(1)}, u32[]{:S(2)}, u32[]{:S(2)}) collective-permute-start(bf16[4,512,128]{2,1,0:T(8,128)(2,1)S(1)} %collective-permute-done.27.refs_2_), channel_id=1, source_target_pairs={{0,1},{1,0},{2,3},{3,2},{4,5},{5,4},{6,7},{7,6},{8,9},{9,8},{10,11... | collective-permute-start | bytes 1572872 | tf_op jit(solution)/shard_map/ppermute | solution.py:96
  115.7 0.1 collective-permute-start.31
  115.8 0.8 copy.11
  116.6 0.6 collective-permute-done.30.refs_6_
  117.3 0.7 collective-permute-done.31.refs_7_
  118.0 7.4 %grad.1 = f32[2048,1024]{1,0:T(8,128)} custom-call(s32[64]{0:T(128)S(1)} %maximum_convert_fusion.refs_11_.ids, s32[115]{0:T(128)S(1)} %dynamic-slice_bitcast_fusion.refs_5_.places.where.table, bf16[4,512,128]{2,1,0:T(8,128)(2,1)S(1)} %stack4.3.refs_0_, bf16[4,512,128]{2,1,0:T(8,128)(2,1)S(1)} %collective-permute-done.25.refs_1_, ...), custom_call_target="tpu_custom_call" | custom-call | flops 1000000000 | bytes 14680064 | tf_op jit(solution)/shard_map/grad/pallas_call | solution.py:442
  125.5 0.7 copy.13
  (44 shorter events, 0.2 us)
Async XLA Ops:
  0.6 7.2 %collective-permute-start.1 = (bf16[512,128]{1,0:T(8,128)(2,1)}, bf16[512,128]{1,0:T(8,128)(2,1)S(1)}, u32[]{:S(2)}, u32[]{:S(2)}) collective-permute-start(bf16[512,128]{1,0:T(8,128)(2,1)} %refs_0_.1), channel_id=1, source_target_pairs={{0,8},{1,3},{2,10},{3,5},{4,12},{5,7},{6,14},{7,1},{8,16},{9,11},{... | collective-permute-start | bytes 393224 | tf_op jit(solution)/shard_map/ppermute | solution.py:96
  2.7 6.7 %collective-permute-start = (bf16[512,128]{1,0:T(8,128)(2,1)}, bf16[512,128]{1,0:T(8,128)(2,1)S(1)}, u32[]{:S(2)}, u32[]{:S(2)}) collective-permute-start(bf16[512,128]{1,0:T(8,128)(2,1)} %refs_0_.1), channel_id=1, source_target_pairs={{0,16},{1,5},{2,18},{3,7},{4,20},{5,1},{6,22},{7,3},{8,24},{9,13},... | collective-permute-start | bytes 393224 | tf_op jit(solution)/shard_map/ppermute | solution.py:96
  5.2 4.3 %collective-permute-start.2 = (bf16[512,128]{1,0:T(8,128)(2,1)}, bf16[512,128]{1,0:T(8,128)(2,1)S(1)}, u32[]{:S(2)}, u32[]{:S(2)}) collective-permute-start(bf16[512,128]{1,0:T(8,128)(2,1)} %refs_0_.1), channel_id=1, source_target_pairs={{0,24},{1,7},{2,26},{3,1},{4,28},{5,3},{6,30},{7,5},{8,0},{9,15},{... | collective-permute-start | bytes 393224 | tf_op jit(solution)/shard_map/ppermute | solution.py:96
  9.5 0.9 copy-start.7
  10.5 5.8 %collective-permute-start.6 = (bf16[4,512,128]{2,1,0:T(8,128)(2,1)S(1)}, bf16[4,512,128]{2,1,0:T(8,128)(2,1)S(1)}, u32[]{:S(2)}, u32[]{:S(2)}) collective-permute-start(bf16[4,512,128]{2,1,0:T(8,128)(2,1)S(1)} %stack4.2.refs_0_.refs_5_), channel_id=1, source_target_pairs={{0,1},{1,0},{2,3},{3,2},{4,5},{5,4},{6,7},{7,6},{8,9},{9,8},{10,11... | collective-permute-start | bytes 1572872 | tf_op jit(solution)/shard_map/ppermute | solution.py:96
  12.9 9.9 %collective-permute-start.5 = (bf16[4,512,128]{2,1,0:T(8,128)(2,1)S(1)}, bf16[4,512,128]{2,1,0:T(8,128)(2,1)S(1)}, u32[]{:S(2)}, u32[]{:S(2)}) collective-permute-start(bf16[4,512,128]{2,1,0:T(8,128)(2,1)S(1)} %stack4.2.refs_0_.refs_5_), channel_id=1, source_target_pairs={{0,4},{1,17},{2,6},{3,19},{4,0},{5,21},{6,2},{7,23},{8,12},{9,25},... | collective-permute-start | bytes 1572872 | tf_op jit(solution)/shard_map/ppermute | solution.py:96
  14.8 14.6 %collective-permute-start.4 = (bf16[4,512,128]{2,1,0:T(8,128)(2,1)S(1)}, bf16[4,512,128]{2,1,0:T(8,128)(2,1)S(1)}, u32[]{:S(2)}, u32[]{:S(2)}) collective-permute-start(bf16[4,512,128]{2,1,0:T(8,128)(2,1)S(1)} %stack4.2.refs_0_.refs_5_), channel_id=1, source_target_pairs={{0,6},{1,25},{2,0},{3,27},{4,2},{5,29},{6,4},{7,31},{8,14},{9,1},{... | collective-permute-start | bytes 1572872 | tf_op jit(solution)/shard_map/ppermute | solution.py:96
  15.9 14.7 %collective-permute-start.3 = (bf16[4,512,128]{2,1,0:T(8,128)(2,1)S(1)}, bf16[4,512,128]{2,1,0:T(8,128)(2,1)S(1)}, u32[]{:S(2)}, u32[]{:S(2)}) collective-permute-start(bf16[4,512,128]{2,1,0:T(8,128)(2,1)S(1)} %stack4.2.refs_0_.refs_5_), channel_id=1, source_target_pairs={{0,2},{1,9},{2,4},{3,11},{4,6},{5,13},{6,0},{7,15},{8,10},{9,17},{... | collective-permute-start | bytes 1572872 | tf_op jit(solution)/shard_map/ppermute | solution.py:96
  22.8 0.7 copy-start.3
  23.5 0.7 copy-start.8
  24.2 9.5 %copy-start.4 = (f32[4096]{0:T(1024)S(1)}, f32[4096]{0:T(1024)}, u32[]{:S(2)}) copy-start(f32[4096]{0:T(1024)} %param.13) | copy-start | bytes 49156
  24.2 9.5 %copy-start.9 = (s32[4,1]{0,1:T(1,128)S(1)}, s32[4,1]{0,1:T(1,128)}, u32[]{:S(2)}) copy-start(s32[4,1]{0,1:T(1,128)} %param.15) | copy-start | bytes 52
  29.5 3.4 %collective-permute-start.9 = (bf16[4,512,128]{2,1,0:T(8,128)(2,1)S(1)}, bf16[4,512,128]{2,1,0:T(8,128)(2,1)S(1)}, u32[]{:S(2)}, u32[]{:S(2)}) collective-permute-start(bf16[4,512,128]{2,1,0:T(8,128)(2,1)S(1)} %collective-permute-done.4.refs_1_), channel_id=1, source_target_pairs={{0,1},{1,0},{2,3},{3,2},{4,5},{5,4},{6,7},{7,6},{8,9},{9,8},{10,11... | collective-permute-start | bytes 1572872 | tf_op jit(solution)/shard_map/ppermute | solution.py:96
  30.6 2.3 %collective-permute-start.7 = (bf16[4,512,128]{2,1,0:T(8,128)(2,1)S(1)}, bf16[4,512,128]{2,1,0:T(8,128)(2,1)S(1)}, u32[]{:S(2)}, u32[]{:S(2)}) collective-permute-start(bf16[4,512,128]{2,1,0:T(8,128)(2,1)S(1)} %collective-permute-done.5.refs_1_.refs_6_), channel_id=1, source_target_pairs={{0,1},{1,0},{2,3},{3,2},{4,5},{5,4},{6,7},{7,6},{8,9},{9,8},{10,11... | collective-permute-start | bytes 1572872 | tf_op jit(solution)/shard_map/ppermute | solution.py:96
  30.7 2.9 %collective-permute-start.8 = (bf16[4,512,128]{2,1,0:T(8,128)(2,1)S(1)}, bf16[4,512,128]{2,1,0:T(8,128)(2,1)S(1)}, u32[]{:S(2)}, u32[]{:S(2)}) collective-permute-start(bf16[4,512,128]{2,1,0:T(8,128)(2,1)S(1)} %collective-permute-done.3.refs_0_), channel_id=1, source_target_pairs={{0,1},{1,0},{2,3},{3,2},{4,5},{5,4},{6,7},{7,6},{8,9},{9,8},{10,11... | collective-permute-start | bytes 1572872 | tf_op jit(solution)/shard_map/ppermute | solution.py:96
  43.0 0.7 copy-start.5
  43.7 4.6 %collective-permute-start.10 = (bf16[16,512,128]{2,1,0:T(8,128)(2,1)}, bf16[16,512,128]{2,1,0:T(8,128)(2,1)}, u32[]{:S(2)}, u32[]{:S(2)}) collective-permute-start(bf16[16,512,128]{2,1,0:T(8,128)(2,1)} %get-tuple-element.37), channel_id=1, source_target_pairs={{0,1},{1,0},{2,3},{3,2},{4,5},{5,4},{6,7},{7,6},{8,9},{9,8},{10,11... | collective-permute-start | bytes 6291464 | tf_op jit(solution)/shard_map/ppermute | solution.py:96
  44.3 12.0 %collective-permute-start.19 = (bf16[1040,128]{1,0:T(8,128)(2,1)S(1)}, bf16[1040,128]{1,0:T(8,128)(2,1)S(1)}, u32[]{:S(2)}, u32[]{:S(2)}) collective-permute-start(bf16[1040,128]{1,0:T(8,128)(2,1)S(1)} %turn.1.refs_3_.refs_8_), channel_id=1, source_target_pairs={{0,96},{32,0},{64,32},{96,64},{1,97},{33,1},{65,33},{97,65},{2,98}... | collective-permute-start | bytes 798728 | tf_op jit(solution)/shard_map/ppermute | solution.py:488
  48.3 11.3 %collective-permute-start.18 = (bf16[1040,128]{1,0:T(8,128)(2,1)S(1)}, bf16[1040,128]{1,0:T(8,128)(2,1)S(1)}, u32[]{:S(2)}, u32[]{:S(2)}) collective-permute-start(bf16[1040,128]{1,0:T(8,128)(2,1)S(1)} %turn.1.refs_3_.refs_8_), channel_id=1, source_target_pairs={{0,32},{32,64},{64,96},{96,0},{1,33},{33,65},{65,97},{97,1},{2,34}... | collective-permute-start | bytes 798728 | tf_op jit(solution)/shard_map/ppermute | solution.py:488
  48.3 12.0 %copy-start = (bf16[512,512]{1,0:T(8,128)(2,1)S(1)}, bf16[512,512]{1,0:T(8,128)(2,1)}, u32[]{:S(2)}) copy-start(bf16[512,512]{1,0:T(8,128)(2,1)} %constant.49.clone.refs_1_) | copy-start | bytes 1572868
  52.5 16.6 %collective-permute-start.12 = (bf16[4,512,128]{2,1,0:T(8,128)(2,1)}, bf16[4,512,128]{2,1,0:T(8,128)(2,1)S(1)}, u32[]{:S(2)}, u32[]{:S(2)}) collective-permute-start(bf16[4,512,128]{2,1,0:T(8,128)(2,1)} %get-tuple-element.39), channel_id=1, source_target_pairs={{0,2},{1,9},{2,4},{3,11},{4,6},{5,13},{6,0},{7,15},{8,10},{9,17},{... | collective-permute-start | bytes 1572872 | tf_op jit(solution)/shard_map/ppermute | solution.py:96
  53.2 15.9 %collective-permute-start.13 = (bf16[4,512,128]{2,1,0:T(8,128)(2,1)}, bf16[4,512,128]{2,1,0:T(8,128)(2,1)}, u32[]{:S(2)}, u32[]{:S(2)}) collective-permute-start(bf16[4,512,128]{2,1,0:T(8,128)(2,1)} %get-tuple-element.40), channel_id=1, source_target_pairs={{0,6},{1,25},{2,0},{3,27},{4,2},{5,29},{6,4},{7,31},{8,14},{9,1},{... | collective-permute-start | bytes 1572872 | tf_op jit(solution)/shard_map/ppermute | solution.py:96
  55.2 13.9 %collective-permute-start.11 = (bf16[4,512,128]{2,1,0:T(8,128)(2,1)}, bf16[4,512,128]{2,1,0:T(8,128)(2,1)}, u32[]{:S(2)}, u32[]{:S(2)}) collective-permute-start(bf16[4,512,128]{2,1,0:T(8,128)(2,1)} %get-tuple-element.38.refs_2_), channel_id=1, source_target_pairs={{0,4},{1,17},{2,6},{3,19},{4,0},{5,21},{6,2},{7,23},{8,12},{9,25},... | collective-permute-start | bytes 1572872 | tf_op jit(solution)/shard_map/ppermute | solution.py:96
  56.3 19.8 %collective-permute-start.17 = (bf16[1040,128]{1,0:T(8,128)(2,1)S(1)}, bf16[1040,128]{1,0:T(8,128)(2,1)}, u32[]{:S(2)}, u32[]{:S(2)}) collective-permute-start(bf16[1040,128]{1,0:T(8,128)(2,1)S(1)} %turn.1.refs_3_.refs_8_), channel_id=1, source_target_pairs={{0,64},{32,96},{64,0},{96,32},{1,65},{33,97},{65,1},{97,33},{2,66}... | collective-permute-start | bytes 798728 | tf_op jit(solution)/shard_map/ppermute | solution.py:488
  59.6 0.7 copy-start.1
  61.8 16.2 %all-to-all-start = ((bf16[32,4,4,256]{3,2,1,0:T(4,128)(2,1)}), bf16[32,4,4,256]{3,2,1,0:T(4,128)(2,1)S(1)}, u32[]{:S(2)}, u32[]{:S(2)}) async-start(bf16[32,4,4,256]{3,2,1,0:T(4,128)(2,1)} %pack.1.refs_9_), calls=%async_computation | async-start | bytes 524288 | tf_op jit(solution)/shard_map/all_to_all | solution.py:493
  71.8 6.2 %collective-permute-start.15 = (bf16[512,128]{1,0:T(8,128)(2,1)}, bf16[512,128]{1,0:T(8,128)(2,1)}, u32[]{:S(2)}, u32[]{:S(2)}) collective-permute-start(bf16[512,128]{1,0:T(8,128)(2,1)} %get-tuple-element.42), channel_id=1, source_target_pairs={{0,8},{1,3},{2,10},{3,5},{4,12},{5,7},{6,14},{7,1},{8,16},{9,11},{... | collective-permute-start | bytes 393224 | tf_op jit(solution)/shard_map/ppermute | solution.py:96
  73.2 4.8 %collective-permute-start.16 = (bf16[512,128]{1,0:T(8,128)(2,1)}, bf16[512,128]{1,0:T(8,128)(2,1)}, u32[]{:S(2)}, u32[]{:S(2)}) collective-permute-start(bf16[512,128]{1,0:T(8,128)(2,1)} %get-tuple-element.43), channel_id=1, source_target_pairs={{0,24},{1,7},{2,26},{3,1},{4,28},{5,3},{6,30},{7,5},{8,0},{9,15},{... | collective-permute-start | bytes 393224 | tf_op jit(solution)/shard_map/ppermute | solution.py:96
  74.5 5.6 %collective-permute-start.14 = (bf16[512,128]{1,0:T(8,128)(2,1)}, bf16[512,128]{1,0:T(8,128)(2,1)}, u32[]{:S(2)}, u32[]{:S(2)}) collective-permute-start(bf16[512,128]{1,0:T(8,128)(2,1)} %get-tuple-element.41.refs_10_), channel_id=1, source_target_pairs={{0,16},{1,5},{2,18},{3,7},{4,20},{5,1},{6,22},{7,3},{8,24},{9,13},... | collective-permute-start | bytes 393224 | tf_op jit(solution)/shard_map/ppermute | solution.py:96
  80.1 0.9 copy-start.6
  81.0 37.0 %copy-start.2 = (bf16[1040,128]{1,0:T(8,128)(2,1)S(1)}, bf16[1040,128]{1,0:T(8,128)(2,1)}, u32[]{:S(2)}) copy-start(bf16[1040,128]{1,0:T(8,128)(2,1)} %copy-done.1) | copy-start | bytes 798724
  82.9 3.9 %collective-permute-start.23 = (bf16[512,128]{1,0:T(8,128)(2,1)S(1)}, bf16[512,128]{1,0:T(8,128)(2,1)S(1)}, u32[]{:S(2)}, u32[]{:S(2)}) collective-permute-start(bf16[512,128]{1,0:T(8,128)(2,1)S(1)} %get-tuple-element.45), channel_id=1, source_target_pairs={{0,24},{1,7},{2,26},{3,1},{4,28},{5,3},{6,30},{7,5},{8,32},{9,47},... | collective-permute-start | bytes 393224 | tf_op jit(solution)/shard_map/ppermute | solution.py:514
  84.4 6.4 %collective-permute-start.22 = (bf16[512,128]{1,0:T(8,128)(2,1)S(1)}, bf16[512,128]{1,0:T(8,128)(2,1)S(1)}, u32[]{:S(2)}, u32[]{:S(2)}) collective-permute-start(bf16[512,128]{1,0:T(8,128)(2,1)S(1)} %get-tuple-element.45), channel_id=1, source_target_pairs={{0,8},{1,3},{2,10},{3,5},{4,12},{5,7},{6,14},{7,1},{8,48},{9,43},{... | collective-permute-start | bytes 393224 | tf_op jit(solution)/shard_map/ppermute | solution.py:514
  84.5 6.4 %collective-permute-start.21 = (bf16[512,128]{1,0:T(8,128)(2,1)S(1)}, bf16[512,128]{1,0:T(8,128)(2,1)S(1)}, u32[]{:S(2)}, u32[]{:S(2)}) collective-permute-start(bf16[512,128]{1,0:T(8,128)(2,1)S(1)} %get-tuple-element.45), channel_id=1, source_target_pairs={{0,16},{1,5},{2,18},{3,7},{4,20},{5,1},{6,22},{7,3},{8,56},{9,45},... | collective-permute-start | bytes 393224 | tf_op jit(solution)/shard_map/ppermute | solution.py:514
  86.1 4.7 %collective-permute-start.20 = (bf16[512,128]{1,0:T(8,128)(2,1)S(1)}, bf16[512,128]{1,0:T(8,128)(2,1)S(1)}, u32[]{:S(2)}, u32[]{:S(2)}) collective-permute-start(bf16[512,128]{1,0:T(8,128)(2,1)S(1)} %get-tuple-element.45), channel_id=1, source_target_pairs={{0,0},{1,1},{2,2},{3,3},{4,4},{5,5},{6,6},{7,7},{8,40},{9,41},{10,... | collective-permute-start | bytes 393224 | tf_op jit(solution)/shard_map/ppermute | solution.py:514
  90.9 17.3 %collective-permute-start.25 = (bf16[4,512,128]{2,1,0:T(8,128)(2,1)S(1)}, bf16[4,512,128]{2,1,0:T(8,128)(2,1)S(1)}, u32[]{:S(2)}, u32[]{:S(2)}) collective-permute-start(bf16[4,512,128]{2,1,0:T(8,128)(2,1)S(1)} %stack4.3.refs_0_), channel_id=1, source_target_pairs={{0,4},{1,17},{2,6},{3,19},{4,0},{5,21},{6,2},{7,23},{8,12},{9,25},... | collective-permute-start | bytes 1572872 | tf_op jit(solution)/shard_map/ppermute | solution.py:96
  101.3 12.5 %collective-permute-start.27 = (bf16[4,512,128]{2,1,0:T(8,128)(2,1)S(1)}, bf16[4,512,128]{2,1,0:T(8,128)(2,1)S(1)}, u32[]{:S(2)}, u32[]{:S(2)}) collective-permute-start(bf16[4,512,128]{2,1,0:T(8,128)(2,1)S(1)} %stack4.3.refs_0_), channel_id=1, source_target_pairs={{0,2},{1,9},{2,4},{3,11},{4,6},{5,13},{6,0},{7,15},{8,10},{9,17},{... | collective-permute-start | bytes 1572872 | tf_op jit(solution)/shard_map/ppermute | solution.py:96
  101.3 14.5 %collective-permute-start.24 = (bf16[4,512,128]{2,1,0:T(8,128)(2,1)S(1)}, bf16[4,512,128]{2,1,0:T(8,128)(2,1)S(1)}, u32[]{:S(2)}, u32[]{:S(2)}) collective-permute-start(bf16[4,512,128]{2,1,0:T(8,128)(2,1)S(1)} %stack4.3.refs_0_), channel_id=1, source_target_pairs={{0,6},{1,25},{2,0},{3,27},{4,2},{5,29},{6,4},{7,31},{8,14},{9,1},{... | collective-permute-start | bytes 1572872 | tf_op jit(solution)/shard_map/ppermute | solution.py:96
  108.2 7.6 %collective-permute-start.26 = (bf16[512,128]{1,0:T(8,128)(2,1)S(1)}, bf16[512,128]{1,0:T(8,128)(2,1)S(1)}, u32[]{:S(2)}, u32[]{:S(2)}) collective-permute-start(bf16[512,128]{1,0:T(8,128)(2,1)S(1)} %get-tuple-element.47.refs_4_), channel_id=1, source_target_pairs={{0,0},{1,1},{2,2},{3,3},{4,4},{5,5},{6,6},{7,7},{8,8},{9,9},{10,10... | collective-permute-start | bytes 393224 | tf_op jit(solution)/shard_map/ppermute | solution.py:520
  108.8 7.8 %collective-permute-start.28 = (bf16[4,512,128]{2,1,0:T(8,128)(2,1)S(1)}, bf16[4,512,128]{2,1,0:T(8,128)(2,1)S(1)}, u32[]{:S(2)}, u32[]{:S(2)}) collective-permute-start(bf16[4,512,128]{2,1,0:T(8,128)(2,1)S(1)} %stack4.3.refs_0_), channel_id=1, source_target_pairs={{0,1},{1,0},{2,3},{3,2},{4,5},{5,4},{6,7},{7,6},{8,9},{9,8},{10,11... | collective-permute-start | bytes 1572872 | tf_op jit(solution)/shard_map/ppermute | solution.py:96
  111.0 6.3 %collective-permute-start.29 = (bf16[4,512,128]{2,1,0:T(8,128)(2,1)S(1)}, bf16[4,512,128]{2,1,0:T(8,128)(2,1)S(1)}, u32[]{:S(2)}, u32[]{:S(2)}) collective-permute-start(bf16[4,512,128]{2,1,0:T(8,128)(2,1)S(1)} %collective-permute-done.25.refs_1_), channel_id=1, source_target_pairs={{0,1},{1,0},{2,3},{3,2},{4,5},{5,4},{6,7},{7,6},{8,9},{9,8},{10,11... | collective-permute-start | bytes 1572872 | tf_op jit(solution)/shard_map/ppermute | solution.py:96
  113.7 3.5 %collective-permute-start.30 = (bf16[4,512,128]{2,1,0:T(8,128)(2,1)S(1)}, bf16[4,512,128]{2,1,0:T(8,128)(2,1)S(1)}, u32[]{:S(2)}, u32[]{:S(2)}) collective-permute-start(bf16[4,512,128]{2,1,0:T(8,128)(2,1)S(1)} %collective-permute-done.27.refs_2_), channel_id=1, source_target_pairs={{0,1},{1,0},{2,3},{3,2},{4,5},{5,4},{6,7},{7,6},{8,9},{9,8},{10,11... | collective-permute-start | bytes 1572872 | tf_op jit(solution)/shard_map/ppermute | solution.py:96
  115.7 2.3 %collective-permute-start.31 = (bf16[4,512,128]{2,1,0:T(8,128)(2,1)S(1)}, bf16[4,512,128]{2,1,0:T(8,128)(2,1)S(1)}, u32[]{:S(2)}, u32[]{:S(2)}) collective-permute-start(bf16[4,512,128]{2,1,0:T(8,128)(2,1)S(1)} %collective-permute-done.24.refs_3_), channel_id=1, source_target_pairs={{0,1},{1,0},{2,3},{3,2},{4,5},{5,4},{6,7},{7,6},{8,9},{9,8},{10,11... | collective-permute-start | bytes 1572872 | tf_op jit(solution)/shard_map/ppermute | solution.py:96

commit v4 on v3

--- a/solution.py
+++ b/solution.py
@@ -333,7 +333,7 @@
             out_specs=[pl.BlockSpec((1, rows, PIECE), lambda e, p: (e, 0, 0))] * 3,
         ),
         out_shape=[jax.ShapeDtypeStruct((4, rows, PIECE), BF)] * 3,
-        compiler_params=LARGE,
+        compiler_params=SMALL,
         name="first_sum",
     )(places, *([mine] * 3), *([got] * 3), *after)
 
@@ -350,7 +350,7 @@
 
 def second_sum(places, mine, got, far, after):
     rows = mine.shape[1]
-    half = rows // 2
+    half = rows
     specs = [
         pl.BlockSpec((1, half, PIECE), lambda i, p, e=e: (p[PLACES[1] + e], i, 0))
         for e in range(1, 4)
@@ -359,7 +359,7 @@
         second_sum_kernel,
         grid_spec=pltpu.PrefetchScalarGridSpec(
             num_scalar_prefetch=1,
-            grid=(2,),
+            grid=(1,),
             in_specs=specs
             + specs
             + [pl.BlockSpec((4, half, PIECE), lambda i, p: (0, i, 0))] * 3

time: 128 us -> 128 us (level)
  transfers between devices with their start and end apart: 33 -> 33, of which waited for: 12 -> 13; matrix products, arithmetic and copies ran while one was open for 2% -> 2% of each run, Pallas kernels for 11% -> 11%
where the time goes in v4:
time: 128 us; the launch traced here: 126 us
  starting transfers between devices  58.7 us (46%)
  Pallas kernels  32.8 us (26%)
  waiting for transfers between devices  25.5 us (20%)
  local copies, waits for them, and re-layouts  8.26 us (6%)
    ppermute x24, starting transfers between devices, send(): return lax.ppermute(value, 'lat', pairs)  39.3 us
    ppermute x24, waiting for transfers between devices, send(): return lax.ppermute(value, 'lat', pairs)  20.4 us
    pallas_call x1, Pallas kernels, encode(): pl.pallas_call(encode_kernel, grid_spec=pltpu.PrefetchScalarGridSpec(num_...  9.42 us
    ppermute x3, starting transfers between devices, body(): lax.ppermute(codes_t, 'tok', [(z, (z + s) % SIDE) for z in range(SIDE)])  7.66 us
    pallas_call x1, Pallas kernels, grad(): pl.pallas_call(grad_kernel, grid_spec=pltpu.PrefetchScalarGridSpec(num_sc...  7.43 us
    all_to_all x1, starting transfers between devices, body(): lax.all_to_all(tile_send, 'lat', split_axis=0, concat_axis=0, tiled=True)  7.18 us
    unnamed x22, local copies, waits for them, and re-layouts  6.04 us
    pallas_call x1, Pallas kernels, begin(): pl.pallas_call(begin_kernel, grid_spec=pltpu.PrefetchScalarGridSpec(num_s...  5.41 us
  transfers between devices with their start and end apart: 33, of which 13 were waited for; matrix products, arithmetic and copies ran while one was open for 2% of the time, Pallas kernels for 11%

profile of v4, /device:TPU:1, one launch (start us, length us, event | category | flops | bytes accessed | tf_op | source)
XLA Modules:
  0.0 126.1 jit_solution(1639331780683697366)
XLA Ops:
  0.6 2.1 %collective-permute-start.1 = (bf16[512,128]{1,0:T(8,128)(2,1)}, bf16[512,128]{1,0:T(8,128)(2,1)S(1)}, u32[]{:S(2)}, u32[]{:S(2)}) collective-permute-start(bf16[512,128]{1,0:T(8,128)(2,1)} %refs_0_.1), channel_id=1, source_target_pairs={{0,8},{1,3},{2,10},{3,5},{4,12},{5,7},{6,14},{7,1},{8,16},{9,11},{... | collective-permute-start | bytes 393224 | tf_op jit(solution)/shard_map/ppermute | solution.py:96
  2.7 2.5 %collective-permute-start = (bf16[512,128]{1,0:T(8,128)(2,1)}, bf16[512,128]{1,0:T(8,128)(2,1)S(1)}, u32[]{:S(2)}, u32[]{:S(2)}) collective-permute-start(bf16[512,128]{1,0:T(8,128)(2,1)} %refs_0_.1), channel_id=1, source_target_pairs={{0,16},{1,5},{2,18},{3,7},{4,20},{5,1},{6,22},{7,3},{8,24},{9,13},... | collective-permute-start | bytes 393224 | tf_op jit(solution)/shard_map/ppermute | solution.py:96
  5.2 1.2 collective-permute-start.2
  6.3 0.8 reshape.48.refs_4_.refs_12_
  7.1 0.7 dynamic-slice_bitcast_fusion.refs_5_.places.where.table
  7.8 1.6 %collective-permute-done.refs_1_ = bf16[512,128]{1,0:T(8,128)(2,1)S(1)} collective-permute-done((bf16[512,128]{1,0:T(8,128)(2,1)}, bf16[512,128]{1,0:T(8,128)(2,1)S(1)}, u32[]{:S(2)}, u32[]{:S(2)}) %collective-permute-start) | collective-permute-done | bytes 131104 | tf_op jit(solution)/shard_map/ppermute | solution.py:96
  9.5 0.9 copy-done.7
  10.5 2.4 %collective-permute-start.6 = (bf16[4,512,128]{2,1,0:T(8,128)(2,1)S(1)}, bf16[4,512,128]{2,1,0:T(8,128)(2,1)S(1)}, u32[]{:S(2)}, u32[]{:S(2)}) collective-permute-start(bf16[4,512,128]{2,1,0:T(8,128)(2,1)S(1)} %stack4.2.refs_0_.refs_5_), channel_id=1, source_target_pairs={{0,1},{1,0},{2,3},{3,2},{4,5},{5,4},{6,7},{7,6},{8,9},{9,8},{10,11... | collective-permute-start | bytes 1572872 | tf_op jit(solution)/shard_map/ppermute | solution.py:96
  12.9 2.0 %collective-permute-start.5 = (bf16[4,512,128]{2,1,0:T(8,128)(2,1)S(1)}, bf16[4,512,128]{2,1,0:T(8,128)(2,1)S(1)}, u32[]{:S(2)}, u32[]{:S(2)}) collective-permute-start(bf16[4,512,128]{2,1,0:T(8,128)(2,1)S(1)} %stack4.2.refs_0_.refs_5_), channel_id=1, source_target_pairs={{0,4},{1,17},{2,6},{3,19},{4,0},{5,21},{6,2},{7,23},{8,12},{9,25},... | collective-permute-start | bytes 1572872 | tf_op jit(solution)/shard_map/ppermute | solution.py:96
  14.8 1.1 collective-permute-start.4
  15.9 0.4 collective-permute-start.3
  16.3 6.4 %collective-permute-done.5.refs_1_.refs_6_ = bf16[4,512,128]{2,1,0:T(8,128)(2,1)S(1)} collective-permute-done((bf16[4,512,128]{2,1,0:T(8,128)(2,1)S(1)}, bf16[4,512,128]{2,1,0:T(8,128)(2,1)S(1)}, u32[]{:S(2)}, u32[]{:S(2)}) %collective-permute-start.5) | collective-permute-done | bytes 524320 | tf_op jit(solution)/shard_map/ppermute | solution.py:96
  22.8 0.7 copy-done.3
  23.5 0.7 copy-done.8
  24.2 5.4 %begin.1.refs_7_ = f32[512,256]{1,0:T(8,128)S(1)} custom-call(s32[4,4]{1,0:T(4,128)S(1)} %bitcast.18, s32[115]{0:T(128)S(1)} %dynamic-slice_bitcast_fusion.refs_5_.places.where.table, bf16[4,512,128]{2,1,0:T(8,128)(2,1)S(1)} %stack4.2.refs_0_.refs_5_, bf16[4,512,128]{2,1,0:T(8,128)(2,1)S(1)} %collective-permute-done.5.refs_1_.refs_6_, ...), custom_call_target="tpu_custom_call" | custom-call | flops 1000000000 | bytes 50331648 | tf_op jit(solution)/shard_map/begin/pallas_call | solution.py:163
  29.6 1.1 collective-permute-start.9
  30.7 0.1 collective-permute-start.7
  30.8 0.4 collective-permute-start.8
  31.2 1.8 %collective-permute-done.7.refs_2_ = bf16[4,512,128]{2,1,0:T(8,128)(2,1)S(1)} collective-permute-done((bf16[4,512,128]{2,1,0:T(8,128)(2,1)S(1)}, bf16[4,512,128]{2,1,0:T(8,128)(2,1)S(1)}, u32[]{:S(2)}, u32[]{:S(2)}) %collective-permute-start.7) | collective-permute-done | bytes 524320 | tf_op jit(solution)/shard_map/ppermute | solution.py:96
  33.0 0.7 collective-permute-done.8.refs_3_
  33.8 9.4 %encode.1 = (bf16[512,256]{1,0:T(8,128)(2,1)S(1)}, bf16[16,512,128]{2,1,0:T(8,128)(2,1)S(1)}, bf16[16,512,128]{2,1,0:T(8,128)(2,1)}, bf16[512,128]{1,0:T(8,128)(2,1)S(1)}) custom-call(s32[4,4]{1,0:T(4,128)S(1)} %bitcast.19, s32[4]{0:T(128)S(1)} %bitcast.20, s32[115]{0:T(128)S(1)} %dynamic-slice_bitcast_fusion.refs_5_.places.where.table, ...), custom_call_target="tpu_custom_call" | custom-call | tf_op jit(solution)/shard_map/encode/pallas_call | solution.py:230
  43.2 0.7 copy-done.5
  43.9 0.4 collective-permute-start.10
  44.2 0.1 convert_element_type.15
  44.3 0.1 turn.1.refs_3_.refs_8_
  44.5 3.8 %collective-permute-start.19 = (bf16[1040,128]{1,0:T(8,128)(2,1)S(1)}, bf16[1040,128]{1,0:T(8,128)(2,1)S(1)}, u32[]{:S(2)}, u32[]{:S(2)}) collective-permute-start(bf16[1040,128]{1,0:T(8,128)(2,1)S(1)} %turn.1.refs_3_.refs_8_), channel_id=1, source_target_pairs={{0,96},{32,0},{64,32},{96,64},{1,97},{33,1},{65,33},{97,65},{2,98}... | collective-permute-start | bytes 798728 | tf_op jit(solution)/shard_map/ppermute | solution.py:488
  48.3 0.1 collective-permute-done.10.refs_3_.refs_4_.refs_5_.refs_1_
  48.4 4.2 %first_sum.1 = (bf16[4,512,128]{2,1,0:T(8,128)(2,1)}, bf16[4,512,128]{2,1,0:T(8,128)(2,1)}, bf16[4,512,128]{2,1,0:T(8,128)(2,1)}) custom-call(s32[115]{0:T(128)S(1)} %dynamic-slice_bitcast_fusion.refs_5_.places.where.table, bf16[16,512,128]{2,1,0:T(8,128)(2,1)S(1)} %get-tuple-element.36.refs_0_.refs_1_.refs_2_, ...), custom_call_target="tpu_custom_call" | custom-call | tf_op jit(solution)/shard_map/first_sum/pallas_call | solution.py:327
  52.5 0.9 collective-permute-start.12
  53.4 1.8 %collective-permute-start.13 = (bf16[4,512,128]{2,1,0:T(8,128)(2,1)}, bf16[4,512,128]{2,1,0:T(8,128)(2,1)}, u32[]{:S(2)}, u32[]{:S(2)}) collective-permute-start(bf16[4,512,128]{2,1,0:T(8,128)(2,1)} %get-tuple-element.40), channel_id=1, source_target_pairs={{0,6},{1,25},{2,0},{3,27},{4,2},{5,29},{6,4},{7,31},{8,14},{9,1},{... | collective-permute-start | bytes 1572872 | tf_op jit(solution)/shard_map/ppermute | solution.py:96
  55.2 0.8 collective-permute-start.11
  56.0 3.9 %collective-permute-start.17 = (bf16[1040,128]{1,0:T(8,128)(2,1)S(1)}, bf16[1040,128]{1,0:T(8,128)(2,1)}, u32[]{:S(2)}, u32[]{:S(2)}) collective-permute-start(bf16[1040,128]{1,0:T(8,128)(2,1)S(1)} %turn.1.refs_3_.refs_8_), channel_id=1, source_target_pairs={{0,64},{32,96},{64,0},{96,32},{1,65},{33,97},{65,1},{97,33},{2,66}... | collective-permute-start | bytes 798728 | tf_op jit(solution)/shard_map/ppermute | solution.py:488
  59.9 0.7 copy-done.1
  60.6 1.5 %pack.1.refs_9_ = bf16[32,4,4,256]{3,2,1,0:T(4,128)(2,1)} custom-call(bf16[512,256]{1,0:T(8,128)(2,1)S(1)} %get-tuple-element.35.refs_0_, bf16[512,512]{1,0:T(8,128)(2,1)S(1)} %copy-done, bf16[4,512,128]{2,1,0:T(8,128)(2,1)} %get-tuple-element.38.refs_2_, bf16[1040,128]{1,0:T(8,128)(2,1)S(1)} %turn.1.refs_3_.refs_8_), custom_call_target="tpu_custom_call" | custom-call | tf_op jit(solution)/shard_map/pack/pallas_call | solution.py:305
  62.1 7.2 %all-to-all-start = ((bf16[32,4,4,256]{3,2,1,0:T(4,128)(2,1)}), bf16[32,4,4,256]{3,2,1,0:T(4,128)(2,1)S(1)}, u32[]{:S(2)}, u32[]{:S(2)}) async-start(bf16[32,4,4,256]{3,2,1,0:T(4,128)(2,1)} %pack.1.refs_9_), calls=%async_computation | async-start | bytes 524288 | tf_op jit(solution)/shard_map/all_to_all | solution.py:493
  69.4 2.7 %second_sum.1 = (bf16[512,128]{1,0:T(8,128)(2,1)}, bf16[512,128]{1,0:T(8,128)(2,1)}, bf16[512,128]{1,0:T(8,128)(2,1)}) custom-call(s32[115]{0:T(128)S(1)} %dynamic-slice_bitcast_fusion.refs_5_.places.where.table, bf16[16,512,128]{2,1,0:T(8,128)(2,1)S(1)} %get-tuple-element.36.refs_0_.refs_1_.refs_2_, ...), custom_call_target="tpu_custom_call" | custom-call | tf_op jit(solution)/shard_map/second_sum/pallas_call | solution.py:358
  72.1 1.4 %collective-permute-start.15 = (bf16[512,128]{1,0:T(8,128)(2,1)}, bf16[512,128]{1,0:T(8,128)(2,1)}, u32[]{:S(2)}, u32[]{:S(2)}) collective-permute-start(bf16[512,128]{1,0:T(8,128)(2,1)} %get-tuple-element.42), channel_id=1, source_target_pairs={{0,8},{1,3},{2,10},{3,5},{4,12},{5,7},{6,14},{7,1},{8,16},{9,11},{... | collective-permute-start | bytes 393224 | tf_op jit(solution)/shard_map/ppermute | solution.py:96
  73.5 1.3 %collective-permute-start.16 = (bf16[512,128]{1,0:T(8,128)(2,1)}, bf16[512,128]{1,0:T(8,128)(2,1)}, u32[]{:S(2)}, u32[]{:S(2)}) collective-permute-start(bf16[512,128]{1,0:T(8,128)(2,1)} %get-tuple-element.43), channel_id=1, source_target_pairs={{0,24},{1,7},{2,26},{3,1},{4,28},{5,3},{6,30},{7,5},{8,0},{9,15},{... | collective-permute-start | bytes 393224 | tf_op jit(solution)/shard_map/ppermute | solution.py:96
  74.8 1.7 %collective-permute-start.14 = (bf16[512,128]{1,0:T(8,128)(2,1)}, bf16[512,128]{1,0:T(8,128)(2,1)}, u32[]{:S(2)}, u32[]{:S(2)}) collective-permute-start(bf16[512,128]{1,0:T(8,128)(2,1)} %get-tuple-element.41.refs_10_), channel_id=1, source_target_pairs={{0,16},{1,5},{2,18},{3,7},{4,20},{5,1},{6,22},{7,3},{8,24},{9,13},... | collective-permute-start | bytes 393224 | tf_op jit(solution)/shard_map/ppermute | solution.py:96
  76.5 0.7 slice_bitcast_fusion.2
  77.1 0.1 maximum_convert_fusion.refs_11_.ids
  77.2 1.0 all-to-all-done.refs_12_
  78.2 2.2 %collective-permute-done.14.refs_5_ = bf16[512,128]{1,0:T(8,128)(2,1)} collective-permute-done((bf16[512,128]{1,0:T(8,128)(2,1)}, bf16[512,128]{1,0:T(8,128)(2,1)}, u32[]{:S(2)}, u32[]{:S(2)}) %collective-permute-start.14) | collective-permute-done | bytes 131104 | tf_op jit(solution)/shard_map/ppermute | solution.py:96
  80.4 0.9 copy-done.6
  81.3 1.9 %error.1 = (bf16[512,128]{1,0:T(8,128)(2,1)S(1)}, bf16[512,128]{1,0:T(8,128)(2,1)S(1)}) custom-call(s32[115]{0:T(128)S(1)} %dynamic-slice_bitcast_fusion.refs_5_.places.where.table, bf16[16,512,128]{2,1,0:T(8,128)(2,1)S(1)} %get-tuple-element.36.refs_0_.refs_1_.refs_2_, bf16[16,512,128]{2,1,0:T(8,128)(2,1)} %collective-permute-done.10.refs_3_.refs_4_.refs_5_.refs_1_, ...), custom_call_target="tpu_custom_call" | custom-call | tf_op jit(solution)/shard_map/error/pallas_call | solution.py:392
  83.2 1.5 %collective-permute-start.23 = (bf16[512,128]{1,0:T(8,128)(2,1)S(1)}, bf16[512,128]{1,0:T(8,128)(2,1)S(1)}, u32[]{:S(2)}, u32[]{:S(2)}) collective-permute-start(bf16[512,128]{1,0:T(8,128)(2,1)S(1)} %get-tuple-element.45), channel_id=1, source_target_pairs={{0,24},{1,7},{2,26},{3,1},{4,28},{5,3},{6,30},{7,5},{8,32},{9,47},... | collective-permute-start | bytes 393224 | tf_op jit(solution)/shard_map/ppermute | solution.py:514
  84.7 0.1 collective-permute-start.22
  84.8 1.7 %collective-permute-start.21 = (bf16[512,128]{1,0:T(8,128)(2,1)S(1)}, bf16[512,128]{1,0:T(8,128)(2,1)S(1)}, u32[]{:S(2)}, u32[]{:S(2)}) collective-permute-start(bf16[512,128]{1,0:T(8,128)(2,1)S(1)} %get-tuple-element.45), channel_id=1, source_target_pairs={{0,16},{1,5},{2,18},{3,7},{4,20},{5,1},{6,22},{7,3},{8,56},{9,45},... | collective-permute-start | bytes 393224 | tf_op jit(solution)/shard_map/ppermute | solution.py:514
  86.5 0.7 collective-permute-start.20
  87.1 4.0 %collective-permute-done.22.refs_2_ = bf16[512,128]{1,0:T(8,128)(2,1)S(1)} collective-permute-done((bf16[512,128]{1,0:T(8,128)(2,1)S(1)}, bf16[512,128]{1,0:T(8,128)(2,1)S(1)}, u32[]{:S(2)}, u32[]{:S(2)}) %collective-permute-start.22) | collective-permute-done | bytes 131104 | tf_op jit(solution)/shard_map/ppermute | solution.py:514
  91.2 9.2 %collective-permute-start.25 = (bf16[4,512,128]{2,1,0:T(8,128)(2,1)S(1)}, bf16[4,512,128]{2,1,0:T(8,128)(2,1)S(1)}, u32[]{:S(2)}, u32[]{:S(2)}) collective-permute-start(bf16[4,512,128]{2,1,0:T(8,128)(2,1)S(1)} %stack4.3.refs_0_), channel_id=1, source_target_pairs={{0,4},{1,17},{2,6},{3,19},{4,0},{5,21},{6,2},{7,23},{8,12},{9,25},... | collective-permute-start | bytes 1572872 | tf_op jit(solution)/shard_map/ppermute | solution.py:96
  100.4 2.7 %collective-permute-start.24 = (bf16[4,512,128]{2,1,0:T(8,128)(2,1)S(1)}, bf16[4,512,128]{2,1,0:T(8,128)(2,1)S(1)}, u32[]{:S(2)}, u32[]{:S(2)}) collective-permute-start(bf16[4,512,128]{2,1,0:T(8,128)(2,1)S(1)} %stack4.3.refs_0_), channel_id=1, source_target_pairs={{0,6},{1,25},{2,0},{3,27},{4,2},{5,29},{6,4},{7,31},{8,14},{9,1},{... | collective-permute-start | bytes 1572872 | tf_op jit(solution)/shard_map/ppermute | solution.py:96
  103.1 4.2 %collective-permute-done.25.refs_1_ = bf16[4,512,128]{2,1,0:T(8,128)(2,1)S(1)} collective-permute-done((bf16[4,512,128]{2,1,0:T(8,128)(2,1)S(1)}, bf16[4,512,128]{2,1,0:T(8,128)(2,1)S(1)}, u32[]{:S(2)}, u32[]{:S(2)}) %collective-permute-start.25) | collective-permute-done | bytes 524320 | tf_op jit(solution)/shard_map/ppermute | solution.py:96
  107.3 0.7 collective-permute-start.26
  108.0 3.0 %collective-permute-start.28 = (bf16[4,512,128]{2,1,0:T(8,128)(2,1)S(1)}, bf16[4,512,128]{2,1,0:T(8,128)(2,1)S(1)}, u32[]{:S(2)}, u32[]{:S(2)}) collective-permute-start(bf16[4,512,128]{2,1,0:T(8,128)(2,1)S(1)} %stack4.3.refs_0_), channel_id=1, source_target_pairs={{0,1},{1,0},{2,3},{3,2},{4,5},{5,4},{6,7},{7,6},{8,9},{9,8},{10,11... | collective-permute-start | bytes 1572872 | tf_op jit(solution)/shard_map/ppermute | solution.py:96
  111.0 0.1 collective-permute-start.29
  111.1 1.8 %collective-permute-done.27.refs_2_ = bf16[4,512,128]{2,1,0:T(8,128)(2,1)S(1)} collective-permute-done((bf16[4,512,128]{2,1,0:T(8,128)(2,1)S(1)}, bf16[4,512,128]{2,1,0:T(8,128)(2,1)S(1)}, u32[]{:S(2)}, u32[]{:S(2)}) %collective-permute-start.27) | collective-permute-done | bytes 524320 | tf_op jit(solution)/shard_map/ppermute | solution.py:96
  112.9 2.9 %collective-permute-start.30 = (bf16[4,512,128]{2,1,0:T(8,128)(2,1)S(1)}, bf16[4,512,128]{2,1,0:T(8,128)(2,1)S(1)}, u32[]{:S(2)}, u32[]{:S(2)}) collective-permute-start(bf16[4,512,128]{2,1,0:T(8,128)(2,1)S(1)} %collective-permute-done.27.refs_2_), channel_id=1, source_target_pairs={{0,1},{1,0},{2,3},{3,2},{4,5},{5,4},{6,7},{7,6},{8,9},{9,8},{10,11... | collective-permute-start | bytes 1572872 | tf_op jit(solution)/shard_map/ppermute | solution.py:96
  115.7 0.1 collective-permute-start.31
  115.8 0.8 copy.11
  116.6 0.6 collective-permute-done.30.refs_6_
  117.3 0.7 collective-permute-done.31.refs_7_
  118.0 7.4 %grad.1 = f32[2048,1024]{1,0:T(8,128)} custom-call(s32[64]{0:T(128)S(1)} %maximum_convert_fusion.refs_11_.ids, s32[115]{0:T(128)S(1)} %dynamic-slice_bitcast_fusion.refs_5_.places.where.table, bf16[4,512,128]{2,1,0:T(8,128)(2,1)S(1)} %stack4.3.refs_0_, bf16[4,512,128]{2,1,0:T(8,128)(2,1)S(1)} %collective-permute-done.25.refs_1_, ...), custom_call_target="tpu_custom_call" | custom-call | flops 1000000000 | bytes 14680064 | tf_op jit(solution)/shard_map/grad/pallas_call | solution.py:442
  125.4 0.7 copy.13
  (44 shorter events, 0.3 us)
Async XLA Ops:
  0.6 7.2 %collective-permute-start.1 = (bf16[512,128]{1,0:T(8,128)(2,1)}, bf16[512,128]{1,0:T(8,128)(2,1)S(1)}, u32[]{:S(2)}, u32[]{:S(2)}) collective-permute-start(bf16[512,128]{1,0:T(8,128)(2,1)} %refs_0_.1), channel_id=1, source_target_pairs={{0,8},{1,3},{2,10},{3,5},{4,12},{5,7},{6,14},{7,1},{8,16},{9,11},{... | collective-permute-start | bytes 393224 | tf_op jit(solution)/shard_map/ppermute | solution.py:96
  2.7 6.7 %collective-permute-start = (bf16[512,128]{1,0:T(8,128)(2,1)}, bf16[512,128]{1,0:T(8,128)(2,1)S(1)}, u32[]{:S(2)}, u32[]{:S(2)}) collective-permute-start(bf16[512,128]{1,0:T(8,128)(2,1)} %refs_0_.1), channel_id=1, source_target_pairs={{0,16},{1,5},{2,18},{3,7},{4,20},{5,1},{6,22},{7,3},{8,24},{9,13},... | collective-permute-start | bytes 393224 | tf_op jit(solution)/shard_map/ppermute | solution.py:96
  5.2 4.3 %collective-permute-start.2 = (bf16[512,128]{1,0:T(8,128)(2,1)}, bf16[512,128]{1,0:T(8,128)(2,1)S(1)}, u32[]{:S(2)}, u32[]{:S(2)}) collective-permute-start(bf16[512,128]{1,0:T(8,128)(2,1)} %refs_0_.1), channel_id=1, source_target_pairs={{0,24},{1,7},{2,26},{3,1},{4,28},{5,3},{6,30},{7,5},{8,0},{9,15},{... | collective-permute-start | bytes 393224 | tf_op jit(solution)/shard_map/ppermute | solution.py:96
  9.5 0.9 copy-start.7
  10.5 5.8 %collective-permute-start.6 = (bf16[4,512,128]{2,1,0:T(8,128)(2,1)S(1)}, bf16[4,512,128]{2,1,0:T(8,128)(2,1)S(1)}, u32[]{:S(2)}, u32[]{:S(2)}) collective-permute-start(bf16[4,512,128]{2,1,0:T(8,128)(2,1)S(1)} %stack4.2.refs_0_.refs_5_), channel_id=1, source_target_pairs={{0,1},{1,0},{2,3},{3,2},{4,5},{5,4},{6,7},{7,6},{8,9},{9,8},{10,11... | collective-permute-start | bytes 1572872 | tf_op jit(solution)/shard_map/ppermute | solution.py:96
  12.9 9.9 %collective-permute-start.5 = (bf16[4,512,128]{2,1,0:T(8,128)(2,1)S(1)}, bf16[4,512,128]{2,1,0:T(8,128)(2,1)S(1)}, u32[]{:S(2)}, u32[]{:S(2)}) collective-permute-start(bf16[4,512,128]{2,1,0:T(8,128)(2,1)S(1)} %stack4.2.refs_0_.refs_5_), channel_id=1, source_target_pairs={{0,4},{1,17},{2,6},{3,19},{4,0},{5,21},{6,2},{7,23},{8,12},{9,25},... | collective-permute-start | bytes 1572872 | tf_op jit(solution)/shard_map/ppermute | solution.py:96
  14.8 14.7 %collective-permute-start.4 = (bf16[4,512,128]{2,1,0:T(8,128)(2,1)S(1)}, bf16[4,512,128]{2,1,0:T(8,128)(2,1)S(1)}, u32[]{:S(2)}, u32[]{:S(2)}) collective-permute-start(bf16[4,512,128]{2,1,0:T(8,128)(2,1)S(1)} %stack4.2.refs_0_.refs_5_), channel_id=1, source_target_pairs={{0,6},{1,25},{2,0},{3,27},{4,2},{5,29},{6,4},{7,31},{8,14},{9,1},{... | collective-permute-start | bytes 1572872 | tf_op jit(solution)/shard_map/ppermute | solution.py:96
  15.9 14.9 %collective-permute-start.3 = (bf16[4,512,128]{2,1,0:T(8,128)(2,1)S(1)}, bf16[4,512,128]{2,1,0:T(8,128)(2,1)S(1)}, u32[]{:S(2)}, u32[]{:S(2)}) collective-permute-start(bf16[4,512,128]{2,1,0:T(8,128)(2,1)S(1)} %stack4.2.refs_0_.refs_5_), channel_id=1, source_target_pairs={{0,2},{1,9},{2,4},{3,11},{4,6},{5,13},{6,0},{7,15},{8,10},{9,17},{... | collective-permute-start | bytes 1572872 | tf_op jit(solution)/shard_map/ppermute | solution.py:96
  22.8 0.7 copy-start.3
  23.5 0.7 copy-start.8
  24.2 9.6 %copy-start.4 = (f32[4096]{0:T(1024)S(1)}, f32[4096]{0:T(1024)}, u32[]{:S(2)}) copy-start(f32[4096]{0:T(1024)} %param.13) | copy-start | bytes 49156
  24.2 9.6 %copy-start.9 = (s32[4,1]{0,1:T(1,128)S(1)}, s32[4,1]{0,1:T(1,128)}, u32[]{:S(2)}) copy-start(s32[4,1]{0,1:T(1,128)} %param.15) | copy-start | bytes 52
  29.6 3.4 %collective-permute-start.9 = (bf16[4,512,128]{2,1,0:T(8,128)(2,1)S(1)}, bf16[4,512,128]{2,1,0:T(8,128)(2,1)S(1)}, u32[]{:S(2)}, u32[]{:S(2)}) collective-permute-start(bf16[4,512,128]{2,1,0:T(8,128)(2,1)S(1)} %collective-permute-done.4.refs_1_), channel_id=1, source_target_pairs={{0,1},{1,0},{2,3},{3,2},{4,5},{5,4},{6,7},{7,6},{8,9},{9,8},{10,11... | collective-permute-start | bytes 1572872 | tf_op jit(solution)/shard_map/ppermute | solution.py:96
  30.7 2.3 %collective-permute-start.7 = (bf16[4,512,128]{2,1,0:T(8,128)(2,1)S(1)}, bf16[4,512,128]{2,1,0:T(8,128)(2,1)S(1)}, u32[]{:S(2)}, u32[]{:S(2)}) collective-permute-start(bf16[4,512,128]{2,1,0:T(8,128)(2,1)S(1)} %collective-permute-done.5.refs_1_.refs_6_), channel_id=1, source_target_pairs={{0,1},{1,0},{2,3},{3,2},{4,5},{5,4},{6,7},{7,6},{8,9},{9,8},{10,11... | collective-permute-start | bytes 1572872 | tf_op jit(solution)/shard_map/ppermute | solution.py:96
  30.8 2.9 %collective-permute-start.8 = (bf16[4,512,128]{2,1,0:T(8,128)(2,1)S(1)}, bf16[4,512,128]{2,1,0:T(8,128)(2,1)S(1)}, u32[]{:S(2)}, u32[]{:S(2)}) collective-permute-start(bf16[4,512,128]{2,1,0:T(8,128)(2,1)S(1)} %collective-permute-done.3.refs_0_), channel_id=1, source_target_pairs={{0,1},{1,0},{2,3},{3,2},{4,5},{5,4},{6,7},{7,6},{8,9},{9,8},{10,11... | collective-permute-start | bytes 1572872 | tf_op jit(solution)/shard_map/ppermute | solution.py:96
  43.2 0.7 copy-start.5
  43.9 4.5 %collective-permute-start.10 = (bf16[16,512,128]{2,1,0:T(8,128)(2,1)}, bf16[16,512,128]{2,1,0:T(8,128)(2,1)}, u32[]{:S(2)}, u32[]{:S(2)}) collective-permute-start(bf16[16,512,128]{2,1,0:T(8,128)(2,1)} %get-tuple-element.37), channel_id=1, source_target_pairs={{0,1},{1,0},{2,3},{3,2},{4,5},{5,4},{6,7},{7,6},{8,9},{9,8},{10,11... | collective-permute-start | bytes 6291464 | tf_op jit(solution)/shard_map/ppermute | solution.py:96
  44.5 11.5 %collective-permute-start.19 = (bf16[1040,128]{1,0:T(8,128)(2,1)S(1)}, bf16[1040,128]{1,0:T(8,128)(2,1)S(1)}, u32[]{:S(2)}, u32[]{:S(2)}) collective-permute-start(bf16[1040,128]{1,0:T(8,128)(2,1)S(1)} %turn.1.refs_3_.refs_8_), channel_id=1, source_target_pairs={{0,96},{32,0},{64,32},{96,64},{1,97},{33,1},{65,33},{97,65},{2,98}... | collective-permute-start | bytes 798728 | tf_op jit(solution)/shard_map/ppermute | solution.py:488
  48.3 11.6 %collective-permute-start.18 = (bf16[1040,128]{1,0:T(8,128)(2,1)S(1)}, bf16[1040,128]{1,0:T(8,128)(2,1)S(1)}, u32[]{:S(2)}, u32[]{:S(2)}) collective-permute-start(bf16[1040,128]{1,0:T(8,128)(2,1)S(1)} %turn.1.refs_3_.refs_8_), channel_id=1, source_target_pairs={{0,32},{32,64},{64,96},{96,0},{1,33},{33,65},{65,97},{97,1},{2,34}... | collective-permute-start | bytes 798728 | tf_op jit(solution)/shard_map/ppermute | solution.py:488
  48.4 12.2 %copy-start = (bf16[512,512]{1,0:T(8,128)(2,1)S(1)}, bf16[512,512]{1,0:T(8,128)(2,1)}, u32[]{:S(2)}) copy-start(bf16[512,512]{1,0:T(8,128)(2,1)} %constant.49.clone.refs_1_) | copy-start | bytes 1572868
  52.5 16.8 %collective-permute-start.12 = (bf16[4,512,128]{2,1,0:T(8,128)(2,1)}, bf16[4,512,128]{2,1,0:T(8,128)(2,1)S(1)}, u32[]{:S(2)}, u32[]{:S(2)}) collective-permute-start(bf16[4,512,128]{2,1,0:T(8,128)(2,1)} %get-tuple-element.39), channel_id=1, source_target_pairs={{0,2},{1,9},{2,4},{3,11},{4,6},{5,13},{6,0},{7,15},{8,10},{9,17},{... | collective-permute-start | bytes 1572872 | tf_op jit(solution)/shard_map/ppermute | solution.py:96
  53.4 15.9 %collective-permute-start.13 = (bf16[4,512,128]{2,1,0:T(8,128)(2,1)}, bf16[4,512,128]{2,1,0:T(8,128)(2,1)}, u32[]{:S(2)}, u32[]{:S(2)}) collective-permute-start(bf16[4,512,128]{2,1,0:T(8,128)(2,1)} %get-tuple-element.40), channel_id=1, source_target_pairs={{0,6},{1,25},{2,0},{3,27},{4,2},{5,29},{6,4},{7,31},{8,14},{9,1},{... | collective-permute-start | bytes 1572872 | tf_op jit(solution)/shard_map/ppermute | solution.py:96
  55.2 14.2 %collective-permute-start.11 = (bf16[4,512,128]{2,1,0:T(8,128)(2,1)}, bf16[4,512,128]{2,1,0:T(8,128)(2,1)}, u32[]{:S(2)}, u32[]{:S(2)}) collective-permute-start(bf16[4,512,128]{2,1,0:T(8,128)(2,1)} %get-tuple-element.38.refs_2_), channel_id=1, source_target_pairs={{0,4},{1,17},{2,6},{3,19},{4,0},{5,21},{6,2},{7,23},{8,12},{9,25},... | collective-permute-start | bytes 1572872 | tf_op jit(solution)/shard_map/ppermute | solution.py:96
  56.0 20.5 %collective-permute-start.17 = (bf16[1040,128]{1,0:T(8,128)(2,1)S(1)}, bf16[1040,128]{1,0:T(8,128)(2,1)}, u32[]{:S(2)}, u32[]{:S(2)}) collective-permute-start(bf16[1040,128]{1,0:T(8,128)(2,1)S(1)} %turn.1.refs_3_.refs_8_), channel_id=1, source_target_pairs={{0,64},{32,96},{64,0},{96,32},{1,65},{33,97},{65,1},{97,33},{2,66}... | collective-permute-start | bytes 798728 | tf_op jit(solution)/shard_map/ppermute | solution.py:488
  59.9 0.7 copy-start.1
  62.1 16.1 %all-to-all-start = ((bf16[32,4,4,256]{3,2,1,0:T(4,128)(2,1)}), bf16[32,4,4,256]{3,2,1,0:T(4,128)(2,1)S(1)}, u32[]{:S(2)}, u32[]{:S(2)}) async-start(bf16[32,4,4,256]{3,2,1,0:T(4,128)(2,1)} %pack.1.refs_9_), calls=%async_computation | async-start | bytes 524288 | tf_op jit(solution)/shard_map/all_to_all | solution.py:493
  72.1 6.1 %collective-permute-start.15 = (bf16[512,128]{1,0:T(8,128)(2,1)}, bf16[512,128]{1,0:T(8,128)(2,1)}, u32[]{:S(2)}, u32[]{:S(2)}) collective-permute-start(bf16[512,128]{1,0:T(8,128)(2,1)} %get-tuple-element.42), channel_id=1, source_target_pairs={{0,8},{1,3},{2,10},{3,5},{4,12},{5,7},{6,14},{7,1},{8,16},{9,11},{... | collective-permute-start | bytes 393224 | tf_op jit(solution)/shard_map/ppermute | solution.py:96
  73.5 4.8 %collective-permute-start.16 = (bf16[512,128]{1,0:T(8,128)(2,1)}, bf16[512,128]{1,0:T(8,128)(2,1)}, u32[]{:S(2)}, u32[]{:S(2)}) collective-permute-start(bf16[512,128]{1,0:T(8,128)(2,1)} %get-tuple-element.43), channel_id=1, source_target_pairs={{0,24},{1,7},{2,26},{3,1},{4,28},{5,3},{6,30},{7,5},{8,0},{9,15},{... | collective-permute-start | bytes 393224 | tf_op jit(solution)/shard_map/ppermute | solution.py:96
  74.8 5.6 %collective-permute-start.14 = (bf16[512,128]{1,0:T(8,128)(2,1)}, bf16[512,128]{1,0:T(8,128)(2,1)}, u32[]{:S(2)}, u32[]{:S(2)}) collective-permute-start(bf16[512,128]{1,0:T(8,128)(2,1)} %get-tuple-element.41.refs_10_), channel_id=1, source_target_pairs={{0,16},{1,5},{2,18},{3,7},{4,20},{5,1},{6,22},{7,3},{8,24},{9,13},... | collective-permute-start | bytes 393224 | tf_op jit(solution)/shard_map/ppermute | solution.py:96
  80.4 0.9 copy-start.6
  81.3 36.7 %copy-start.2 = (bf16[1040,128]{1,0:T(8,128)(2,1)S(1)}, bf16[1040,128]{1,0:T(8,128)(2,1)}, u32[]{:S(2)}) copy-start(bf16[1040,128]{1,0:T(8,128)(2,1)} %copy-done.1) | copy-start | bytes 798724
  83.2 3.9 %collective-permute-start.23 = (bf16[512,128]{1,0:T(8,128)(2,1)S(1)}, bf16[512,128]{1,0:T(8,128)(2,1)S(1)}, u32[]{:S(2)}, u32[]{:S(2)}) collective-permute-start(bf16[512,128]{1,0:T(8,128)(2,1)S(1)} %get-tuple-element.45), channel_id=1, source_target_pairs={{0,24},{1,7},{2,26},{3,1},{4,28},{5,3},{6,30},{7,5},{8,32},{9,47},... | collective-permute-start | bytes 393224 | tf_op jit(solution)/shard_map/ppermute | solution.py:514
  84.7 6.4 %collective-permute-start.22 = (bf16[512,128]{1,0:T(8,128)(2,1)S(1)}, bf16[512,128]{1,0:T(8,128)(2,1)S(1)}, u32[]{:S(2)}, u32[]{:S(2)}) collective-permute-start(bf16[512,128]{1,0:T(8,128)(2,1)S(1)} %get-tuple-element.45), channel_id=1, source_target_pairs={{0,8},{1,3},{2,10},{3,5},{4,12},{5,7},{6,14},{7,1},{8,48},{9,43},{... | collective-permute-start | bytes 393224 | tf_op jit(solution)/shard_map/ppermute | solution.py:514
  84.8 6.4 %collective-permute-start.21 = (bf16[512,128]{1,0:T(8,128)(2,1)S(1)}, bf16[512,128]{1,0:T(8,128)(2,1)S(1)}, u32[]{:S(2)}, u32[]{:S(2)}) collective-permute-start(bf16[512,128]{1,0:T(8,128)(2,1)S(1)} %get-tuple-element.45), channel_id=1, source_target_pairs={{0,16},{1,5},{2,18},{3,7},{4,20},{5,1},{6,22},{7,3},{8,56},{9,45},... | collective-permute-start | bytes 393224 | tf_op jit(solution)/shard_map/ppermute | solution.py:514
  86.5 4.7 %collective-permute-start.20 = (bf16[512,128]{1,0:T(8,128)(2,1)S(1)}, bf16[512,128]{1,0:T(8,128)(2,1)S(1)}, u32[]{:S(2)}, u32[]{:S(2)}) collective-permute-start(bf16[512,128]{1,0:T(8,128)(2,1)S(1)} %get-tuple-element.45), channel_id=1, source_target_pairs={{0,0},{1,1},{2,2},{3,3},{4,4},{5,5},{6,6},{7,7},{8,40},{9,41},{10,... | collective-permute-start | bytes 393224 | tf_op jit(solution)/shard_map/ppermute | solution.py:514
  91.2 16.1 %collective-permute-start.25 = (bf16[4,512,128]{2,1,0:T(8,128)(2,1)S(1)}, bf16[4,512,128]{2,1,0:T(8,128)(2,1)S(1)}, u32[]{:S(2)}, u32[]{:S(2)}) collective-permute-start(bf16[4,512,128]{2,1,0:T(8,128)(2,1)S(1)} %stack4.3.refs_0_), channel_id=1, source_target_pairs={{0,4},{1,17},{2,6},{3,19},{4,0},{5,21},{6,2},{7,23},{8,12},{9,25},... | collective-permute-start | bytes 1572872 | tf_op jit(solution)/shard_map/ppermute | solution.py:96
  100.4 12.5 %collective-permute-start.27 = (bf16[4,512,128]{2,1,0:T(8,128)(2,1)S(1)}, bf16[4,512,128]{2,1,0:T(8,128)(2,1)S(1)}, u32[]{:S(2)}, u32[]{:S(2)}) collective-permute-start(bf16[4,512,128]{2,1,0:T(8,128)(2,1)S(1)} %stack4.3.refs_0_), channel_id=1, source_target_pairs={{0,2},{1,9},{2,4},{3,11},{4,6},{5,13},{6,0},{7,15},{8,10},{9,17},{... | collective-permute-start | bytes 1572872 | tf_op jit(solution)/shard_map/ppermute | solution.py:96
  100.4 15.3 %collective-permute-start.24 = (bf16[4,512,128]{2,1,0:T(8,128)(2,1)S(1)}, bf16[4,512,128]{2,1,0:T(8,128)(2,1)S(1)}, u32[]{:S(2)}, u32[]{:S(2)}) collective-permute-start(bf16[4,512,128]{2,1,0:T(8,128)(2,1)S(1)} %stack4.3.refs_0_), channel_id=1, source_target_pairs={{0,6},{1,25},{2,0},{3,27},{4,2},{5,29},{6,4},{7,31},{8,14},{9,1},{... | collective-permute-start | bytes 1572872 | tf_op jit(solution)/shard_map/ppermute | solution.py:96
  107.3 8.4 %collective-permute-start.26 = (bf16[512,128]{1,0:T(8,128)(2,1)S(1)}, bf16[512,128]{1,0:T(8,128)(2,1)S(1)}, u32[]{:S(2)}, u32[]{:S(2)}) collective-permute-start(bf16[512,128]{1,0:T(8,128)(2,1)S(1)} %get-tuple-element.47.refs_4_), channel_id=1, source_target_pairs={{0,0},{1,1},{2,2},{3,3},{4,4},{5,5},{6,6},{7,7},{8,8},{9,9},{10,10... | collective-permute-start | bytes 393224 | tf_op jit(solution)/shard_map/ppermute | solution.py:520
  108.0 8.7 %collective-permute-start.28 = (bf16[4,512,128]{2,1,0:T(8,128)(2,1)S(1)}, bf16[4,512,128]{2,1,0:T(8,128)(2,1)S(1)}, u32[]{:S(2)}, u32[]{:S(2)}) collective-permute-start(bf16[4,512,128]{2,1,0:T(8,128)(2,1)S(1)} %stack4.3.refs_0_), channel_id=1, source_target_pairs={{0,1},{1,0},{2,3},{3,2},{4,5},{5,4},{6,7},{7,6},{8,9},{9,8},{10,11... | collective-permute-start | bytes 1572872 | tf_op jit(solution)/shard_map/ppermute | solution.py:96
  111.0 6.3 %collective-permute-start.29 = (bf16[4,512,128]{2,1,0:T(8,128)(2,1)S(1)}, bf16[4,512,128]{2,1,0:T(8,128)(2,1)S(1)}, u32[]{:S(2)}, u32[]{:S(2)}) collective-permute-start(bf16[4,512,128]{2,1,0:T(8,128)(2,1)S(1)} %collective-permute-done.25.refs_1_), channel_id=1, source_target_pairs={{0,1},{1,0},{2,3},{3,2},{4,5},{5,4},{6,7},{7,6},{8,9},{9,8},{10,11... | collective-permute-start | bytes 1572872 | tf_op jit(solution)/shard_map/ppermute | solution.py:96
  112.9 4.4 %collective-permute-start.30 = (bf16[4,512,128]{2,1,0:T(8,128)(2,1)S(1)}, bf16[4,512,128]{2,1,0:T(8,128)(2,1)S(1)}, u32[]{:S(2)}, u32[]{:S(2)}) collective-permute-start(bf16[4,512,128]{2,1,0:T(8,128)(2,1)S(1)} %collective-permute-done.27.refs_2_), channel_id=1, source_target_pairs={{0,1},{1,0},{2,3},{3,2},{4,5},{5,4},{6,7},{7,6},{8,9},{9,8},{10,11... | collective-permute-start | bytes 1572872 | tf_op jit(solution)/shard_map/ppermute | solution.py:96
  115.7 2.3 %collective-permute-start.31 = (bf16[4,512,128]{2,1,0:T(8,128)(2,1)S(1)}, bf16[4,512,128]{2,1,0:T(8,128)(2,1)S(1)}, u32[]{:S(2)}, u32[]{:S(2)}) collective-permute-start(bf16[4,512,128]{2,1,0:T(8,128)(2,1)S(1)} %collective-permute-done.24.refs_3_), channel_id=1, source_target_pairs={{0,1},{1,0},{2,3},{3,2},{4,5},{5,4},{6,7},{7,6},{8,9},{9,8},{10,11... | collective-permute-start | bytes 1572872 | tf_op jit(solution)/shard_map/ppermute | solution.py:96
